TPU v7x, 256 devices: a whole 4x4x8 slice. The times are simulated.
256 devices in a mesh: gx: 16 (over y_hi, z), gy: 8 (over x, core), gz: 2 (over y_lo).
Axes of the slice: x: 4, y: 4 (y_hi: 2, y_lo: 2; y = y_hi * 2 + y_lo), z: 8, core: 2. Of those that a mesh axis runs over, the one named last changes fastest.
Arguments:
- start_field: float32 [3, 128, 192, 256], P(None, 'gx', 'gy', 'gz'), may hold values from -6 to 6
- stiffness: float32 [128, 192, 256], P('gx', 'gy', 'gz'), may hold values from 1 to 10
- mass: float32 [128, 192, 256], P('gx', 'gy', 'gz'), may hold values from 0.5 to 20
- sens_values: float32 [3, 2, 128, 4096], P(None, 'gz', ('gx', 'gy')), may hold values from -48 to 48
- sens_cells: int32 [2, 128, 4096], P('gz', ('gx', 'gy')), may hold values from 0 to 24575
- sens_counts: int32 [2, 128, 128], P('gz', ('gx', 'gy')), may hold values from 0 to 32, as said below
- hull_cells: int32 [16, 16, 4096], P('gx', ('gy', 'gz')), may hold values from 0 to 24575
- hull_patches: int32 [16, 16, 4096], P('gx', ('gy', 'gz')), may hold values from 0 to 262143
Outputs:
- adjoint_field: float32 [3, 128, 192, 256], P(None, 'gx', 'gy', 'gz')
- patch_gradient: float32 [3, 1024, 4096], P(None, ('gy', 'gz'), 'gx')
Inputs may be any that keep to these rules, and one draw needn't show every extreme that they name: sens_counts[g, s, j] counts the live slots among the 32 slots that flow partition s of vertical block g sends to mesh block j. Every partition fills some block, and in every vertical block one mesh block receives 32 live slots from every partition.
All inputs are finite; a program needn't handle non-finite values.
Results may differ from a plain program's by a relative error of at most 0.0001.
Values sent between devices are 32-bit elements; how exact they have to be, the bound alone decides.
No kernel may reach another device: no remote copies, remote signals or barrier semaphores. Data moves between devices by JAX's collectives and lax.ppermute only.
A program may use at most 320 MiB of HBM per device.

v0:
```python
import jax
import jax.numpy as jnp
from jax import lax
from jax.sharding import PartitionSpec as P

SWEEPS = 3
PROWS_DEV = 256
PCOLS_DEV = 64


relax_weight = 0.8


def with_halo(cells, sides, width):
    for axis, dim in sides:
        count = lax.axis_size(axis)
        ends = count - 1
        head = lax.slice_in_dim(cells, 0, width, axis=dim)
        tail = lax.slice_in_dim(cells, cells.shape[dim] - width, cells.shape[dim], axis=dim)
        cells = jnp.concatenate(
            [
                lax.ppermute(tail, axis, [(i, (i + 1) % count) for i in range(ends)]),
                cells,
                lax.ppermute(head, axis, [((i + 1) % count, i) for i in range(ends)]),
            ],
            axis=dim,
        )
    return cells


def face_cuts():
    middle = slice(1, -1)
    result = []
    for axis_num in range(3):
        for side_cut in (slice(2, None), slice(None, -2)):
            parts = [middle, middle, middle]
            parts[axis_num] = side_cut
            result.append(tuple(parts))
    return result


def relax_sweep(field_rim, stiff_rim, source, mass):
    middle = (slice(1, -1), slice(1, -1), slice(1, -1))
    center = field_rim[(slice(None),) + middle]
    stiff_center = stiff_rim[middle]
    weight_sum = jnp.zeros_like(stiff_center)
    flux_sum = jnp.zeros_like(center)
    for cut in face_cuts():
        weight = 0.5 * (stiff_center + stiff_rim[cut])
        weight_sum = weight_sum + weight
        flux_sum = flux_sum + weight * (center - field_rim[(slice(None),) + cut])
    mass_term = mass * (center + 0.25 * jnp.sum(center, axis=0))
    residual = source - flux_sum - mass_term
    diagonal = weight_sum + 1.25 * mass
    updated = center + relax_weight * residual / diagonal
    return updated


def per_device(
    start_field, stiffness, mass, sens_values, sens_cells, sens_counts, hull_cells, hull_patches
):
    cells_x, cells_y, cells_z = stiffness.shape
    capacity = sens_values.shape[3] // sens_counts.shape[2]
    slot_ids = lax.iota(jnp.int32, sens_values.shape[3])
    limits = jnp.repeat(sens_counts[0, 0], capacity)
    live_slots = slot_ids % capacity < limits
    payload = jnp.concatenate(
        [jnp.where(live_slots, sens_values, 0.0), sens_cells.astype(jnp.float32)[None]], axis=0
    )
    arrived = lax.all_to_all(payload, ("gx", "gy"), split_axis=3, concat_axis=2, tiled=True)
    arrived = arrived.reshape(4, -1)
    cell_ids = arrived[3].astype(jnp.int32)
    source = (
        jnp.zeros((3, cells_x * cells_y * cells_z), jnp.float32).at[:, cell_ids].add(arrived[:3])
    )
    source = source.reshape(3, cells_x, cells_y, cells_z)
    stiff_rim = with_halo(stiffness, (("gx", 0), ("gy", 1), ("gz", 2)), 1)
    field_now = start_field
    for sweep in range(SWEEPS):
        field_rim = with_halo(field_now, (("gx", 1), ("gy", 2), ("gz", 3)), 1)
        field_now = relax_sweep(field_rim, stiff_rim, source, mass)
    flat_field = field_now.reshape(3, -1)
    flat_stiff = stiffness.reshape(-1)
    hull_ids = hull_cells[0, 0]
    hull_values = flat_field[:, hull_ids] * flat_stiff[hull_ids]
    patch_ids = hull_patches[0, 0]
    girth_total = PCOLS_DEV * lax.axis_size(("gy", "gz"))
    partial_grid = (
        jnp.zeros((3, girth_total * PROWS_DEV), jnp.float32).at[:, patch_ids].add(hull_values)
    )
    partial_grid = partial_grid.reshape(3, girth_total, PROWS_DEV)
    patch = lax.psum_scatter(partial_grid, ("gy", "gz"), scatter_dimension=1, tiled=True)
    return (field_now, patch)


def solution(mesh):
    placed = (
        P(None, "gx", "gy", "gz"),
        P("gx", "gy", "gz"),
        P("gx", "gy", "gz"),
        P(None, "gz", ("gx", "gy"), None),
        P("gz", ("gx", "gy"), None),
        P("gz", ("gx", "gy"), None),
        P("gx", ("gy", "gz"), None),
        P("gx", ("gy", "gz"), None),
    )
    return jax.shard_map(
        per_device,
        mesh=mesh,
        in_specs=placed,
        out_specs=(P(None, "gx", "gy", "gz"), P(None, ("gy", "gz"), "gx")),
        check_vma=False,
    )
```

profile of v0, /device:TPU:1, one launch (start us, length us, event | category | flops | bytes accessed | tf_op | source)
XLA Modules:
  0.0 616.0 jit_solution(3176204956875739263)
XLA Ops:
  7.2 0.7 fusion.110
  7.9 1.3 collective-permute-start
  9.2 5.0 collective-permute-start.2
  14.2 1.4 fusion.107
  15.6 1.3 collective-permute-start.1
  16.9 4.8 collective-permute-start.3
  21.7 0.7 broadcast_in_dim.17
  22.5 0.8 copy_select_fusion
  23.4 0.9 constant_dynamic-update-slice_fusion.1
  24.3 4.4 collective-permute-start.6
  28.8 1.9 collective-permute-start.4
  30.7 0.7 convert_bitcast_fusion
  31.4 2.3 collective-permute-done.4
  33.8 3.2 collective-permute-start.10
  37.1 1.3 collective-permute-start.8
  38.4 2.4 copy.64
  40.8 0.5 broadcast.125
  41.3 19.3 %reduce.2 = f32[4096,4]{1,0:T(8,128)} reduce(f32[4096,1,1,4]{3,2,1,0:T(1,128)S(1)} %bitcast.28, f32[]{:T(128)} %broadcast.125), dimensions={1,2}, to_apply=%bitcast.20.reduce_sub_computation | reduce | bytes 131076
  60.6 4.1 reshape.165
  64.7 17.4 %all-to-all-start = ((f32[128,1,128]{2,1,0:T(1,128)}), f32[128,1,128]{2,1,0:T(1,128)S(1)}, u32[]{:S(2)}, u32[]{:S(2)}) async-start(f32[128,1,128]{2,1,0:T(1,128)} %reshape.165), calls=%async_computation | async-start | bytes 131072 | tf_op jit(solution)/shard_map/all_to_all | solution.py:70
  82.2 1.1 multiply_add_fusion
  83.3 0.8 constant_dynamic-update-slice_fusion.5
  84.1 3.5 collective-permute-start.7
  87.7 1.9 collective-permute-start.5
  89.6 3.4 collective-permute-done.5
  93.1 1.1 fusion.103
  94.2 1.3 collective-permute-start.9
  95.5 6.5 %collective-permute-start.11 = (f32[3,10,26,1]{3,2,1,0:T(8,128)}, f32[3,10,26,1]{3,2,1,0:T(8,128)}, u32[]{:S(2)}, u32[]{:S(2)}) collective-permute-start(f32[3,10,26,1]{3,2,1,0:T(8,128)} %get-tuple-element.20), channel_id=1, source_target_pairs={{0,1},{2,3},{4,5},{6,7},{8,9},{10,11},{12,13},{14,15},{16,17},{18,... | collective-permute-start | bytes 9368 | tf_op jit(solution)/shard_map/ppermute | solution.py:22
  102.0 0.7 reduce.3
  102.7 3.4 reshape.166
  106.1 91.6 %fusion.5 = s32[4096]{0:T(1024)S(1)} fusion(f32[4,1,1,4096]{0,2,1,3:T(1,128)S(1)} %bitcast.25), kind=kLoop, calls=%fused_computation.10 | loop fusion | flops 4096 | bytes 32768 | tf_op jit(solution)/shard_map/convert_element_type | solution.py:72
  197.7 0.6 compare_select_fusion.2
  198.3 1.9 copy.65
  200.3 0.6 copy.66
  200.9 27.8 %scatter_custom_fusion = f32[3,24576]{0,1:T(8,128)} fusion(s32[4096]{0:T(1024)} %bitcast.33, f32[4096,3]{1,0:T(8,128)S(1)} %copy.66, f32[]{:T(128)} %constant.10.clone.1), kind=kCustom, calls=%fused_computation.7 | custom fusion | flops 12288 | bytes 295424 | tf_op jit(solution)/shard_map/scatter-add | solution.py:74
  228.7 7.6 %copy.67 = f32[3,8,24,128]{3,2,1,0:T(8,128)S(1)} copy(f32[3,8,24,128]{0,3,2,1:T(8,128)} %bitcast.24) | data formatting | bytes 589824 | tf_op jit(solution)/shard_map/reshape | solution.py:76
  236.4 1.6 fusion.93
  238.1 3.1 collective-permute-start.13
  241.2 1.3 collective-permute-start.12
  242.5 3.4 collective-permute-done.12
  245.9 3.5 collective-permute-start.15
  249.4 1.9 collective-permute-start.14
  251.4 3.1 collective-permute-done.14
  254.8 1.3 collective-permute-start.16
  256.1 4.0 collective-permute-start.17
  260.1 8.0 %collective-permute-done.16 = f32[3,10,26,1]{3,2,1,0:T(8,128)S(1)} collective-permute-done((f32[3,10,26,1]{3,2,1,0:T(8,128)S(1)}, f32[3,10,26,1]{3,2,1,0:T(8,128)S(1)}, u32[]{:S(2)}, u32[]{:S(2)}) %collective-permute-start.16) | collective-permute-done | bytes 3152 | tf_op jit(solution)/shard_map/ppermute | solution.py:24
  268.1 1.8 collective-permute-done.17
  269.9 0.5 fusion.91
  270.4 3.3 collective-permute-start.19
  273.7 1.3 collective-permute-start.18
  275.0 5.1 sort
  280.2 4.5 collective-permute-start.21
  284.7 1.9 collective-permute-start.20
  286.7 23.0 %gather_fusion.1 = f32[4096]{0:T(1024)S(1)} fusion(f32[24576]{0:T(1024)S(1)} %bitcast.23, s32[4096]{0:T(1024)S(1)} %get-tuple-element.42), kind=kCustom, calls=%fused_computation.1 | custom fusion | bytes 49152 | tf_op jit(solution)/shard_map/gather | solution.py:85
  310.0 1.3 collective-permute-start.22
  311.3 4.2 collective-permute-start.23
  315.5 7.1 %collective-permute-done.22 = f32[3,10,26,1]{3,2,1,0:T(8,128)S(1)} collective-permute-done((f32[3,10,26,1]{3,2,1,0:T(8,128)S(1)}, f32[3,10,26,1]{3,2,1,0:T(8,128)S(1)}, u32[]{:S(2)}, u32[]{:S(2)}) %collective-permute-start.22) | collective-permute-done | bytes 3152 | tf_op jit(solution)/shard_map/ppermute | solution.py:24
  322.6 1.8 collective-permute-done.23
  324.9 6.6 %copy.70 = f32[3,8,24,128]{0,3,2,1:T(8,128)} copy(f32[3,8,24,128]{3,2,1,0:T(8,128)S(1)} %fusion.16) | data formatting | bytes 589824 | tf_op jit(solution)/shard_map/add | solution.py:55
  331.5 15.3 %gather_fusion = f32[4096,3]{1,0:T(8,128)S(1)} fusion(f32[3,24576]{0,1:T(8,128)} %bitcast.27, s32[4096]{0:T(1024)S(1)} %get-tuple-element.42), kind=kCustom, calls=%fused_computation | custom fusion | bytes 114688 | tf_op jit(solution)/shard_map/gather | solution.py:85
  346.8 1.9 broadcast_multiply_fusion
  348.8 106.0 %scatter_custom_fusion.1 = f32[3,262144]{0,1:T(8,128)} fusion(s32[4096]{0:T(1024)S(1)} %get-tuple-element.2, f32[]{:T(128)} %constant.10.clone.1, f32[4096,3]{1,0:T(8,128)} %broadcast_multiply_fusion, s32[4096]{0:T(1024)S(1)} %get-tuple-element.41), kind=kCustom, calls=%fused_computation.5 | custom fusion | flops 12288 | bytes 3146240 | tf_op jit(solution)/shard_map/scatter-add | solution.py:89
  454.8 70.7 %copy.71 = f32[3,1024,256]{2,1,0:T(8,128)} copy(f32[3,1024,256]{0,2,1:T(8,128)} %bitcast.13) | data formatting | bytes 6291456 | tf_op jit(solution)/shard_map/reshape | solution.py:91
  525.5 83.3 %reduce-scatter.2.cloned.1.call-done = f32[3,64,256]{2,1,0:T(8,128)} async-done(((f32[3,1024,256]{2,1,0:T(8,128)}), f32[3,64,256]{2,1,0:T(8,128)}) %reduce-scatter.2.cloned.1.call-update) | async-done | bytes 196624 | tf_op jit(solution)/shard_map/reduce_scatter | solution.py:92
  (69 shorter events, 1.7 us)
Async XLA Ops:
  7.9 16.4 %collective-permute-start = (f32[1,24,128]{2,1,0:T(8,128)S(1)}, f32[1,24,128]{2,1,0:T(8,128)S(1)}, u32[]{:S(2)}, u32[]{:S(2)}) collective-permute-start(f32[1,24,128]{2,1,0:T(8,128)S(1)} %get-tuple-element.39), channel_id=1, source_target_pairs={{16,0},{32,16},{48,32},{64,48},{80,64},{96,80},{112,96},{128,112},... | collective-permute-start | bytes 36872 | tf_op jit(solution)/shard_map/ppermute | solution.py:24
  9.2 14.2 %collective-permute-start.2 = (f32[1,24,128]{2,1,0:T(8,128)S(1)}, f32[1,24,128]{2,1,0:T(8,128)S(1)}, u32[]{:S(2)}, u32[]{:S(2)}) collective-permute-start(f32[1,24,128]{2,1,0:T(8,128)S(1)} %get-tuple-element.40), channel_id=1, source_target_pairs={{0,16},{16,32},{32,48},{48,64},{64,80},{80,96},{96,112},{112,128},... | collective-permute-start | bytes 36872 | tf_op jit(solution)/shard_map/ppermute | solution.py:22
  15.6 68.5 %collective-permute-start.1 = (f32[3,1,24,128]{3,2,1,0:T(8,128)}, f32[3,1,24,128]{3,2,1,0:T(8,128)S(1)}, u32[]{:S(2)}, u32[]{:S(2)}) collective-permute-start(f32[3,1,24,128]{3,2,1,0:T(8,128)} %get-tuple-element.31), channel_id=1, source_target_pairs={{16,0},{32,16},{48,32},{64,48},{80,64},{96,80},{112,96},{128,112},... | collective-permute-start | bytes 110600 | tf_op jit(solution)/shard_map/ppermute | solution.py:24
  16.9 66.4 %collective-permute-start.3 = (f32[3,1,24,128]{3,2,1,0:T(8,128)S(1)}, f32[3,1,24,128]{3,2,1,0:T(8,128)}, u32[]{:S(2)}, u32[]{:S(2)}) collective-permute-start(f32[3,1,24,128]{3,2,1,0:T(8,128)S(1)} %get-tuple-element.32), channel_id=1, source_target_pairs={{0,16},{16,32},{32,48},{48,64},{64,80},{80,96},{96,112},{112,128},... | collective-permute-start | bytes 110600 | tf_op jit(solution)/shard_map/ppermute | solution.py:22
  24.3 7.1 %collective-permute-start.6 = (f32[10,1,128]{2,1,0:T(1,128)S(1)}, f32[10,1,128]{2,1,0:T(1,128)S(1)}, u32[]{:S(2)}, u32[]{:S(2)}) collective-permute-start(f32[10,1,128]{2,1,0:T(1,128)S(1)} %get-tuple-element.37), channel_id=1, source_target_pairs={{0,2},{2,4},{4,6},{6,8},{8,10},{10,12},{12,14},{1,3},{3,5},{5,7},{... | collective-permute-start | bytes 15368 | tf_op jit(solution)/shard_map/ppermute | solution.py:22
  28.8 4.9 collective-permute-start.4
  33.8 48.3 %collective-permute-start.10 = (f32[10,26,1]{2,1,0:T(8,128)S(1)}, f32[10,26,1]{2,1,0:T(8,128)S(1)}, u32[]{:S(2)}, u32[]{:S(2)}) collective-permute-start(f32[10,26,1]{2,1,0:T(8,128)S(1)} %get-tuple-element.35), channel_id=1, source_target_pairs={{0,1},{2,3},{4,5},{6,7},{8,9},{10,11},{12,13},{14,15},{16,17},{18,... | collective-permute-start | bytes 3128 | tf_op jit(solution)/shard_map/ppermute | solution.py:22
  37.1 45.1 %collective-permute-start.8 = (f32[10,26,1]{2,1,0:T(8,128)S(1)}, f32[10,26,1]{2,1,0:T(8,128)}, u32[]{:S(2)}, u32[]{:S(2)}) collective-permute-start(f32[10,26,1]{2,1,0:T(8,128)S(1)} %get-tuple-element.36), channel_id=1, source_target_pairs={{1,0},{3,2},{5,4},{7,6},{9,8},{11,10},{13,12},{15,14},{17,16},{19,... | collective-permute-start | bytes 3128 | tf_op jit(solution)/shard_map/ppermute | solution.py:24
  60.6 21.5 %copy-start = (f32[8,24,128]{2,1,0:T(8,128)S(1)}, f32[8,24,128]{2,1,0:T(8,128)}, u32[]{:S(2)}) copy-start(f32[8,24,128]{2,1,0:T(8,128)} %param.9) | copy-start | bytes 294916
  60.6 21.5 %copy-start.1 = (f32[8,24,128]{2,1,0:T(8,128)S(1)}, f32[8,24,128]{2,1,0:T(8,128)}, u32[]{:S(2)}) copy-start(f32[8,24,128]{2,1,0:T(8,128)} %param.10) | copy-start | bytes 294916
  60.6 23.4 %copy-start.2 = (f32[3,8,24,128]{3,2,1,0:T(8,128)S(1)}, f32[3,8,24,128]{3,2,1,0:T(8,128)}, u32[]{:S(2)}) copy-start(f32[3,8,24,128]{3,2,1,0:T(8,128)} %param.8) | copy-start | bytes 884740
  64.7 37.3 %all-to-all-start = ((f32[128,1,128]{2,1,0:T(1,128)}), f32[128,1,128]{2,1,0:T(1,128)S(1)}, u32[]{:S(2)}, u32[]{:S(2)}) async-start(f32[128,1,128]{2,1,0:T(1,128)} %reshape.165), calls=%async_computation | async-start | bytes 131072 | tf_op jit(solution)/shard_map/all_to_all | solution.py:70
  82.1 526.7 %reduce-scatter.2.cloned.1.call-start = ((), (), s32[]{:S(2)}) async-start(), calls=%async_computation.2 | async-start | bytes 3342336 | tf_op jit(solution)/shard_map/reduce_scatter | solution.py:92
  84.1 5.5 collective-permute-start.7
  87.7 5.3 collective-permute-start.5
  89.6 12.4 %copy-start.5 = (f32[3,10,1,128]{3,2,1,0:T(1,128)}, f32[3,10,1,128]{3,2,1,0:T(1,128)S(1)}, u32[]{:S(2)}) copy-start(f32[3,10,1,128]{3,2,1,0:T(1,128)S(1)} %collective-permute-done.7) | copy-start | bytes 46084
  93.0 9.0 %copy-start.7 = (f32[3,10,1,128]{3,2,1,0:T(1,128)}, f32[3,10,1,128]{3,2,1,0:T(1,128)S(1)}, u32[]{:S(2)}) copy-start(f32[3,10,1,128]{3,2,1,0:T(1,128)S(1)} %collective-permute-done.5) | copy-start | bytes 46084
  94.2 142.2 %collective-permute-start.9 = (f32[3,10,26,1]{3,2,1,0:T(8,128)}, f32[3,10,26,1]{3,2,1,0:T(8,128)}, u32[]{:S(2)}, u32[]{:S(2)}) collective-permute-start(f32[3,10,26,1]{3,2,1,0:T(8,128)} %get-tuple-element.19), channel_id=1, source_target_pairs={{1,0},{3,2},{5,4},{7,6},{9,8},{11,10},{13,12},{15,14},{17,16},{19,... | collective-permute-start | bytes 9368 | tf_op jit(solution)/shard_map/ppermute | solution.py:24
  95.5 140.9 %collective-permute-start.11 = (f32[3,10,26,1]{3,2,1,0:T(8,128)}, f32[3,10,26,1]{3,2,1,0:T(8,128)}, u32[]{:S(2)}, u32[]{:S(2)}) collective-permute-start(f32[3,10,26,1]{3,2,1,0:T(8,128)} %get-tuple-element.20), channel_id=1, source_target_pairs={{0,1},{2,3},{4,5},{6,7},{8,9},{10,11},{12,13},{14,15},{16,17},{18,... | collective-permute-start | bytes 9368 | tf_op jit(solution)/shard_map/ppermute | solution.py:22
  228.7 7.7 %copy-start.3 = (f32[3,8,24,128]{3,2,1,0:T(8,128)S(1)}, f32[3,8,24,128]{3,2,1,0:T(8,128)}, u32[]{:S(2)}) copy-start(f32[3,8,24,128]{3,2,1,0:T(8,128)} %param.8) | copy-start | bytes 884740
  228.7 7.7 %copy-start.6 = (f32[3,10,1,128]{3,2,1,0:T(1,128)S(1)}, f32[3,10,1,128]{3,2,1,0:T(1,128)}, u32[]{:S(2)}) copy-start(f32[3,10,1,128]{3,2,1,0:T(1,128)} %copy-done.5) | copy-start | bytes 46084
  228.7 7.7 %copy-start.8 = (f32[3,10,1,128]{3,2,1,0:T(1,128)S(1)}, f32[3,10,1,128]{3,2,1,0:T(1,128)}, u32[]{:S(2)}) copy-start(f32[3,10,1,128]{3,2,1,0:T(1,128)} %copy-done.7) | copy-start | bytes 46084
  236.3 15.0 %copy-start.9 = (s32[1,1,4096]{2,1,0:T(1,128)S(1)}, s32[1,1,4096]{2,1,0:T(1,128)}, u32[]{:S(2)}) copy-start(s32[1,1,4096]{2,1,0:T(1,128)} %param.14) | copy-start | bytes 49156
  238.1 4.4 collective-permute-start.13
  241.2 4.7 collective-permute-start.12
  245.9 5.5 collective-permute-start.15
  249.4 5.0 collective-permute-start.14
  254.7 20.3 %copy-start.10 = (s32[1,1,4096]{2,1,0:T(1,128)S(1)}, s32[1,1,4096]{2,1,0:T(1,128)}, u32[]{:S(2)}) copy-start(s32[1,1,4096]{2,1,0:T(1,128)} %param.15) | copy-start | bytes 49156
  254.8 13.3 %collective-permute-start.16 = (f32[3,10,26,1]{3,2,1,0:T(8,128)S(1)}, f32[3,10,26,1]{3,2,1,0:T(8,128)S(1)}, u32[]{:S(2)}, u32[]{:S(2)}) collective-permute-start(f32[3,10,26,1]{3,2,1,0:T(8,128)S(1)} %get-tuple-element.17), channel_id=1, source_target_pairs={{1,0},{3,2},{5,4},{7,6},{9,8},{11,10},{13,12},{15,14},{17,16},{19,... | collective-permute-start | bytes 9368 | tf_op jit(solution)/shard_map/ppermute | solution.py:24
  256.1 13.8 %collective-permute-start.17 = (f32[3,10,26,1]{3,2,1,0:T(8,128)S(1)}, f32[3,10,26,1]{3,2,1,0:T(8,128)S(1)}, u32[]{:S(2)}, u32[]{:S(2)}) collective-permute-start(f32[3,10,26,1]{3,2,1,0:T(8,128)S(1)} %get-tuple-element.18), channel_id=1, source_target_pairs={{0,1},{2,3},{4,5},{6,7},{8,9},{10,11},{12,13},{14,15},{16,17},{18,... | collective-permute-start | bytes 9368 | tf_op jit(solution)/shard_map/ppermute | solution.py:22
  270.4 9.8 %collective-permute-start.19 = (f32[3,1,24,128]{3,2,1,0:T(8,128)S(1)}, f32[3,1,24,128]{3,2,1,0:T(8,128)S(1)}, u32[]{:S(2)}, u32[]{:S(2)}) collective-permute-start(f32[3,1,24,128]{3,2,1,0:T(8,128)S(1)} %get-tuple-element.27), channel_id=1, source_target_pairs={{0,16},{16,32},{32,48},{48,64},{64,80},{80,96},{96,112},{112,128},... | collective-permute-start | bytes 110600 | tf_op jit(solution)/shard_map/ppermute | solution.py:22
  273.7 6.5 %collective-permute-start.18 = (f32[3,1,24,128]{3,2,1,0:T(8,128)S(1)}, f32[3,1,24,128]{3,2,1,0:T(8,128)S(1)}, u32[]{:S(2)}, u32[]{:S(2)}) collective-permute-start(f32[3,1,24,128]{3,2,1,0:T(8,128)S(1)} %get-tuple-element.28), channel_id=1, source_target_pairs={{16,0},{32,16},{48,32},{64,48},{80,64},{96,80},{112,96},{128,112},... | collective-permute-start | bytes 110600 | tf_op jit(solution)/shard_map/ppermute | solution.py:24
  280.2 29.5 %collective-permute-start.21 = (f32[3,10,1,128]{3,2,1,0:T(1,128)S(1)}, f32[3,10,1,128]{3,2,1,0:T(1,128)S(1)}, u32[]{:S(2)}, u32[]{:S(2)}) collective-permute-start(f32[3,10,1,128]{3,2,1,0:T(1,128)S(1)} %get-tuple-element.21), channel_id=1, source_target_pairs={{0,2},{2,4},{4,6},{6,8},{8,10},{10,12},{12,14},{1,3},{3,5},{5,7},{... | collective-permute-start | bytes 46088 | tf_op jit(solution)/shard_map/ppermute | solution.py:22
  284.7 25.0 %collective-permute-start.20 = (f32[3,10,1,128]{3,2,1,0:T(1,128)S(1)}, f32[3,10,1,128]{3,2,1,0:T(1,128)S(1)}, u32[]{:S(2)}, u32[]{:S(2)}) collective-permute-start(f32[3,10,1,128]{3,2,1,0:T(1,128)S(1)} %get-tuple-element.22), channel_id=1, source_target_pairs={{2,0},{4,2},{6,4},{8,6},{10,8},{12,10},{14,12},{3,1},{5,3},{7,5},{... | collective-permute-start | bytes 46088 | tf_op jit(solution)/shard_map/ppermute | solution.py:24
  310.0 12.6 %collective-permute-start.22 = (f32[3,10,26,1]{3,2,1,0:T(8,128)S(1)}, f32[3,10,26,1]{3,2,1,0:T(8,128)S(1)}, u32[]{:S(2)}, u32[]{:S(2)}) collective-permute-start(f32[3,10,26,1]{3,2,1,0:T(8,128)S(1)} %get-tuple-element.15), channel_id=1, source_target_pairs={{1,0},{3,2},{5,4},{7,6},{9,8},{11,10},{13,12},{15,14},{17,16},{19,... | collective-permute-start | bytes 9368 | tf_op jit(solution)/shard_map/ppermute | solution.py:24
  311.3 13.1 %collective-permute-start.23 = (f32[3,10,26,1]{3,2,1,0:T(8,128)S(1)}, f32[3,10,26,1]{3,2,1,0:T(8,128)S(1)}, u32[]{:S(2)}, u32[]{:S(2)}) collective-permute-start(f32[3,10,26,1]{3,2,1,0:T(8,128)S(1)} %get-tuple-element.16), channel_id=1, source_target_pairs={{0,1},{2,3},{4,5},{6,7},{8,9},{10,11},{12,13},{14,15},{16,17},{18,... | collective-permute-start | bytes 9368 | tf_op jit(solution)/shard_map/ppermute | solution.py:22
  324.9 6.6 %copy-start.4 = (f32[3,8,24,128]{3,2,1,0:T(8,128)}, f32[3,8,24,128]{3,2,1,0:T(8,128)S(1)}, u32[]{:S(2)}) copy-start(f32[3,8,24,128]{3,2,1,0:T(8,128)S(1)} %fusion.16) | copy-start | bytes 884740
Sparse Core Ops, SparseCore 0:
  525.6 83.1 reduce-scatter.1
where the time goes:
time: 626 us; the launch traced here: 616 us
  other arithmetic  259 us (41%)
  local copies, waits for them, and re-layouts  143 us (23%)
  waiting for transfers between devices  114 us (18%)
  starting transfers between devices  85.5 us (14%)
  between operations  15.1 us (2%)
    scatter-add x3, other arithmetic, per_device(): jnp.zeros((3, girth_total * PROWS_DEV), jnp.float32).at[:, patch_ids]  111 us
    convert_element_type x1, other arithmetic, per_device(): cell_ids = arrived[3].astype(jnp.int32)  91.6 us
    reduce_scatter x1, waiting for transfers between devices, per_device(): lax.psum_scatter(partial_grid, ('gy', 'gz'), scatter_dimension=1, tiled=T...  83.3 us
    reshape x1, local copies, waits for them, and re-layouts, per_device(): partial_grid = partial_grid.reshape(3, girth_total, PROWS_DEV)  70.7 us
    ppermute x12, starting transfers between devices, with_halo(): lax.ppermute(tail, axis, [(i, (i + 1) % count) for i in range(ends)])  50.1 us
    gather x2, local copies, waits for them, and re-layouts, per_device(): hull_values = flat_field[:, hull_ids] * flat_stiff[hull_ids]  38.4 us
    scatter-add x1, other arithmetic, per_device(): jnp.zeros((3, cells_x * cells_y * cells_z), jnp.float32).at[:, cell_ids]  27.8 us
    ppermute x12, waiting for transfers between devices, with_halo(): lax.ppermute(head, axis, [((i + 1) % count, i) for i in range(ends)])  27.2 us
  transfers between devices with their start and end apart: 26, of which 9 were waited for; matrix products, arithmetic and copies ran while one was open for 32% of the time, Pallas kernels for 0%

commit v1 on v0

v1 whole, which is shorter than its diff:
```python
import jax
import jax.numpy as jnp
from jax import lax
from jax.experimental import pallas as pl
from jax.experimental.pallas import tpu as pltpu
from jax.sharding import PartitionSpec as P

CX, CY, CZ = 8, 24, 128
LANES = 128
SLOTS = 4096
SLOT_ROWS = SLOTS // LANES
BLOCKS = 128
CAP = 32
HULL_DESTS = 16
PATCH_BLOCK = 64 * 256
HULL_ROWS = 3
HULL_CAP = HULL_ROWS * LANES - 1
Y_ROWS = 20
Y_FIELDS = ((0, 3), (3, 3), (6, 3), (9, 3), (12, 2), (14, 2), (16, 2), (18, 2))
Z_ROWS = 24
EXT_X = CX + 6
EXT_Y = 32
RELAX = 0.8

f32, bf16, i32 = jnp.float32, jnp.bfloat16, jnp.int32
PARAMS = pltpu.CompilerParams(vmem_limit_bytes=56 * 1024 * 1024)


def iota(shape, dim):
    return lax.broadcasted_iota(i32, shape, dim)


def halves(values):
    high = values.astype(bf16).astype(f32)
    return high, values - high


def dot_last(a, b):
    return lax.dot_general(a, b, (((1,), (1,)), ((), ())), preferred_element_type=f32)


def pack_slots(values_ref, cells_ref, counts_ref, out_ref):
    counts = counts_ref[...].astype(f32)
    spread = jnp.where(iota((SLOT_ROWS, BLOCKS), 1) // 4 == iota((SLOT_ROWS, BLOCKS), 0), counts, 0.0)
    place = jnp.where(iota((BLOCKS, LANES), 0) % 4 == iota((BLOCKS, LANES), 1) // CAP, 1.0, 0.0)
    limits = jnp.dot(spread.astype(bf16), place.astype(bf16), preferred_element_type=f32)
    lane = iota((SLOT_ROWS, LANES), 1)
    live = (lane % CAP).astype(f32) < limits
    parts = [jnp.where(live, values_ref[c], 0.0) for c in range(3)] + [cells_ref[...].astype(f32)]
    quarter = lane // CAP
    row = iota((SLOT_ROWS, LANES), 0)
    for q in range(4):
        message = jnp.zeros((SLOT_ROWS, LANES), f32)
        for c in range(4):
            turned = parts[c] if c == q else pltpu.roll(parts[c], (c - q) * CAP % LANES, 1)
            message = jnp.where(quarter == c, turned, message)
        below = jnp.where(row >= 2, pltpu.roll(message, 2, 0), 0.0)
        above = jnp.where(row < SLOT_ROWS - 2, pltpu.roll(message, SLOT_ROWS - 2, 0), 0.0)
        out_ref[pl.ds(3 * q, SLOT_ROWS, stride=12), :] = below
        out_ref[pl.ds(3 * q + 1, SLOT_ROWS, stride=12), :] = message
        out_ref[pl.ds(3 * q + 2, SLOT_ROWS, stride=12), :] = above


def scatter_slots(slots_ref, field_ref, stiff_ref, mass_ref, xlow_ref, xhigh_ref, source_ref, ylow_ref, yhigh_ref, rows_s, lanes_s, left_s, right_s):
    lane = iota((SLOT_ROWS, LANES), 1)
    quarter = lane // CAP
    own_rows = CY * CX
    side_rows = CY * 2

    def unpack(k):
        parts = [jnp.zeros((SLOT_ROWS, LANES), f32) for _ in range(4)]
        for q in range(4):
            message = slots_ref[pl.ds(3 * q + k, SLOT_ROWS, stride=12), :]
            for c in range(4):
                turned = message if c == q else pltpu.roll(message, (q - c) * CAP % LANES, 1)
                parts[c] = jnp.where(quarter == q, turned, parts[c])
        ids = parts[3].astype(i32)
        pieces = []
        for c in range(3):
            pieces.extend(halves(parts[c]))
        return ids // LANES, ids % LANES, pieces

    lane_number = iota((LANES, LANES), 0)
    row_number = iota((own_rows, LANES), 0)
    side_number = iota((side_rows, LANES), 0)
    rows, lanes, pieces = unpack(1)
    for r in range(SLOT_ROWS):
        cut = slice(r * LANES, (r + 1) * LANES)
        rows_s[:, cut] = jnp.where(row_number == rows[r : r + 1, :], 1.0, 0.0).astype(bf16)
        here = lane_number == lanes[r : r + 1, :]
        for n in range(6):
            lanes_s[n * LANES : (n + 1) * LANES, cut] = jnp.where(here, pieces[n][r : r + 1, :], 0.0).astype(bf16)
    sums = dot_last(rows_s[...], lanes_s[...])
    for c in range(3):
        one = sums[:, 2 * c * LANES : (2 * c + 1) * LANES] + sums[:, (2 * c + 1) * LANES : (2 * c + 2) * LANES]
        source_ref[c, 2 : 2 + CX] = one.reshape(CX, CY, LANES)
    for k, first, target in ((0, own_rows - side_rows, 0), (2, 0, 2 + CX)):
        rows, lanes, pieces = unpack(k)
        for r in range(SLOT_ROWS):
            cut = slice(r * LANES, (r + 1) * LANES)
            here = side_number == rows[r : r + 1, :] - first
            for n in range(6):
                left_s[n * side_rows : (n + 1) * side_rows, cut] = jnp.where(here, pieces[n][r : r + 1, :], 0.0).astype(bf16)
            right_s[:, cut] = jnp.where(lane_number == lanes[r : r + 1, :], 1.0, 0.0).astype(bf16)
        sums = dot_last(left_s[...], right_s[...])
        for c in range(3):
            one = sums[2 * c * side_rows : (2 * c + 1) * side_rows] + sums[(2 * c + 1) * side_rows : (2 * c + 2) * side_rows]
            source_ref[c, target : target + 2] = one.reshape(2, CY, LANES)
    for out_ref, low in ((ylow_ref, True), (yhigh_ref, False)):
        for number, (start, width) in enumerate(Y_FIELDS):
            rows = slice(0, width) if low else slice(CY - width, CY)
            here = slice(start, start + width)
            if number >= 5:
                out_ref[:, here, :] = source_ref[number - 5, :, rows, :]
                continue
            if number < 4:
                before, after = slice(3 * number + 1, 3 * number + 3), slice(3 * number, 3 * number + 2)
            else:
                before = after = slice(12, 14)
            own = field_ref.at[number] if number < 3 else (stiff_ref if number == 3 else mass_ref)
            out_ref[0:2, here, :] = xlow_ref[before, rows, :]
            out_ref[2 : 2 + CX, here, :] = own[:, rows, :]
            out_ref[2 + CX :, here, :] = xhigh_ref[after, rows, :]


def route_hull(cells_ref, patches_ref, where_ref, ids_ref, rows_s, lanes_s):
    patches = patches_ref[...]
    cells = cells_ref[...]
    dest = patches // PATCH_BLOCK
    local = patches % PATCH_BLOCK
    hits = [jnp.where(dest == d, 1.0, 0.0) for d in range(HULL_DESTS)]
    stacked = jnp.concatenate(hits, axis=0).astype(bf16)
    upto = jnp.where(iota((LANES, LANES), 0) <= iota((LANES, LANES), 1), 1.0, 0.0).astype(bf16)
    total = HULL_DESTS * SLOT_ROWS
    within = jnp.dot(stacked, upto, preferred_element_type=f32)
    row_sums = jnp.dot(stacked, jnp.ones((LANES, LANES), bf16), preferred_element_type=f32)
    a, b = iota((total, total), 0), iota((total, total), 1)
    earlier = jnp.where((a // SLOT_ROWS == b // SLOT_ROWS) & (b < a), 1.0, 0.0).astype(bf16)
    offsets = jnp.dot(earlier, row_sums.astype(bf16), preferred_element_type=f32)
    rank = jnp.zeros((SLOT_ROWS, LANES), f32)
    for d in range(HULL_DESTS):
        cut = slice(d * SLOT_ROWS, (d + 1) * SLOT_ROWS)
        rank = rank + hits[d] * (within[cut] + offsets[cut] - 1.0)
    rank = rank.astype(i32)
    overflow = jnp.max(jnp.where(rank >= HULL_CAP, 1.0, 0.0))
    slot_row = jnp.where(rank < HULL_CAP, dest * HULL_ROWS + rank // LANES, -1)
    slot_lane = rank % LANES
    payload = [cells // LANES, cells % LANES, local // 256 + 1, local % 256]
    payload = [p.astype(f32) for p in payload]
    count = HULL_DESTS * HULL_ROWS
    row_number = iota((count, LANES), 0)
    lane_number = iota((LANES, LANES), 0)
    for r in range(SLOT_ROWS):
        cut = slice(r * LANES, (r + 1) * LANES)
        here = row_number == slot_row[r : r + 1, :]
        for n in range(4):
            rows_s[n * count : (n + 1) * count, cut] = jnp.where(here, payload[n][r : r + 1, :], 0.0).astype(bf16)
        lanes_s[:, cut] = jnp.where(lane_number == slot_lane[r : r + 1, :], 1.0, 0.0).astype(bf16)
    placed = dot_last(rows_s[...], lanes_s[...])
    where_ref[...] = placed[: 2 * count].astype(i32)
    ids = jnp.maximum((placed[2 * count : 3 * count] - 1.0) * 256.0 + placed[3 * count :] + 1.0, 0.0)
    last = (iota((count, LANES), 1) == LANES - 1) & (row_number % HULL_ROWS == HULL_ROWS - 1)
    ids_ref[...] = jnp.where(last, overflow, ids)


def widen(side_ref, field_ref, stiff_ref, mass_ref, source_ref, xlow_ref, xhigh_ref, ylow_ref, yhigh_ref, ext_ref, z_ref):
    side = side_ref[0]
    lane = iota((1, 1, LANES), 2)
    zeros = jnp.zeros((EXT_X, EXT_Y - CY, LANES), f32)
    total = jnp.zeros((EXT_X - 2, EXT_Y, LANES), f32)
    for number, (start, width) in enumerate(Y_FIELDS):
        target = ext_ref.at[number]
        target[:, CY:, :] = zeros
        if number >= 5:
            target[1 : EXT_X - 1, :CY, :] = source_ref[number - 5]
            target[0, :CY, :] = jnp.zeros((CY, LANES), f32)
            target[EXT_X - 1, :CY, :] = jnp.zeros((CY, LANES), f32)
        elif number == 4:
            target[0, :CY, :] = jnp.zeros((CY, LANES), f32)
            target[EXT_X - 1, :CY, :] = jnp.zeros((CY, LANES), f32)
            target[1:3, :CY, :] = xlow_ref[12:14]
            target[3 : 3 + CX, :CY, :] = mass_ref[...]
            target[3 + CX : 5 + CX, :CY, :] = xhigh_ref[12:14]
        else:
            own = field_ref.at[number] if number < 3 else stiff_ref
            target[0:3, :CY, :] = xlow_ref[3 * number : 3 * number + 3]
            target[3 : 3 + CX, :CY, :] = own[...]
            target[3 + CX :, :CY, :] = xhigh_ref[3 * number : 3 * number + 3]
        target[1 : EXT_X - 1, CY : CY + width, :] = yhigh_ref[:, start : start + width, :]
        target[1 : EXT_X - 1, EXT_Y - width :, :] = ylow_ref[:, start : start + width, :]
        shift = jnp.where(side == 0, (3 * number + 3) % LANES, 3 * number)
        turned = pltpu.roll(target[1 : EXT_X - 1].reshape((EXT_X - 2) * EXT_Y, LANES), shift, 1)
        turned = turned.reshape(EXT_X - 2, EXT_Y, LANES)
        total = jnp.where((lane >= 3 * number) & (lane < 3 * number + 3), turned, total)
    flipped = jnp.transpose(total.reshape((EXT_X - 2) * EXT_Y, LANES))
    z_ref[...] = flipped[:Z_ROWS]


def relax_and_gather(
    side_ref, ext_ref, z_ref, where_ref, ids_ref, out_ref, message_ref, first_s, second_s, stiff_s, weight_s, keep_s, couple_s, push_s, turned_s
):
    side = side_ref[0]
    wide = 2 * LANES
    rows = (EXT_X - 2) * EXT_Y
    lane = iota((1, 1, LANES), 2)
    padded = jnp.concatenate([z_ref[...], jnp.zeros((LANES - Z_ROWS, rows), f32)], axis=0)
    columns = jnp.transpose(padded)
    first_lane = jnp.where(side == 0, 0, LANES - 3)
    near = (lane >= first_lane) & (lane < first_lane + 3)

    def beyond(number):
        shift = jnp.where(side == 0, (LANES - 3 * number) % LANES, (2 * LANES - 3 - 3 * number) % LANES)
        return jnp.where(near, pltpu.roll(columns, shift, 1).reshape(EXT_X - 2, EXT_Y, LANES), 0.0)

    empty = jnp.zeros((EXT_Y, LANES), f32)
    for c in range(3):
        first_s[c, :, :, :LANES] = ext_ref[c]
        first_s[c, 1 : EXT_X - 1, :, LANES:] = beyond(c)
        first_s[c, 0, :, LANES:] = empty
        first_s[c, EXT_X - 1, :, LANES:] = empty
    stiff_s[:, :, :LANES] = ext_ref[3]
    stiff_s[1 : EXT_X - 1, :, LANES:] = beyond(3)
    stiff_s[0, :, LANES:] = empty
    stiff_s[EXT_X - 1, :, LANES:] = empty
    keep_s[:, :, :LANES] = ext_ref[4, 1 : EXT_X - 1]
    keep_s[:, :, LANES:] = beyond(4)
    for c in range(3):
        push_s[c, :, :, :LANES] = ext_ref[5 + c, 1 : EXT_X - 1]
        push_s[c, :, :, LANES:] = beyond(5 + c)

    def around(ref_at, x):
        middle = ref_at(x)
        return middle, (
            ref_at(x + 1),
            ref_at(x - 1),
            pltpu.roll(middle, EXT_Y - 1, 0),
            pltpu.roll(middle, 1, 0),
            pltpu.roll(middle, wide - 1, 1),
            pltpu.roll(middle, 1, 1),
        )

    def prepare(i, carry):
        middle, others = around(lambda x: stiff_s[x], i + 1)
        weights = [0.5 * (middle + other) for other in others]
        weight_sum = weights[0] + weights[1] + weights[2] + weights[3] + weights[4] + weights[5]
        mass = keep_s[i]
        inside = middle > 0.0
        rate = jnp.where(inside, RELAX / jnp.where(inside, weight_sum + 1.25 * mass, 1.0), 0.0)
        for n in range(6):
            weight_s[n, i] = rate * weights[n]
        keep_s[i] = jnp.where(inside, 1.0 - rate * (weight_sum + mass), 0.0)
        couple_s[i] = 0.25 * rate * mass
        for c in range(3):
            push_s[c, i] = rate * push_s[c, i]
        return carry

    lax.fori_loop(0, EXT_X - 2, prepare, 0)

    def sweep(source, target, lowest, highest):
        def one(x, carry):
            i = x - 1
            gathered = [around(lambda y, c=c: source[c, y], x) for c in range(3)]
            shared = couple_s[i] * (gathered[0][0] + gathered[1][0] + gathered[2][0])
            for c in range(3):
                middle, others = gathered[c]
                value = keep_s[i] * middle + (push_s[c, i] - shared)
                for n in range(6):
                    value = value + weight_s[n, i] * others[n]
                target[c, x] = value
            return carry

        lax.fori_loop(lowest, highest, one, 0)

    sweep(first_s, second_s, 1, EXT_X - 1)
    sweep(second_s, first_s, 2, EXT_X - 2)
    sweep(first_s, second_s, 3, EXT_X - 3)

    own_rows = CX * CY
    blank = jnp.zeros((2 * LANES - own_rows, LANES), f32)
    for c in range(3):
        result = second_s[c, 3 : 3 + CX, :CY, :LANES]
        out_ref[c] = result
        scaled = (result * stiff_s[3 : 3 + CX, :CY, :LANES]).reshape(own_rows, LANES)
        high, low = halves(scaled)
        cut = slice(c * LANES, (c + 1) * LANES)
        turned_s[cut, : 2 * LANES] = jnp.transpose(jnp.concatenate([high, blank], axis=0)).astype(bf16)
        turned_s[cut, 2 * LANES :] = jnp.transpose(jnp.concatenate([low, blank], axis=0)).astype(bf16)
    count = HULL_DESTS * HULL_ROWS
    row_number = iota((2 * LANES, LANES), 0)
    lane_number = iota((LANES, LANES), 0)
    for d in range(HULL_DESTS):
        chosen = []
        for i in range(HULL_ROWS):
            r = d * HULL_ROWS + i
            chosen.append(jnp.where(row_number == where_ref[r : r + 1, :], 1.0, 0.0).astype(bf16))
        chosen = jnp.concatenate(chosen, axis=1)
        found = jnp.dot(turned_s[...], jnp.concatenate([chosen, chosen], axis=0), preferred_element_type=f32)
        for i in range(HULL_ROWS):
            r = d * HULL_ROWS + i
            here = lane_number == where_ref[count + r : count + r + 1, :]
            for c in range(3):
                part = found[c * LANES : (c + 1) * LANES, i * LANES : (i + 1) * LANES]
                value = jnp.sum(jnp.where(here, part, 0.0), axis=0, keepdims=True)
                spot = d * 4 * HULL_ROWS + c * HULL_ROWS + i
                message_ref[spot : spot + 1, :] = value
            spot = d * 4 * HULL_ROWS + 3 * HULL_ROWS + i
            message_ref[spot : spot + 1, :] = ids_ref[r : r + 1, :]


def scatter_hull(nodes_ref, out_ref):
    row_number = iota((64, LANES), 0)
    column_number = iota((256, LANES), 0)
    sums = jnp.zeros((6 * 64, 256), f32)
    for s in range(HULL_DESTS):
        lefts, rights = [], []
        for i in range(HULL_ROWS):
            base = s * 4 * HULL_ROWS + i
            ids = nodes_ref[base + 3 * HULL_ROWS : base + 3 * HULL_ROWS + 1, :].astype(i32) - 1
            here = row_number == (ids >> 8)
            pieces = []
            for c in range(3):
                values = nodes_ref[base + c * HULL_ROWS : base + c * HULL_ROWS + 1, :]
                pieces.extend(jnp.where(here, part, 0.0).astype(bf16) for part in halves(values))
            lefts.append(jnp.concatenate(pieces, axis=0))
            rights.append(jnp.where(column_number == (ids & 255), 1.0, 0.0).astype(bf16))
        sums = sums + dot_last(jnp.concatenate(lefts, axis=1), jnp.concatenate(rights, axis=1))
    for c in range(3):
        out_ref[c] = sums[2 * c * 64 : (2 * c + 1) * 64] + sums[(2 * c + 1) * 64 : (2 * c + 2) * 64]


def shaped(*shape, dtype=f32):
    return jax.ShapeDtypeStruct(shape, dtype)


def call(kernel, outs, scratch, cost, *args, scalars=0):
    specs = [pl.BlockSpec(memory_space=pltpu.SMEM)] * scalars + [pl.BlockSpec(memory_space=pltpu.VMEM)] * (len(args) - scalars)
    many = isinstance(outs, tuple)
    vmem = pl.BlockSpec(memory_space=pltpu.VMEM)
    return pl.pallas_call(
        kernel,
        out_shape=outs,
        in_specs=specs,
        out_specs=tuple(vmem for _ in outs) if many else vmem,
        scratch_shapes=[pltpu.VMEM(shape, dtype) for shape, dtype in scratch],
        compiler_params=PARAMS,
        cost_estimate=pl.CostEstimate(flops=cost, bytes_accessed=1 << 20, transcendentals=0),
        name=kernel.__name__,
    )(*args)


def step(axis, values, up):
    count = lax.axis_size(axis)
    pairs = [(i, i + 1) if up else (i + 1, i) for i in range(count - 1)]
    return lax.ppermute(values, axis, pairs)


def per_device(start_field, stiffness, mass, sens_values, sens_cells, sens_counts, hull_cells, hull_patches):
    last = jnp.concatenate([start_field[:, CX - 3 :].reshape(9, CY, CZ), stiffness[CX - 3 :], mass[CX - 2 :]], axis=0)
    first = jnp.concatenate([start_field[:, :3].reshape(9, CY, CZ), stiffness[:3], mass[:2]], axis=0)
    xlow = step("gx", last, True)
    xhigh = step("gx", first, False)
    packed = call(
        pack_slots,
        shaped(3 * BLOCKS, LANES),
        [],
        1 << 20,
        sens_values.reshape(3, SLOT_ROWS, LANES),
        sens_cells.reshape(SLOT_ROWS, LANES),
        sens_counts.reshape(1, BLOCKS),
    )
    arrived = lax.all_to_all(packed, ("gx", "gy"), split_axis=0, concat_axis=0, tiled=True)
    source, first_rows, last_rows = call(
        scatter_slots,
        (shaped(3, CX + 4, CY, CZ), shaped(CX + 4, Y_ROWS, CZ), shaped(CX + 4, Y_ROWS, CZ)),
        [((CX * CY, SLOTS), bf16), ((6 * LANES, SLOTS), bf16), ((12 * CY, SLOTS), bf16), ((LANES, SLOTS), bf16)],
        1 << 32,
        arrived,
        start_field,
        stiffness,
        mass,
        xlow,
        xhigh,
    )
    ylow = step("gy", last_rows, True)
    yhigh = step("gy", first_rows, False)
    count = HULL_DESTS * HULL_ROWS
    where, ids = call(
        route_hull,
        (shaped(2 * count, LANES, dtype=i32), shaped(count, LANES)),
        [((4 * count, SLOTS), bf16), ((LANES, SLOTS), bf16)],
        1 << 31,
        hull_cells.reshape(SLOT_ROWS, LANES),
        hull_patches.reshape(SLOT_ROWS, LANES),
    )
    side = lax.axis_index("gz").astype(i32).reshape(1)
    rows = (EXT_X - 2) * EXT_Y
    ext, faces = call(
        widen,
        (shaped(8, EXT_X, EXT_Y, CZ), shaped(Z_ROWS, rows)),
        [],
        1 << 20,
        side,
        start_field,
        stiffness,
        mass,
        source,
        xlow,
        xhigh,
        ylow,
        yhigh,
        scalars=1,
    )
    faces = lax.ppermute(faces, "gz", [(0, 1), (1, 0)])
    wide = (EXT_X - 2, EXT_Y, 2 * CZ)
    full = (EXT_X, EXT_Y, 2 * CZ)
    field, outgoing = call(
        relax_and_gather,
        (shaped(3, CX, CY, CZ), shaped(4 * count, LANES)),
        [
            ((3,) + full, f32),
            ((3,) + full, f32),
            (full, f32),
            ((6,) + wide, f32),
            (wide, f32),
            (wide, f32),
            ((3,) + wide, f32),
            ((3 * LANES, 4 * LANES), bf16),
        ],
        1 << 32,
        side,
        ext,
        faces,
        where,
        ids,
        scalars=1,
    )
    nodes = lax.all_to_all(outgoing, ("gy", "gz"), split_axis=0, concat_axis=0, tiled=True)
    overflow = jnp.max(nodes.reshape(HULL_DESTS, 4 * HULL_ROWS, LANES)[:, -1, -1])

    def in_messages():
        return call(scatter_hull, shaped(3, 64, 256), [], 1 << 32, nodes)

    def every_node():
        cells = hull_cells[0, 0]
        values = field.reshape(3, -1)[:, cells] * stiffness.reshape(-1)[cells]
        sent = jnp.concatenate([values, hull_patches[0].astype(f32)], axis=0)
        sent = jnp.broadcast_to(sent[None], (HULL_DESTS,) + sent.shape)
        got = lax.all_to_all(sent, ("gy", "gz"), split_axis=0, concat_axis=0, tiled=True)
        got = jnp.swapaxes(got, 0, 1).reshape(4, -1)
        spots = got[3].astype(i32) - lax.axis_index(("gy", "gz")) * PATCH_BLOCK
        mine = (spots >= 0) & (spots < PATCH_BLOCK)
        added = jnp.where(mine, got[:3], 0.0)
        patch = jnp.zeros((3, PATCH_BLOCK), f32).at[:, jnp.where(mine, spots, 0)].add(added)
        return patch.reshape(3, 64, 256)

    patch = lax.cond(overflow > 0.0, every_node, in_messages)
    return field, patch


def solution(mesh):
    placed = (
        P(None, "gx", "gy", "gz"),
        P("gx", "gy", "gz"),
        P("gx", "gy", "gz"),
        P(None, "gz", ("gx", "gy"), None),
        P("gz", ("gx", "gy"), None),
        P("gz", ("gx", "gy"), None),
        P("gx", ("gy", "gz"), None),
        P("gx", ("gy", "gz"), None),
    )
    return jax.shard_map(
        per_device,
        mesh=mesh,
        in_specs=placed,
        out_specs=(P(None, "gx", "gy", "gz"), P(None, ("gy", "gz"), "gx")),
        check_vma=False,
    )
```

time: 626 us -> 92.4 us (0.15); the launches traced: 616 us -> 91.5 us
  other arithmetic: 259 us -> 0.72 us
  local copies, waits for them, and re-layouts: 143 us -> 10.5 us
  waiting for transfers between devices: 114 us -> 20.5 us
  starting transfers between devices: 85.5 us -> 29.2 us
  Pallas kernels: 0 us -> 29.1 us
  between operations: 15.1 us -> 1.41 us
    scatter-add x4 -> x0, other arithmetic: 139 us -> none  [the longest x3 111 us: per_device(): jnp.zeros((3, girth_total * PROWS_DEV), jnp.float32).at[:, patch_ids]]
    convert_element_type x1 -> x0, other arithmetic: 91.6 us -> none  [per_device(): cell_ids = arrived[3].astype(jnp.int32)]
    reduce_scatter x1 -> x0, waiting for transfers between devices: 83.3 us -> none  [per_device(): lax.psum_scatter(partial_grid, ('gy', 'gz'), scatter_dimension=1, tiled=T...]
    reshape x3 -> x0, local copies, waits for them, and re-layouts: 78.4 us -> none  [the longest x1 70.7 us: per_device(): partial_grid = partial_grid.reshape(3, girth_total, PROWS_DEV)]
    ppermute x24 -> x5, starting transfers between devices: 68 us -> 9.44 us  [the longest x4 9.04 us: step(): return lax.ppermute(values, axis, pairs)]
    gather x2 -> x0, local copies, waits for them, and re-layouts: 38.4 us -> none  [per_device(): hull_values = flat_field[:, hull_ids] * flat_stiff[hull_ids]]
    pallas_call x0 -> x6, Pallas kernels: none -> 29.1 us  [call(): pl.pallas_call(kernel, out_shape=outs, in_specs=specs, out_specs=tuple((v...]
    ppermute x24 -> x5, waiting for transfers between devices: 30.8 us -> 4.97 us  [the longest x4 4.72 us: step(): return lax.ppermute(values, axis, pairs)]
  transfers between devices with their start and end apart: 26 -> 7, of which waited for: 9 -> 5; matrix products, arithmetic and copies ran while one was open for 32% -> 3% of each run, Pallas kernels for 0% -> 3%
where the time goes in v1:
time: 92.4 us; the launch traced here: 91.5 us
  starting transfers between devices  29.2 us (32%)
  Pallas kernels  29.1 us (31%)
  waiting for transfers between devices  20.5 us (22%)
  local copies, waits for them, and re-layouts  10.5 us (11%)
  between operations  1.41 us (2%)
    pallas_call x6, Pallas kernels, call(): pl.pallas_call(kernel, out_shape=outs, in_specs=specs, out_specs=tuple((v...  29.1 us
    all_to_all x1, starting transfers between devices, per_device(): lax.all_to_all(packed, ('gx', 'gy'), split_axis=0, concat_axis=0, tiled=T...  16.4 us
    all_to_all x1, waiting for transfers between devices, per_device(): lax.all_to_all(packed, ('gx', 'gy'), split_axis=0, concat_axis=0, tiled=T...  9.3 us
    ppermute x4, starting transfers between devices, step(): return lax.ppermute(values, axis, pairs)  9.04 us
    all_to_all x1, waiting for transfers between devices, per_device(): lax.all_to_all(outgoing, ('gy', 'gz'), split_axis=0, concat_axis=0, tiled...  6.25 us
    ppermute x4, waiting for transfers between devices, step(): return lax.ppermute(values, axis, pairs)  4.72 us
    all_to_all x1, starting transfers between devices, per_device(): lax.all_to_all(outgoing, ('gy', 'gz'), split_axis=0, concat_axis=0, tiled...  3.41 us
    unnamed x18, local copies, waits for them, and re-layouts  3.26 us
  transfers between devices with their start and end apart: 7, of which 5 were waited for; matrix products, arithmetic and copies ran while one was open for 3% of the time, Pallas kernels for 3%

profile of v1, /device:TPU:1, one launch (start us, length us, event | category | flops | bytes accessed | tf_op | source)
XLA Modules:
  0.0 91.5 jit_solution(2236874613167105652)
XLA Ops:
  0.6 1.7 %pack_slots.1 = f32[384,128]{1,0:T(8,128)} custom-call(f32[3,32,128]{2,1,0:T(8,128)} %bitcast.39, s32[32,128]{1,0:T(8,128)} %bitcast.40, s32[1,128]{1,0:T(1,128)} %bitcast.43), custom_call_target="tpu_custom_call" | custom-call | flops 1048576 | bytes 1048576 | tf_op jit(solution)/shard_map/pack_slots/pallas_call | solution.py:339
  2.4 1.7 %all_to_all.21 = f32[128,3,128]{2,1,0:T(4,128)} reshape(f32[384,128]{1,0:T(8,128)} %pack_slots.1) | data formatting | bytes 393216 | tf_op jit(solution)/shard_map/all_to_all | solution.py:371
  4.1 16.4 %all-to-all-start.1 = ((f32[128,3,128]{2,1,0:T(4,128)}), f32[128,3,128]{2,1,0:T(4,128)S(1)}, u32[]{:S(2)}, u32[]{:S(2)}) async-start(f32[128,3,128]{2,1,0:T(4,128)} %all_to_all.21), calls=%async_computation.1 | async-start | bytes 524288 | tf_op jit(solution)/shard_map/all_to_all | solution.py:371
  20.5 0.8 fusion.6
  21.2 0.8 fusion.5
  22.0 1.0 %fusion.4 = (f32[3,3,24,128]{3,2,1,0:T(8,128)S(1)}, f32[3,3,24,128]{3,2,1,0:T(8,128)S(1)}) fusion(f32[3,8,24,128]{3,2,1,0:T(8,128)} %field_ref.3), kind=kLoop, calls=%fused_computation.19 | loop fusion | bytes 442368 | tf_op jit(solution)/shard_map/slice | solution.py:359
  23.0 0.0 copy-start
  23.0 3.4 %collective-permute-start = (f32[14,24,128]{2,1,0:T(8,128)S(1)}, f32[14,24,128]{2,1,0:T(8,128)S(1)}, u32[]{:S(2)}, u32[]{:S(2)}) collective-permute-start(f32[14,24,128]{2,1,0:T(8,128)S(1)} %pad_maximum_fusion.1), channel_id=1, source_target_pairs={{0,16},{16,32},{32,48},{48,64},{64,80},{80,96},{96,112},{112,128},... | collective-permute-start | bytes 516104 | tf_op jit(solution)/shard_map/ppermute | solution.py:354
  26.5 1.3 %collective-permute-start.1 = (f32[14,24,128]{2,1,0:T(8,128)S(1)}, f32[14,24,128]{2,1,0:T(8,128)S(1)}, u32[]{:S(2)}, u32[]{:S(2)}) collective-permute-start(f32[14,24,128]{2,1,0:T(8,128)S(1)} %pad_maximum_fusion.2), channel_id=1, source_target_pairs={{16,0},{32,16},{48,32},{64,48},{80,64},{96,80},{112,96},{128,112},... | collective-permute-start | bytes 516104 | tf_op jit(solution)/shard_map/ppermute | solution.py:354
  27.8 9.3 %all-to-all-done.1 = f32[128,3,128]{2,1,0:T(4,128)S(1)} async-done(((f32[128,3,128]{2,1,0:T(4,128)}), f32[128,3,128]{2,1,0:T(4,128)S(1)}, u32[]{:S(2)}, u32[]{:S(2)}) %all-to-all-start.1) | async-done | bytes 196640 | tf_op jit(solution)/shard_map/all_to_all | solution.py:371
  37.1 0.8 all_to_all.23.slots_ref
  37.9 0.0 copy-start.5
  37.9 0.0 copy-start.6
  37.9 0.0 collective-permute-done.xlow_ref
  37.9 0.0 copy-start.1
  37.9 0.0 collective-permute-done.1.xhigh_ref
  37.9 0.7 copy-done.1
  38.6 0.0 copy-start.2
  38.6 0.7 copy-done.2
  39.2 7.3 %scatter_slots.1 = (f32[3,12,24,128]{3,2,1,0:T(8,128)}, f32[12,20,128]{2,1,0:T(8,128)}, f32[12,20,128]{2,1,0:T(8,128)}) custom-call(f32[384,128]{1,0:T(8,128)} %all_to_all.23.slots_ref, f32[3,8,24,128]{3,2,1,0:T(8,128)} %field_ref.3, f32[8,24,128]{2,1,0:T(8,128)} %stiff_ref.3, f32[8,24,128]{2,1,0:T(8,128)} %mass_ref.3, f32[14,24,128]{2,1,0:T(8,128)} %copy-done.1, ...), custom_call_target="tpu_custom_call" | custom-call | flops 4294967296 | bytes 1048576 | tf_op jit(solution)/shard_map/scatter_slots/pallas_call | solution.py:339
  46.5 2.4 %collective-permute-start.2 = (f32[12,20,128]{2,1,0:T(8,128)}, f32[12,20,128]{2,1,0:T(8,128)S(1)}, u32[]{:S(2)}, u32[]{:S(2)}) collective-permute-start(f32[12,20,128]{2,1,0:T(8,128)} %get-tuple-element.29), channel_id=1, source_target_pairs={{0,2},{2,4},{4,6},{6,8},{8,10},{10,12},{12,14},{1,3},{3,5},{5,7},{... | collective-permute-start | bytes 368648 | tf_op jit(solution)/shard_map/ppermute | solution.py:354
  48.9 1.9 %collective-permute-start.3 = (f32[12,20,128]{2,1,0:T(8,128)}, f32[12,20,128]{2,1,0:T(8,128)S(1)}, u32[]{:S(2)}, u32[]{:S(2)}) collective-permute-start(f32[12,20,128]{2,1,0:T(8,128)} %get-tuple-element.30), channel_id=1, source_target_pairs={{2,0},{4,2},{6,4},{8,6},{10,8},{12,10},{14,12},{3,1},{5,3},{7,5},{... | collective-permute-start | bytes 368648 | tf_op jit(solution)/shard_map/ppermute | solution.py:354
  50.8 0.4 collective-permute-done.2.ylow_ref
  51.3 0.0 copy-start.3
  51.3 4.3 %collective-permute-done.3.yhigh_ref = f32[12,20,128]{2,1,0:T(8,128)S(1)} collective-permute-done((f32[12,20,128]{2,1,0:T(8,128)}, f32[12,20,128]{2,1,0:T(8,128)S(1)}, u32[]{:S(2)}, u32[]{:S(2)}) %collective-permute-start.3) | collective-permute-done | bytes 122912 | tf_op jit(solution)/shard_map/ppermute | solution.py:354
  55.5 0.0 copy-start.4
  55.5 0.0 copy-done.3
  55.6 0.6 copy-done.4
  56.2 0.0 copy-done
  56.2 3.2 %widen.1 = (f32[8,14,32,128]{3,2,1,0:T(8,128)}, f32[24,384]{1,0:T(8,128)}) custom-call(s32[1]{0:T(128)} %bitcast.12.side_ref, f32[3,8,24,128]{3,2,1,0:T(8,128)} %field_ref.3, f32[8,24,128]{2,1,0:T(8,128)S(1)} %copy-done, f32[8,24,128]{2,1,0:T(8,128)} %mass_ref.3, f32[3,12,24,128]{3,2,1,0:T(8,128)} %get-tuple-element.28.source_ref, f32[14,24,128]{2,1,0:T(8,128)} %copy-done.1, ...), custom_call_target="tpu_custom_call" | custom-call | flops 1048576 | bytes 1048576 | tf_op jit(solution)/shard_map/widen/pallas_call | solution.py:339
  59.4 0.4 collective-permute-start.4
  59.8 0.0 copy-done.5
  59.8 0.0 copy-done.6
  59.8 2.4 %route_hull.1 = (s32[96,128]{1,0:T(8,128)}, f32[48,128]{1,0:T(8,128)}) custom-call(s32[32,128]{1,0:T(8,128)S(1)} %bitcast.41, s32[32,128]{1,0:T(8,128)S(1)} %bitcast.42), custom_call_target="tpu_custom_call" | custom-call | flops 2147483648 | bytes 1048576 | tf_op jit(solution)/shard_map/route_hull/pallas_call | solution.py:339
  62.2 0.3 collective-permute-done.4.z_ref
  62.4 0.0 copy-start.7
  62.4 0.6 copy-done.7
  63.0 11.8 %relax_and_gather.1 = (f32[3,8,24,128]{3,2,1,0:T(8,128)}, f32[192,128]{1,0:T(8,128)}) custom-call(s32[1]{0:T(128)} %bitcast.12.side_ref, f32[8,14,32,128]{3,2,1,0:T(8,128)} %get-tuple-element.31.ext_ref, f32[24,384]{1,0:T(8,128)} %copy-done.7, s32[96,128]{1,0:T(8,128)} %get-tuple-element.33.where_ref, f32[48,128]{1,0:T(8,128)} %get-tuple-element.34.ids_ref), custom_call_target="tpu_custom_call" | custom-call | flops 4294967296 | bytes 1048576 | tf_op jit(solution)/shard_map/relax_and_gather/pallas_call | solution.py:339
  74.9 1.6 %all_to_all.24 = f32[16,12,128]{2,1,0:T(8,128)} reshape(f32[192,128]{1,0:T(8,128)} %get-tuple-element.36) | data formatting | bytes 196608 | tf_op jit(solution)/shard_map/all_to_all | solution.py:437
  76.4 3.4 %all-to-all-start.2 = ((f32[16,12,128]{2,1,0:T(8,128)}), f32[16,12,128]{2,1,0:T(8,128)S(1)}, u32[]{:S(2)}, u32[]{:S(2)}) async-start(f32[16,12,128]{2,1,0:T(8,128)} %all_to_all.24), calls=%async_computation.2 | async-start | bytes 262144 | tf_op jit(solution)/shard_map/all_to_all | solution.py:437
  79.9 6.3 %all-to-all-done.2 = f32[16,12,128]{2,1,0:T(8,128)S(1)} async-done(((f32[16,12,128]{2,1,0:T(8,128)}), f32[16,12,128]{2,1,0:T(8,128)S(1)}, u32[]{:S(2)}, u32[]{:S(2)}) %all-to-all-start.2) | async-done | bytes 98336 | tf_op jit(solution)/shard_map/all_to_all | solution.py:437
  86.1 0.7 slice_reduce_fusion
  87.5 3.4 %conditional.1 = (f32[3,64,256]{2,1,0:T(8,128)S(1)}) conditional(s32[]{:T(128)} %convert_element_type.29, f32[16,12,128]{2,1,0:T(8,128)S(1)} %all-to-all-done.2, (f32[3,8,24,128]{3,2,1,0:T(8,128)}, s32[1,1,4096]{2,1,0:T(1,128)S(1)}, f32[8,24,128]{2,1,0:T(8,128)S(1)}, s32[1,1,4096]{2,1,0:T(1,128)S(1)}) %tuple.34), branch_computations={%region_1.0_spmd, %region_2.4_spmd} | conditional | flops 4294967296 | bytes 10502788 | solution.py:456
  87.5 0.7 all_to_all.4.nodes_ref
  88.1 2.7 %scatter_hull.1 = f32[3,64,256]{2,1,0:T(8,128)S(1)} custom-call(f32[192,128]{1,0:T(8,128)} %all_to_all.4.nodes_ref), custom_call_target="tpu_custom_call" | custom-call | flops 4294967296 | bytes 1048576 | tf_op jit(solution)/shard_map/cond/branch_0_fun/scatter_hull/pallas_call | solution.py:339
  90.8 0.0 copy-start.8
  90.8 0.7 copy-done.8
  (2 shorter events, 0.0 us)
Async XLA Ops:
  4.1 33.0 %all-to-all-start.1 = ((f32[128,3,128]{2,1,0:T(4,128)}), f32[128,3,128]{2,1,0:T(4,128)S(1)}, u32[]{:S(2)}, u32[]{:S(2)}) async-start(f32[128,3,128]{2,1,0:T(4,128)} %all_to_all.21), calls=%async_computation.1 | async-start | bytes 524288 | tf_op jit(solution)/shard_map/all_to_all | solution.py:371
  23.0 33.2 %copy-start = (f32[8,24,128]{2,1,0:T(8,128)S(1)}, f32[8,24,128]{2,1,0:T(8,128)}, u32[]{:S(2)}) copy-start(f32[8,24,128]{2,1,0:T(8,128)} %stiff_ref.3) | copy-start | bytes 294916
  23.0 14.8 %collective-permute-start = (f32[14,24,128]{2,1,0:T(8,128)S(1)}, f32[14,24,128]{2,1,0:T(8,128)S(1)}, u32[]{:S(2)}, u32[]{:S(2)}) collective-permute-start(f32[14,24,128]{2,1,0:T(8,128)S(1)} %pad_maximum_fusion.1), channel_id=1, source_target_pairs={{0,16},{16,32},{32,48},{48,64},{64,80},{80,96},{96,112},{112,128},... | collective-permute-start | bytes 516104 | tf_op jit(solution)/shard_map/ppermute | solution.py:354
  26.5 11.4 %collective-permute-start.1 = (f32[14,24,128]{2,1,0:T(8,128)S(1)}, f32[14,24,128]{2,1,0:T(8,128)S(1)}, u32[]{:S(2)}, u32[]{:S(2)}) collective-permute-start(f32[14,24,128]{2,1,0:T(8,128)S(1)} %pad_maximum_fusion.2), channel_id=1, source_target_pairs={{16,0},{32,16},{48,32},{64,48},{80,64},{96,80},{112,96},{128,112},... | collective-permute-start | bytes 516104 | tf_op jit(solution)/shard_map/ppermute | solution.py:354
  37.9 21.9 %copy-start.5 = (s32[1,1,4096]{2,1,0:T(1,128)S(1)}, s32[1,1,4096]{2,1,0:T(1,128)}, u32[]{:S(2)}) copy-start(s32[1,1,4096]{2,1,0:T(1,128)} %param.16) | copy-start | bytes 49156
  37.9 21.9 %copy-start.6 = (s32[1,1,4096]{2,1,0:T(1,128)S(1)}, s32[1,1,4096]{2,1,0:T(1,128)}, u32[]{:S(2)}) copy-start(s32[1,1,4096]{2,1,0:T(1,128)} %param.17) | copy-start | bytes 49156
  37.9 0.7 copy-start.1
  38.6 0.7 copy-start.2
  46.5 4.8 %collective-permute-start.2 = (f32[12,20,128]{2,1,0:T(8,128)}, f32[12,20,128]{2,1,0:T(8,128)S(1)}, u32[]{:S(2)}, u32[]{:S(2)}) collective-permute-start(f32[12,20,128]{2,1,0:T(8,128)} %get-tuple-element.29), channel_id=1, source_target_pairs={{0,2},{2,4},{4,6},{6,8},{8,10},{10,12},{12,14},{1,3},{3,5},{5,7},{... | collective-permute-start | bytes 368648 | tf_op jit(solution)/shard_map/ppermute | solution.py:354
  48.9 6.7 %collective-permute-start.3 = (f32[12,20,128]{2,1,0:T(8,128)}, f32[12,20,128]{2,1,0:T(8,128)S(1)}, u32[]{:S(2)}, u32[]{:S(2)}) collective-permute-start(f32[12,20,128]{2,1,0:T(8,128)} %get-tuple-element.30), channel_id=1, source_target_pairs={{2,0},{4,2},{6,4},{8,6},{10,8},{12,10},{14,12},{3,1},{5,3},{7,5},{... | collective-permute-start | bytes 368648 | tf_op jit(solution)/shard_map/ppermute | solution.py:354
  51.3 4.3 %copy-start.3 = (f32[12,20,128]{2,1,0:T(8,128)}, f32[12,20,128]{2,1,0:T(8,128)S(1)}, u32[]{:S(2)}) copy-start(f32[12,20,128]{2,1,0:T(8,128)S(1)} %collective-permute-done.2.ylow_ref) | copy-start | bytes 368644
  55.5 0.7 copy-start.4
  59.4 3.0 %collective-permute-start.4 = (f32[24,384]{1,0:T(8,128)}, f32[24,384]{1,0:T(8,128)S(1)}, u32[]{:S(2)}, u32[]{:S(2)}) collective-permute-start(f32[24,384]{1,0:T(8,128)} %get-tuple-element.32), channel_id=1, source_target_pairs={{0,1},{1,0},{2,3},{3,2},{4,5},{5,4},{6,7},{7,6},{8,9},{9,8},{10,11... | collective-permute-start | bytes 110600 | tf_op jit(solution)/shard_map/ppermute | solution.py:413
  62.4 0.6 copy-start.7
  76.4 9.7 %all-to-all-start.2 = ((f32[16,12,128]{2,1,0:T(8,128)}), f32[16,12,128]{2,1,0:T(8,128)S(1)}, u32[]{:S(2)}, u32[]{:S(2)}) async-start(f32[16,12,128]{2,1,0:T(8,128)} %all_to_all.24), calls=%async_computation.2 | async-start | bytes 262144 | tf_op jit(solution)/shard_map/all_to_all | solution.py:437
  90.8 0.7 copy-start.8

commit v2 on v1

--- a/solution.py
+++ b/solution.py
@@ -1,3 +1,5 @@
+import functools
+
 import jax
 import jax.numpy as jnp
 from jax import lax
@@ -23,7 +25,7 @@
 RELAX = 0.8
 
 f32, bf16, i32 = jnp.float32, jnp.bfloat16, jnp.int32
-PARAMS = pltpu.CompilerParams(vmem_limit_bytes=56 * 1024 * 1024)
+PARAMS = pltpu.CompilerParams(vmem_limit_bytes=24 * 1024 * 1024)
 
 
 def iota(shape, dim):
@@ -39,7 +41,25 @@
     return lax.dot_general(a, b, (((1,), (1,)), ((), ())), preferred_element_type=f32)
 
 
-def pack_slots(values_ref, cells_ref, counts_ref, out_ref):
+def pack_slots(
+    gx_ref, values_hbm, cells_hbm, counts_hbm, field_hbm, stiff_hbm, mass_hbm, out_ref, even_ref, odd_ref, values_ref, cells_ref, counts_ref, sems
+):
+    copies = [
+        pltpu.make_async_copy(values_hbm, values_ref, sems.at[0]),
+        pltpu.make_async_copy(cells_hbm, cells_ref, sems.at[1]),
+        pltpu.make_async_copy(counts_hbm, counts_ref, sems.at[2]),
+    ]
+    odd = lax.rem(gx_ref[0], 2)
+    for slab, up in ((even_ref, 1 - odd), (odd_ref, odd)):
+        planes, mass_planes = pl.ds(up * (CX - 3), 3), pl.ds(up * (CX - 2), 2)
+        for c in range(3):
+            copies.append(pltpu.make_async_copy(field_hbm.at[c, planes], slab.at[pl.ds(3 * c, 3)], sems.at[len(copies)]))
+        copies.append(pltpu.make_async_copy(stiff_hbm.at[planes], slab.at[pl.ds(9, 3)], sems.at[len(copies)]))
+        copies.append(pltpu.make_async_copy(mass_hbm.at[mass_planes], slab.at[pl.ds(12, 2)], sems.at[len(copies)]))
+    for copy in copies:
+        copy.start()
+    for copy in copies[:3]:
+        copy.wait()
     counts = counts_ref[...].astype(f32)
     spread = jnp.where(iota((SLOT_ROWS, BLOCKS), 1) // 4 == iota((SLOT_ROWS, BLOCKS), 0), counts, 0.0)
     place = jnp.where(iota((BLOCKS, LANES), 0) % 4 == iota((BLOCKS, LANES), 1) // CAP, 1.0, 0.0)
@@ -59,9 +79,11 @@
         out_ref[pl.ds(3 * q, SLOT_ROWS, stride=12), :] = below
         out_ref[pl.ds(3 * q + 1, SLOT_ROWS, stride=12), :] = message
         out_ref[pl.ds(3 * q + 2, SLOT_ROWS, stride=12), :] = above
-
-
-def scatter_slots(slots_ref, field_ref, stiff_ref, mass_ref, xlow_ref, xhigh_ref, source_ref, ylow_ref, yhigh_ref, rows_s, lanes_s, left_s, right_s):
+    for copy in copies[3:]:
+        copy.wait()
+
+
+def scatter_slots(slots_ref, source_ref, rows_s, lanes_s, left_s, right_s):
     lane = iota((SLOT_ROWS, LANES), 1)
     quarter = lane // CAP
     own_rows = CY * CX
@@ -81,7 +103,7 @@
         return ids // LANES, ids % LANES, pieces
 
     lane_number = iota((LANES, LANES), 0)
-    row_number = iota((own_rows, LANES), 0)
+    row_number = iota((2 * LANES, LANES), 0)
     side_number = iota((side_rows, LANES), 0)
     rows, lanes, pieces = unpack(1)
     for r in range(SLOT_ROWS):
@@ -90,10 +112,10 @@
         here = lane_number == lanes[r : r + 1, :]
         for n in range(6):
             lanes_s[n * LANES : (n + 1) * LANES, cut] = jnp.where(here, pieces[n][r : r + 1, :], 0.0).astype(bf16)
-    sums = dot_last(rows_s[...], lanes_s[...])
+    sums = dot_last(lanes_s[...], rows_s[...])
     for c in range(3):
-        one = sums[:, 2 * c * LANES : (2 * c + 1) * LANES] + sums[:, (2 * c + 1) * LANES : (2 * c + 2) * LANES]
-        source_ref[c, 2 : 2 + CX] = one.reshape(CX, CY, LANES)
+        one = sums[2 * c * LANES : (2 * c + 1) * LANES] + sums[(2 * c + 1) * LANES : (2 * c + 2) * LANES]
+        source_ref[c, 2 : 2 + CX] = jnp.transpose(one)[:own_rows].reshape(CX, CY, LANES)
     for k, first, target in ((0, own_rows - side_rows, 0), (2, 0, 2 + CX)):
         rows, lanes, pieces = unpack(k)
         for r in range(SLOT_ROWS):
@@ -106,21 +128,33 @@
         for c in range(3):
             one = sums[2 * c * side_rows : (2 * c + 1) * side_rows] + sums[(2 * c + 1) * side_rows : (2 * c + 2) * side_rows]
             source_ref[c, target : target + 2] = one.reshape(2, CY, LANES)
-    for out_ref, low in ((ylow_ref, True), (yhigh_ref, False)):
-        for number, (start, width) in enumerate(Y_FIELDS):
-            rows = slice(0, width) if low else slice(CY - width, CY)
-            here = slice(start, start + width)
+
+
+def by_parity(place, even, odd):
+    index, count = place
+    is_odd = lax.rem(index, 2) == 1
+    low = jnp.where(is_odd, even, odd) * jnp.where(index > 0, 1.0, 0.0)
+    high = jnp.where(is_odd, odd, even) * jnp.where(index < count - 1, 1.0, 0.0)
+    return low, high
+
+
+def pack_y(n_gx, gx_ref, gy_ref, source_ref, field_ref, stiff_ref, mass_ref, xeven_ref, xodd_ref, even_ref, odd_ref):
+    is_odd = lax.rem(gy_ref[0], 2) == 1
+    for number, (start, width) in enumerate(Y_FIELDS):
+        here = slice(start, start + width)
+        ends = slice(0, width), slice(CY - width, CY)
+        pieces = [[], []]
+        for n, rows in enumerate(ends):
             if number >= 5:
-                out_ref[:, here, :] = source_ref[number - 5, :, rows, :]
+                pieces[n].append((slice(0, CX + 4), source_ref[number - 5, :, rows, :]))
                 continue
-            if number < 4:
-                before, after = slice(3 * number + 1, 3 * number + 3), slice(3 * number, 3 * number + 2)
-            else:
-                before = after = slice(12, 14)
-            own = field_ref.at[number] if number < 3 else (stiff_ref if number == 3 else mass_ref)
-            out_ref[0:2, here, :] = xlow_ref[before, rows, :]
-            out_ref[2 : 2 + CX, here, :] = own[:, rows, :]
-            out_ref[2 + CX :, here, :] = xhigh_ref[after, rows, :]
+            planes = slice(3 * number, 3 * number + 3) if number < 4 else slice(12, 14)
+            low, high = by_parity((gx_ref[0], n_gx), xeven_ref[planes, rows, :], xodd_ref[planes, rows, :])
+            own = field_ref[number, :, rows, :] if number < 3 else (stiff_ref if number == 3 else mass_ref)[:, rows, :]
+            pieces[n].extend([(slice(0, 2), low[-2:]), (slice(2, 2 + CX), own), (slice(2 + CX, CX + 4), high[:2])])
+        for (where, first), (_, last) in zip(*pieces):
+            even_ref[where, here, :] = jnp.where(is_odd, first, last)
+            odd_ref[where, here, :] = jnp.where(is_odd, last, first)
 
 
 def route_hull(cells_ref, patches_ref, where_ref, ids_ref, rows_s, lanes_s):
@@ -163,7 +197,7 @@
     ids_ref[...] = jnp.where(last, overflow, ids)
 
 
-def widen(side_ref, field_ref, stiff_ref, mass_ref, source_ref, xlow_ref, xhigh_ref, ylow_ref, yhigh_ref, ext_ref, z_ref):
+def widen(n_gx, n_gy, gx_ref, gy_ref, side_ref, field_ref, stiff_ref, mass_ref, source_ref, xeven_ref, xodd_ref, yeven_ref, yodd_ref, ext_ref, z_ref):
     side = side_ref[0]
     lane = iota((1, 1, LANES), 2)
     zeros = jnp.zeros((EXT_X, EXT_Y - CY, LANES), f32)
@@ -178,16 +212,21 @@
         elif number == 4:
             target[0, :CY, :] = jnp.zeros((CY, LANES), f32)
             target[EXT_X - 1, :CY, :] = jnp.zeros((CY, LANES), f32)
-            target[1:3, :CY, :] = xlow_ref[12:14]
+            low, high = by_parity((gx_ref[0], n_gx), xeven_ref[12:14], xodd_ref[12:14])
+            target[1:3, :CY, :] = low
             target[3 : 3 + CX, :CY, :] = mass_ref[...]
-            target[3 + CX : 5 + CX, :CY, :] = xhigh_ref[12:14]
+            target[3 + CX : 5 + CX, :CY, :] = high
         else:
             own = field_ref.at[number] if number < 3 else stiff_ref
-            target[0:3, :CY, :] = xlow_ref[3 * number : 3 * number + 3]
+            planes = slice(3 * number, 3 * number + 3)
+            low, high = by_parity((gx_ref[0], n_gx), xeven_ref[planes], xodd_ref[planes])
+            target[0:3, :CY, :] = low
             target[3 : 3 + CX, :CY, :] = own[...]
-            target[3 + CX :, :CY, :] = xhigh_ref[3 * number : 3 * number + 3]
-        target[1 : EXT_X - 1, CY : CY + width, :] = yhigh_ref[:, start : start + width, :]
-        target[1 : EXT_X - 1, EXT_Y - width :, :] = ylow_ref[:, start : start + width, :]
+            target[3 + CX :, :CY, :] = high
+        here = slice(start, start + width)
+        low, high = by_parity((gy_ref[0], n_gy), yeven_ref[:, here, :], yodd_ref[:, here, :])
+        target[1 : EXT_X - 1, CY : CY + width, :] = high
+        target[1 : EXT_X - 1, EXT_Y - width :, :] = low
         shift = jnp.where(side == 0, (3 * number + 3) % LANES, 3 * number)
         turned = pltpu.roll(target[1 : EXT_X - 1].reshape((EXT_X - 2) * EXT_Y, LANES), shift, 1)
         turned = turned.reshape(EXT_X - 2, EXT_Y, LANES)
@@ -273,13 +312,35 @@
 
     sweep(first_s, second_s, 1, EXT_X - 1)
     sweep(second_s, first_s, 2, EXT_X - 2)
-    sweep(first_s, second_s, 3, EXT_X - 3)
+
+    def finish(x, carry):
+        i = x - 1
+        middles = [first_s[c, x, :CY, :LANES] for c in range(3)]
+        shared = couple_s[i, :CY, :LANES] * (middles[0] + middles[1] + middles[2])
+        for c in range(3):
+            columns = first_s[c, x, :, :LANES]
+            halo = first_s[c, x, :CY, LANES:]
+            others = (
+                first_s[c, x + 1, :CY, :LANES],
+                first_s[c, x - 1, :CY, :LANES],
+                pltpu.roll(columns, EXT_Y - 1, 0)[:CY],
+                pltpu.roll(columns, 1, 0)[:CY],
+                pltpu.roll(jnp.where(last_lane == 0, halo, middles[c]), LANES - 1, 1),
+                pltpu.roll(jnp.where(last_lane == LANES - 1, halo, middles[c]), 1, 1),
+            )
+            value = keep_s[i, :CY, :LANES] * middles[c] + (push_s[c, i, :CY, :LANES] - shared)
+            for n in range(6):
+                value = value + weight_s[n, i, :CY, :LANES] * others[n]
+            out_ref[c, x - 3] = value
+        return carry
+
+    last_lane = iota((CY, LANES), 1)
+    lax.fori_loop(3, 3 + CX, finish, 0)
 
     own_rows = CX * CY
     blank = jnp.zeros((2 * LANES - own_rows, LANES), f32)
     for c in range(3):
-        result = second_s[c, 3 : 3 + CX, :CY, :LANES]
-        out_ref[c] = result
+        result = out_ref[c]
         scaled = (result * stiff_s[3 : 3 + CX, :CY, :LANES]).reshape(own_rows, LANES)
         high, low = halves(scaled)
         cut = slice(c * LANES, (c + 1) * LANES)
@@ -288,33 +349,38 @@
     count = HULL_DESTS * HULL_ROWS
     row_number = iota((2 * LANES, LANES), 0)
     lane_number = iota((LANES, LANES), 0)
-    for d in range(HULL_DESTS):
+    group = 2 * HULL_ROWS
+    for g in range(count // group):
         chosen = []
-        for i in range(HULL_ROWS):
-            r = d * HULL_ROWS + i
+        for i in range(group):
+            r = g * group + i
             chosen.append(jnp.where(row_number == where_ref[r : r + 1, :], 1.0, 0.0).astype(bf16))
         chosen = jnp.concatenate(chosen, axis=1)
         found = jnp.dot(turned_s[...], jnp.concatenate([chosen, chosen], axis=0), preferred_element_type=f32)
-        for i in range(HULL_ROWS):
-            r = d * HULL_ROWS + i
+        for i in range(group):
+            r = g * group + i
             here = lane_number == where_ref[count + r : count + r + 1, :]
+            base = r // HULL_ROWS * 4 * HULL_ROWS + r % HULL_ROWS
             for c in range(3):
                 part = found[c * LANES : (c + 1) * LANES, i * LANES : (i + 1) * LANES]
-                value = jnp.sum(jnp.where(here, part, 0.0), axis=0, keepdims=True)
-                spot = d * 4 * HULL_ROWS + c * HULL_ROWS + i
-                message_ref[spot : spot + 1, :] = value
-            spot = d * 4 * HULL_ROWS + 3 * HULL_ROWS + i
+                spot = base + c * HULL_ROWS
+                message_ref[spot : spot + 1, :] = jnp.sum(jnp.where(here, part, 0.0), axis=0, keepdims=True)
+            spot = base + 3 * HULL_ROWS
             message_ref[spot : spot + 1, :] = ids_ref[r : r + 1, :]
 
 
-def scatter_hull(nodes_ref, out_ref):
+def scatter_hull(nodes_ref, out_hbm, overflow_ref, out_ref, sem):
+    flags = nodes_ref[pl.ds(4 * HULL_ROWS - 1, HULL_DESTS, stride=4 * HULL_ROWS), :]
+    last = iota((HULL_DESTS, LANES), 1) == LANES - 1
+    overflow_ref[0] = jnp.max(jnp.where(last, flags, 0.0)).astype(i32)
     row_number = iota((64, LANES), 0)
     column_number = iota((256, LANES), 0)
     sums = jnp.zeros((6 * 64, 256), f32)
-    for s in range(HULL_DESTS):
+    batch = 4
+    for first in range(0, HULL_DESTS, batch):
         lefts, rights = [], []
-        for i in range(HULL_ROWS):
-            base = s * 4 * HULL_ROWS + i
+        for n in range(batch * HULL_ROWS):
+            base = (first + n // HULL_ROWS) * 4 * HULL_ROWS + n % HULL_ROWS
             ids = nodes_ref[base + 3 * HULL_ROWS : base + 3 * HULL_ROWS + 1, :].astype(i32) - 1
             here = row_number == (ids >> 8)
             pieces = []
@@ -326,89 +392,124 @@
         sums = sums + dot_last(jnp.concatenate(lefts, axis=1), jnp.concatenate(rights, axis=1))
     for c in range(3):
         out_ref[c] = sums[2 * c * 64 : (2 * c + 1) * 64] + sums[(2 * c + 1) * 64 : (2 * c + 2) * 64]
+    copy = pltpu.make_async_copy(out_ref, out_hbm, sem)
+    copy.start()
+    copy.wait()
 
 
 def shaped(*shape, dtype=f32):
     return jax.ShapeDtypeStruct(shape, dtype)
 
 
-def call(kernel, outs, scratch, cost, *args, scalars=0):
-    specs = [pl.BlockSpec(memory_space=pltpu.SMEM)] * scalars + [pl.BlockSpec(memory_space=pltpu.VMEM)] * (len(args) - scalars)
-    many = isinstance(outs, tuple)
-    vmem = pl.BlockSpec(memory_space=pltpu.VMEM)
+def call(kernel, outs, scratch, cost, *args, places="", out_places=""):
+    spaces = {"V": pltpu.VMEM, "S": pltpu.SMEM, "H": pltpu.HBM}
+
+    def specs(count, names):
+        names = names + "V" * (count - len(names))
+        return [pl.BlockSpec(memory_space=spaces[name]) for name in names]
+
+    args = [pltpu.with_memory_space_constraint(arg, pltpu.HBM) if place == "H" else arg for arg, place in zip(args, places + "V" * len(args))]
+    if isinstance(outs, tuple):
+        outs = tuple(pltpu.HBM(out.shape, out.dtype) if place == "H" else out for out, place in zip(outs, out_places + "V" * len(outs)))
     return pl.pallas_call(
         kernel,
         out_shape=outs,
-        in_specs=specs,
-        out_specs=tuple(vmem for _ in outs) if many else vmem,
-        scratch_shapes=[pltpu.VMEM(shape, dtype) for shape, dtype in scratch],
+        in_specs=specs(len(args), places),
+        out_specs=tuple(specs(len(outs), out_places)) if isinstance(outs, tuple) else specs(1, out_places)[0],
+        scratch_shapes=scratch,
         compiler_params=PARAMS,
         cost_estimate=pl.CostEstimate(flops=cost, bytes_accessed=1 << 20, transcendentals=0),
-        name=kernel.__name__,
+        name=getattr(kernel, "func", kernel).__name__,
     )(*args)
 
 
-def step(axis, values, up):
+def pair_exchange(axis, even, odd):
     count = lax.axis_size(axis)
-    pairs = [(i, i + 1) if up else (i + 1, i) for i in range(count - 1)]
-    return lax.ppermute(values, axis, pairs)
+    results = []
+    for first, values in ((0, even), (1, odd)):
+        pairs = [(i, (i + 1) % count) for i in range(first, count, 2)]
+        results.append(lax.ppermute(values, axis, pairs + [(b, a) for a, b in pairs]))
+    return results
 
 
 def per_device(start_field, stiffness, mass, sens_values, sens_cells, sens_counts, hull_cells, hull_patches):
-    last = jnp.concatenate([start_field[:, CX - 3 :].reshape(9, CY, CZ), stiffness[CX - 3 :], mass[CX - 2 :]], axis=0)
-    first = jnp.concatenate([start_field[:, :3].reshape(9, CY, CZ), stiffness[:3], mass[:2]], axis=0)
-    xlow = step("gx", last, True)
-    xhigh = step("gx", first, False)
-    packed = call(
+    slabs = shaped(14, CY, CZ)
+    gx, gy, side = (lax.axis_index(axis).astype(i32).reshape(1) for axis in ("gx", "gy", "gz"))
+    packed, even, odd = call(
         pack_slots,
-        shaped(3 * BLOCKS, LANES),
-        [],
+        (shaped(3 * BLOCKS, LANES), slabs, slabs),
+        [
+            pltpu.VMEM((3, SLOT_ROWS, LANES), f32),
+            pltpu.VMEM((SLOT_ROWS, LANES), i32),
+            pltpu.VMEM((1, BLOCKS), i32),
+            pltpu.SemaphoreType.DMA((13,)),
+        ],
         1 << 20,
+        gx,
         sens_values.reshape(3, SLOT_ROWS, LANES),
         sens_cells.reshape(SLOT_ROWS, LANES),
         sens_counts.reshape(1, BLOCKS),
-    )
-    arrived = lax.all_to_all(packed, ("gx", "gy"), split_axis=0, concat_axis=0, tiled=True)
-    source, first_rows, last_rows = call(
-        scatter_slots,
-        (shaped(3, CX + 4, CY, CZ), shaped(CX + 4, Y_ROWS, CZ), shaped(CX + 4, Y_ROWS, CZ)),
-        [((CX * CY, SLOTS), bf16), ((6 * LANES, SLOTS), bf16), ((12 * CY, SLOTS), bf16), ((LANES, SLOTS), bf16)],
-        1 << 32,
-        arrived,
         start_field,
         stiffness,
         mass,
-        xlow,
-        xhigh,
-    )
-    ylow = step("gy", last_rows, True)
-    yhigh = step("gy", first_rows, False)
+        places="SHHHHHH",
+    )
+    packed = packed.reshape(BLOCKS, 1, 3 * LANES)
+    arrived = lax.all_to_all(packed, ("gx", "gy"), split_axis=0, concat_axis=0, tiled=True)
+    xeven, xodd = pair_exchange("gx", even, odd)
     count = HULL_DESTS * HULL_ROWS
     where, ids = call(
         route_hull,
         (shaped(2 * count, LANES, dtype=i32), shaped(count, LANES)),
-        [((4 * count, SLOTS), bf16), ((LANES, SLOTS), bf16)],
+        [pltpu.VMEM((4 * count, SLOTS), bf16), pltpu.VMEM((LANES, SLOTS), bf16)],
         1 << 31,
         hull_cells.reshape(SLOT_ROWS, LANES),
         hull_patches.reshape(SLOT_ROWS, LANES),
     )
-    side = lax.axis_index("gz").astype(i32).reshape(1)
+    arrived = arrived.reshape(3 * BLOCKS, LANES)
+    source = call(
+        scatter_slots,
+        shaped(3, CX + 4, CY, CZ),
+        [pltpu.VMEM((rows, SLOTS), bf16) for rows in (2 * LANES, 6 * LANES, 12 * CY, LANES)],
+        1 << 32,
+        arrived,
+    )
+    y_message = shaped(CX + 4, Y_ROWS, CZ)
+    n_gx, n_gy = lax.axis_size("gx"), lax.axis_size("gy")
+    even, odd = call(
+        functools.partial(pack_y, n_gx),
+        (y_message, y_message),
+        [],
+        1 << 20,
+        gx,
+        gy,
+        source,
+        start_field,
+        stiffness,
+        mass,
+        xeven,
+        xodd,
+        places="SS",
+    )
+    yeven, yodd = pair_exchange("gy", even, odd)
     rows = (EXT_X - 2) * EXT_Y
     ext, faces = call(
-        widen,
+        functools.partial(widen, n_gx, n_gy),
         (shaped(8, EXT_X, EXT_Y, CZ), shaped(Z_ROWS, rows)),
         [],
         1 << 20,
+        gx,
+        gy,
         side,
         start_field,
         stiffness,
         mass,
         source,
-        xlow,
-        xhigh,
-        ylow,
-        yhigh,
-        scalars=1,
+        xeven,
+        xodd,
+        yeven,
+        yodd,
+        places="SSS",
     )
     faces = lax.ppermute(faces, "gz", [(0, 1), (1, 0)])
     wide = (EXT_X - 2, EXT_Y, 2 * CZ)
@@ -417,14 +518,14 @@
         relax_and_gather,
         (shaped(3, CX, CY, CZ), shaped(4 * count, LANES)),
         [
-            ((3,) + full, f32),
-            ((3,) + full, f32),
-            (full, f32),
-            ((6,) + wide, f32),
-            (wide, f32),
-            (wide, f32),
-            ((3,) + wide, f32),
-            ((3 * LANES, 4 * LANES), bf16),
+            pltpu.VMEM((3,) + full, f32),
+            pltpu.VMEM((3,) + full, f32),
+            pltpu.VMEM(full, f32),
+            pltpu.VMEM((6,) + wide, f32),
+            pltpu.VMEM(wide, f32),
+            pltpu.VMEM(wide, f32),
+            pltpu.VMEM((3,) + wide, f32),
+            pltpu.VMEM((3 * LANES, 4 * LANES), bf16),
         ],
         1 << 32,
         side,
@@ -432,13 +533,22 @@
         faces,
         where,
         ids,
-        scalars=1,
-    )
+        places="S",
+    )
+    outgoing = outgoing.reshape(HULL_DESTS, 1, 4 * HULL_ROWS * LANES)
     nodes = lax.all_to_all(outgoing, ("gy", "gz"), split_axis=0, concat_axis=0, tiled=True)
-    overflow = jnp.max(nodes.reshape(HULL_DESTS, 4 * HULL_ROWS, LANES)[:, -1, -1])
+    nodes = nodes.reshape(4 * count, LANES)
+    patch, overflow = call(
+        scatter_hull,
+        (shaped(3, 64, 256), shaped(1, dtype=i32)),
+        [pltpu.VMEM((3, 64, 256), f32), pltpu.SemaphoreType.DMA],
+        1 << 32,
+        nodes,
+        out_places="HS",
+    )
 
     def in_messages():
-        return call(scatter_hull, shaped(3, 64, 256), [], 1 << 32, nodes)
+        return patch
 
     def every_node():
         cells = hull_cells[0, 0]
@@ -453,7 +563,7 @@
         patch = jnp.zeros((3, PATCH_BLOCK), f32).at[:, jnp.where(mine, spots, 0)].add(added)
         return patch.reshape(3, 64, 256)
 
-    patch = lax.cond(overflow > 0.0, every_node, in_messages)
+    patch = lax.cond(overflow[0] > 0, every_node, in_messages)
     return field, patch
 
 

time: 92.4 us -> 74.2 us (0.80)
  local copies, waits for them, and re-layouts: 10.5 us -> 0.02 us
  Pallas kernels: 29.1 us -> 22 us
    pallas_call x6 -> x7, Pallas kernels: 29.1 us -> 22 us  [call(): pl.pallas_call(kernel, out_shape=outs, in_specs=specs(len(args), places),...]
    all_to_all x4 -> x0, local copies, waits for them, and re-layouts: 4.68 us -> none  [the longest x2 2.48 us: per_device(): lax.all_to_all(packed, ('gx', 'gy'), split_axis=0, concat_axis=0, tiled=T...]
    unnamed x18 -> x10, local copies, waits for them, and re-layouts: 3.26 us -> 0.02 us
    slice x3 -> x0, local copies, waits for them, and re-layouts: 2.52 us -> none  [the longest x1 0.97 us: per_device(): start_field[:, :3].reshape(9, CY, CZ)]
    all_to_all x1, starting transfers between devices: 3.41 us -> 5.48 us  [per_device(): lax.all_to_all(outgoing, ('gy', 'gz'), split_axis=0, concat_axis=0, tiled...]
    ppermute x4, starting transfers between devices: 9.04 us -> 7.61 us  [pair_exchange(): lax.ppermute(values, axis, pairs + [(b, a) for a, b in pairs])]
  transfers between devices with their start and end apart: 7 -> 7, of which waited for: 5 -> 5; matrix products, arithmetic and copies ran while one was open for 3% -> 0% of each run, Pallas kernels for 3% -> 9%
where the time goes in v2:
time: 74.2 us; the launch traced here: 73.9 us
  starting transfers between devices  30.1 us (41%)
  Pallas kernels  22 us (30%)
  waiting for transfers between devices  20.2 us (27%)
  between operations  1.6 us (2%)
    pallas_call x7, Pallas kernels, call(): pl.pallas_call(kernel, out_shape=outs, in_specs=specs(len(args), places),...  22 us
    all_to_all x1, starting transfers between devices, per_device(): lax.all_to_all(packed, ('gx', 'gy'), split_axis=0, concat_axis=0, tiled=T...  16.4 us
    all_to_all x1, waiting for transfers between devices, per_device(): lax.all_to_all(packed, ('gx', 'gy'), split_axis=0, concat_axis=0, tiled=T...  8.6 us
    ppermute x4, starting transfers between devices, pair_exchange(): lax.ppermute(values, axis, pairs + [(b, a) for a, b in pairs])  7.61 us
    all_to_all x1, waiting for transfers between devices, per_device(): lax.all_to_all(outgoing, ('gy', 'gz'), split_axis=0, concat_axis=0, tiled...  6.28 us
    all_to_all x1, starting transfers between devices, per_device(): lax.all_to_all(outgoing, ('gy', 'gz'), split_axis=0, concat_axis=0, tiled...  5.48 us
    ppermute x4, waiting for transfers between devices, pair_exchange(): lax.ppermute(values, axis, pairs + [(b, a) for a, b in pairs])  4.67 us
  transfers between devices with their start and end apart: 7, of which 5 were waited for; matrix products, arithmetic and copies ran while one was open for 0% of the time, Pallas kernels for 9%

profile of v2, /device:TPU:1, one launch (start us, length us, event | category | flops | bytes accessed | tf_op | source)
XLA Modules:
  0.0 73.9 jit_solution(3046257121160431325)
XLA Ops:
  0.6 0.0 copy-start
  0.6 0.0 copy-start.1
  0.7 0.0 copy-start.2
  0.7 1.9 %pack_slots.1 = (f32[384,128]{1,0:T(8,128)}, f32[14,24,128]{2,1,0:T(8,128)S(1)}, f32[14,24,128]{2,1,0:T(8,128)S(1)}) custom-call(s32[1]{0:T(128)} %bitcast.13.gx_ref, f32[3,32,128]{2,1,0:T(8,128)} %bitcast.44, s32[32,128]{1,0:T(8,128)} %bitcast.45, s32[1,128]{1,0:T(1,128)} %bitcast.48, f32[3,8,24,128]{3,2,1,0:T(8,128)} %field_ref.3, ...), custom_call_target="tpu_custom_call" | custom-call | flops 1048576 | bytes 1048576 | tf_op jit(solution)/shard_map/pack_slots/pallas_call | solution.py:414
  2.6 16.4 %all-to-all-start.1 = ((f32[128,1,384]{2,1,0:T(1,128)}), f32[128,1,384]{2,1,0:T(1,128)S(1)}, u32[]{:S(2)}, u32[]{:S(2)}) async-start(f32[128,1,384]{2,1,0:T(1,128)} %bitcast.18), calls=%async_computation.1 | async-start | bytes 393216 | tf_op jit(solution)/shard_map/all_to_all | solution.py:458
  19.0 1.5 %collective-permute-start = (f32[14,24,128]{2,1,0:T(8,128)S(1)}, f32[14,24,128]{2,1,0:T(8,128)S(1)}, u32[]{:S(2)}, u32[]{:S(2)}) collective-permute-start(f32[14,24,128]{2,1,0:T(8,128)S(1)} %get-tuple-element.32), channel_id=1, source_target_pairs={{0,16},{32,48},{64,80},{96,112},{128,144},{160,176},{192,208},{224... | collective-permute-start | bytes 516104 | tf_op jit(solution)/shard_map/ppermute | solution.py:431
  20.5 5.4 %collective-permute-start.1 = (f32[14,24,128]{2,1,0:T(8,128)S(1)}, f32[14,24,128]{2,1,0:T(8,128)S(1)}, u32[]{:S(2)}, u32[]{:S(2)}) collective-permute-start(f32[14,24,128]{2,1,0:T(8,128)S(1)} %get-tuple-element.33), channel_id=1, source_target_pairs={{16,32},{48,64},{80,96},{112,128},{144,160},{176,192},{208,224},{2... | collective-permute-start | bytes 516104 | tf_op jit(solution)/shard_map/ppermute | solution.py:431
  25.9 8.6 %all-to-all-done.1 = f32[128,1,384]{2,1,0:T(1,128)S(1)} async-done(((f32[128,1,384]{2,1,0:T(1,128)}), f32[128,1,384]{2,1,0:T(1,128)S(1)}, u32[]{:S(2)}, u32[]{:S(2)}) %all-to-all-start.1) | async-done | bytes 196640 | tf_op jit(solution)/shard_map/all_to_all | solution.py:458
  34.5 0.0 copy-start.3
  34.5 0.0 copy-start.4
  34.5 5.2 %scatter_slots.1.source_ref = f32[3,12,24,128]{3,2,1,0:T(8,128)S(1)} custom-call(f32[384,128]{1,0:T(8,128)S(1)} %bitcast.32), custom_call_target="tpu_custom_call" | custom-call | flops 4294967296 | bytes 1048576 | tf_op jit(solution)/shard_map/scatter_slots/pallas_call | solution.py:414
  39.7 0.0 collective-permute-done.xeven_ref
  39.7 0.0 collective-permute-done.1.xodd_ref
  39.8 0.0 copy-done
  39.8 0.0 copy-done.1
  39.8 0.0 copy-done.2
  39.8 0.1 pack_y.1
  39.9 0.5 collective-permute-start.2
  40.4 0.2 collective-permute-start.3
  40.6 0.8 %collective-permute-done.2.yeven_ref = f32[12,20,128]{2,1,0:T(8,128)S(1)} collective-permute-done((f32[12,20,128]{2,1,0:T(8,128)S(1)}, f32[12,20,128]{2,1,0:T(8,128)S(1)}, u32[]{:S(2)}, u32[]{:S(2)}) %collective-permute-start.2) | collective-permute-done | bytes 122912 | tf_op jit(solution)/shard_map/ppermute | solution.py:431
  41.4 3.9 %collective-permute-done.3.yodd_ref = f32[12,20,128]{2,1,0:T(8,128)S(1)} collective-permute-done((f32[12,20,128]{2,1,0:T(8,128)S(1)}, f32[12,20,128]{2,1,0:T(8,128)S(1)}, u32[]{:S(2)}, u32[]{:S(2)}) %collective-permute-start.3) | collective-permute-done | bytes 122912 | tf_op jit(solution)/shard_map/ppermute | solution.py:431
  45.2 0.6 widen.1
  45.8 0.6 collective-permute-start.4
  46.5 0.0 copy-done.3
  46.5 0.0 copy-done.4
  46.5 1.7 %route_hull.1 = (s32[96,128]{1,0:T(8,128)S(1)}, f32[48,128]{1,0:T(8,128)S(1)}) custom-call(s32[32,128]{1,0:T(8,128)S(1)} %bitcast.46, s32[32,128]{1,0:T(8,128)S(1)} %bitcast.47), custom_call_target="tpu_custom_call" | custom-call | flops 2147483648 | bytes 1048576 | tf_op jit(solution)/shard_map/route_hull/pallas_call | solution.py:414
  48.2 0.7 collective-permute-done.4.z_ref
  48.9 9.8 %relax_and_gather.1 = (f32[3,8,24,128]{3,2,1,0:T(8,128)}, f32[192,128]{1,0:T(8,128)}) custom-call(s32[1]{0:T(128)} %bitcast.12.side_ref, f32[8,14,32,128]{3,2,1,0:T(8,128)S(1)} %get-tuple-element.36.ext_ref, f32[24,384]{1,0:T(8,128)S(1)} %collective-permute-done.4.z_ref, s32[96,128]{1,0:T(8,128)S(1)} %get-tuple-element.38.where_ref, ...), custom_call_target="tpu_custom_call" | custom-call | flops 4294967296 | bytes 1048576 | tf_op jit(solution)/shard_map/relax_and_gather/pallas_call | solution.py:414
  58.7 5.5 %all-to-all-start.2 = ((f32[16,1,1536]{2,1,0:T(1,128)}), f32[16,1,1536]{2,1,0:T(1,128)S(1)}, u32[]{:S(2)}, u32[]{:S(2)}) async-start(f32[16,1,1536]{2,1,0:T(1,128)} %bitcast.22), calls=%async_computation.2 | async-start | bytes 196608 | tf_op jit(solution)/shard_map/all_to_all | solution.py:539
  64.2 6.3 %all-to-all-done.2 = f32[16,1,1536]{2,1,0:T(1,128)S(1)} async-done(((f32[16,1,1536]{2,1,0:T(1,128)}), f32[16,1,1536]{2,1,0:T(1,128)S(1)}, u32[]{:S(2)}, u32[]{:S(2)}) %all-to-all-start.2) | async-done | bytes 98336 | tf_op jit(solution)/shard_map/all_to_all | solution.py:539
  70.4 2.6 %scatter_hull.1 = (f32[3,64,256]{2,1,0:T(8,128)}, s32[1]{0:T(128)}) custom-call(f32[192,128]{1,0:T(8,128)S(1)} %bitcast.33), custom_call_target="tpu_custom_call" | custom-call | flops 4294967296 | bytes 1048576 | tf_op jit(solution)/shard_map/scatter_hull/pallas_call | solution.py:414
  (1 shorter events, 0.0 us)
Async XLA Ops:
  0.6 39.1 %copy-start = (f32[3,8,24,128]{3,2,1,0:T(8,128)S(1)}, f32[3,8,24,128]{3,2,1,0:T(8,128)}, u32[]{:S(2)}) copy-start(f32[3,8,24,128]{3,2,1,0:T(8,128)} %field_ref.3) | copy-start | bytes 884740
  0.6 39.1 %copy-start.1 = (f32[8,24,128]{2,1,0:T(8,128)S(1)}, f32[8,24,128]{2,1,0:T(8,128)}, u32[]{:S(2)}) copy-start(f32[8,24,128]{2,1,0:T(8,128)} %mass_ref.3) | copy-start | bytes 294916
  0.7 39.1 %copy-start.2 = (f32[8,24,128]{2,1,0:T(8,128)S(1)}, f32[8,24,128]{2,1,0:T(8,128)}, u32[]{:S(2)}) copy-start(f32[8,24,128]{2,1,0:T(8,128)} %stiff_ref.3) | copy-start | bytes 294916
  2.6 31.9 %all-to-all-start.1 = ((f32[128,1,384]{2,1,0:T(1,128)}), f32[128,1,384]{2,1,0:T(1,128)S(1)}, u32[]{:S(2)}, u32[]{:S(2)}) async-start(f32[128,1,384]{2,1,0:T(1,128)} %bitcast.18), calls=%async_computation.1 | async-start | bytes 393216 | tf_op jit(solution)/shard_map/all_to_all | solution.py:458
  19.0 20.7 %collective-permute-start = (f32[14,24,128]{2,1,0:T(8,128)S(1)}, f32[14,24,128]{2,1,0:T(8,128)S(1)}, u32[]{:S(2)}, u32[]{:S(2)}) collective-permute-start(f32[14,24,128]{2,1,0:T(8,128)S(1)} %get-tuple-element.32), channel_id=1, source_target_pairs={{0,16},{32,48},{64,80},{96,112},{128,144},{160,176},{192,208},{224... | collective-permute-start | bytes 516104 | tf_op jit(solution)/shard_map/ppermute | solution.py:431
  20.5 19.3 %collective-permute-start.1 = (f32[14,24,128]{2,1,0:T(8,128)S(1)}, f32[14,24,128]{2,1,0:T(8,128)S(1)}, u32[]{:S(2)}, u32[]{:S(2)}) collective-permute-start(f32[14,24,128]{2,1,0:T(8,128)S(1)} %get-tuple-element.33), channel_id=1, source_target_pairs={{16,32},{48,64},{80,96},{112,128},{144,160},{176,192},{208,224},{2... | collective-permute-start | bytes 516104 | tf_op jit(solution)/shard_map/ppermute | solution.py:431
  34.5 12.0 %copy-start.3 = (s32[1,1,4096]{2,1,0:T(1,128)S(1)}, s32[1,1,4096]{2,1,0:T(1,128)}, u32[]{:S(2)}) copy-start(s32[1,1,4096]{2,1,0:T(1,128)} %param.16) | copy-start | bytes 49156
  34.5 12.0 %copy-start.4 = (s32[1,1,4096]{2,1,0:T(1,128)S(1)}, s32[1,1,4096]{2,1,0:T(1,128)}, u32[]{:S(2)}) copy-start(s32[1,1,4096]{2,1,0:T(1,128)} %param.17) | copy-start | bytes 49156
  39.9 1.5 %collective-permute-start.2 = (f32[12,20,128]{2,1,0:T(8,128)S(1)}, f32[12,20,128]{2,1,0:T(8,128)S(1)}, u32[]{:S(2)}, u32[]{:S(2)}) collective-permute-start(f32[12,20,128]{2,1,0:T(8,128)S(1)} %get-tuple-element.34), channel_id=1, source_target_pairs={{0,2},{4,6},{8,10},{12,14},{2,0},{6,4},{10,8},{14,12},{1,3},{5,7},... | collective-permute-start | bytes 368648 | tf_op jit(solution)/shard_map/ppermute | solution.py:431
  40.4 4.9 %collective-permute-start.3 = (f32[12,20,128]{2,1,0:T(8,128)S(1)}, f32[12,20,128]{2,1,0:T(8,128)S(1)}, u32[]{:S(2)}, u32[]{:S(2)}) collective-permute-start(f32[12,20,128]{2,1,0:T(8,128)S(1)} %get-tuple-element.35), channel_id=1, source_target_pairs={{2,4},{6,8},{10,12},{14,0},{4,2},{8,6},{12,10},{0,14},{3,5},{7,9},... | collective-permute-start | bytes 368648 | tf_op jit(solution)/shard_map/ppermute | solution.py:431
  45.8 3.1 %collective-permute-start.4 = (f32[24,384]{1,0:T(8,128)S(1)}, f32[24,384]{1,0:T(8,128)S(1)}, u32[]{:S(2)}, u32[]{:S(2)}) collective-permute-start(f32[24,384]{1,0:T(8,128)S(1)} %get-tuple-element.37), channel_id=1, source_target_pairs={{0,1},{1,0},{2,3},{3,2},{4,5},{5,4},{6,7},{7,6},{8,9},{9,8},{10,11... | collective-permute-start | bytes 110600 | tf_op jit(solution)/shard_map/ppermute | solution.py:514
  58.7 11.8 %all-to-all-start.2 = ((f32[16,1,1536]{2,1,0:T(1,128)}), f32[16,1,1536]{2,1,0:T(1,128)S(1)}, u32[]{:S(2)}, u32[]{:S(2)}) async-start(f32[16,1,1536]{2,1,0:T(1,128)} %bitcast.22), calls=%async_computation.2 | async-start | bytes 196608 | tf_op jit(solution)/shard_map/all_to_all | solution.py:539

commit v3 on v2

--- a/solution.py
+++ b/solution.py
@@ -17,9 +17,9 @@
 PATCH_BLOCK = 64 * 256
 HULL_ROWS = 3
 HULL_CAP = HULL_ROWS * LANES - 1
-Y_ROWS = 20
-Y_FIELDS = ((0, 3), (3, 3), (6, 3), (9, 3), (12, 2), (14, 2), (16, 2), (18, 2))
-Z_ROWS = 24
+Y_ROWS = 14
+Y_FIELDS = ((0, 3), (3, 3), (6, 3), (9, 3), (12, 2))
+Z_ROWS = 16
 EXT_X = CX + 6
 EXT_Y = 32
 RELAX = 0.8
@@ -39,6 +39,14 @@
 
 def dot_last(a, b):
     return lax.dot_general(a, b, (((1,), (1,)), ((), ())), preferred_element_type=f32)
+
+
+def by_parity(place, even, odd):
+    index, count = place
+    is_odd = lax.rem(index, 2) == 1
+    low = jnp.where(is_odd, even, odd) * jnp.where(index > 0, 1.0, 0.0)
+    high = jnp.where(is_odd, odd, even) * jnp.where(index < count - 1, 1.0, 0.0)
+    return low, high
 
 
 def pack_slots(
@@ -83,7 +91,7 @@
         copy.wait()
 
 
-def scatter_slots(slots_ref, source_ref, rows_s, lanes_s, left_s, right_s):
+def scatter_slots(gy_ref, slots_ref, source_ref, even_ref, odd_ref, rows_s, lanes_s, left_s, right_s):
     lane = iota((SLOT_ROWS, LANES), 1)
     quarter = lane // CAP
     own_rows = CY * CX
@@ -128,29 +136,32 @@
         for c in range(3):
             one = sums[2 * c * side_rows : (2 * c + 1) * side_rows] + sums[(2 * c + 1) * side_rows : (2 * c + 2) * side_rows]
             source_ref[c, target : target + 2] = one.reshape(2, CY, LANES)
-
-
-def by_parity(place, even, odd):
-    index, count = place
-    is_odd = lax.rem(index, 2) == 1
-    low = jnp.where(is_odd, even, odd) * jnp.where(index > 0, 1.0, 0.0)
-    high = jnp.where(is_odd, odd, even) * jnp.where(index < count - 1, 1.0, 0.0)
-    return low, high
-
-
-def pack_y(n_gx, gx_ref, gy_ref, source_ref, field_ref, stiff_ref, mass_ref, xeven_ref, xodd_ref, even_ref, odd_ref):
+    is_odd = lax.rem(gy_ref[0], 2) == 1
+    for c in range(3):
+        here = slice(2 * c, 2 * c + 2)
+        first, last = source_ref[c, :, 0:2, :], source_ref[c, :, CY - 2 :, :]
+        even_ref[:, here, :] = jnp.where(is_odd, first, last)
+        odd_ref[:, here, :] = jnp.where(is_odd, last, first)
+
+
+def pack_y(n_gx, gx_ref, gy_ref, field_hbm, stiff_hbm, mass_hbm, xeven_ref, xodd_ref, even_ref, odd_ref, ends_ref, sems):
+    copies = []
+    for number in range(5):
+        own = field_hbm.at[number] if number < 3 else (stiff_hbm if number == 3 else mass_hbm)
+        for n, rows in enumerate((pl.ds(0, 8), pl.ds(CY - 8, 8))):
+            copies.append(pltpu.make_async_copy(own.at[:, rows], ends_ref.at[number, n], sems.at[len(copies)]))
+    for copy in copies:
+        copy.start()
+    for copy in copies:
+        copy.wait()
     is_odd = lax.rem(gy_ref[0], 2) == 1
     for number, (start, width) in enumerate(Y_FIELDS):
         here = slice(start, start + width)
-        ends = slice(0, width), slice(CY - width, CY)
+        planes = slice(3 * number, 3 * number + 3) if number < 4 else slice(12, 14)
         pieces = [[], []]
-        for n, rows in enumerate(ends):
-            if number >= 5:
-                pieces[n].append((slice(0, CX + 4), source_ref[number - 5, :, rows, :]))
-                continue
-            planes = slice(3 * number, 3 * number + 3) if number < 4 else slice(12, 14)
+        for n, (rows, own_rows) in enumerate(((slice(0, width), slice(0, width)), (slice(CY - width, CY), slice(8 - width, 8)))):
             low, high = by_parity((gx_ref[0], n_gx), xeven_ref[planes, rows, :], xodd_ref[planes, rows, :])
-            own = field_ref[number, :, rows, :] if number < 3 else (stiff_ref if number == 3 else mass_ref)[:, rows, :]
+            own = ends_ref[number, n, :, own_rows, :]
             pieces[n].extend([(slice(0, 2), low[-2:]), (slice(2, 2 + CX), own), (slice(2 + CX, CX + 4), high[:2])])
         for (where, first), (_, last) in zip(*pieces):
             even_ref[where, here, :] = jnp.where(is_odd, first, last)
@@ -197,103 +208,130 @@
     ids_ref[...] = jnp.where(last, overflow, ids)
 
 
-def widen(n_gx, n_gy, gx_ref, gy_ref, side_ref, field_ref, stiff_ref, mass_ref, source_ref, xeven_ref, xodd_ref, yeven_ref, yodd_ref, ext_ref, z_ref):
-    side = side_ref[0]
+def pack_z(side, arrays, z_ref):
     lane = iota((1, 1, LANES), 2)
+    total = jnp.zeros((EXT_X - 2, EXT_Y, LANES), f32)
+    for number, array in enumerate(arrays):
+        shift = jnp.where(side == 0, (3 * number + 3) % LANES, 3 * number)
+        turned = pltpu.roll(array.reshape((EXT_X - 2) * EXT_Y, LANES), shift, 1).reshape(EXT_X - 2, EXT_Y, LANES)
+        total = jnp.where((lane >= 3 * number) & (lane < 3 * number + 3), turned, total)
+    z_ref[...] = jnp.transpose(total.reshape((EXT_X - 2) * EXT_Y, LANES))[:Z_ROWS]
+
+
+def unpack_z(side, z_ref):
+    rows = (EXT_X - 2) * EXT_Y
+    lane = iota((1, 1, LANES), 2)
+    columns = jnp.transpose(jnp.concatenate([z_ref[...], jnp.zeros((LANES - Z_ROWS, rows), f32)], axis=0))
+    first_lane = jnp.where(side == 0, 0, LANES - 3)
+    near = (lane >= first_lane) & (lane < first_lane + 3)
+
+    def beyond(number):
+        shift = jnp.where(side == 0, (LANES - 3 * number) % LANES, (2 * LANES - 3 - 3 * number) % LANES)
+        return jnp.where(near, pltpu.roll(columns, shift, 1).reshape(EXT_X - 2, EXT_Y, LANES), 0.0)
+
+    return beyond
+
+
+def widen_fixed(n_gx, n_gy, gx_ref, gy_ref, side_ref, field_ref, stiff_ref, mass_ref, xeven_ref, xodd_ref, yeven_ref, yodd_ref, ext_ref, z_ref):
     zeros = jnp.zeros((EXT_X, EXT_Y - CY, LANES), f32)
-    total = jnp.zeros((EXT_X - 2, EXT_Y, LANES), f32)
     for number, (start, width) in enumerate(Y_FIELDS):
         target = ext_ref.at[number]
         target[:, CY:, :] = zeros
-        if number >= 5:
-            target[1 : EXT_X - 1, :CY, :] = source_ref[number - 5]
+        planes = slice(3 * number, 3 * number + 3) if number < 4 else slice(12, 14)
+        low, high = by_parity((gx_ref[0], n_gx), xeven_ref[planes], xodd_ref[planes])
+        own = field_ref.at[number] if number < 3 else (stiff_ref if number == 3 else mass_ref)
+        if width < 3:
             target[0, :CY, :] = jnp.zeros((CY, LANES), f32)
             target[EXT_X - 1, :CY, :] = jnp.zeros((CY, LANES), f32)
-        elif number == 4:
-            target[0, :CY, :] = jnp.zeros((CY, LANES), f32)
-            target[EXT_X - 1, :CY, :] = jnp.zeros((CY, LANES), f32)
-            low, high = by_parity((gx_ref[0], n_gx), xeven_ref[12:14], xodd_ref[12:14])
-            target[1:3, :CY, :] = low
-            target[3 : 3 + CX, :CY, :] = mass_ref[...]
-            target[3 + CX : 5 + CX, :CY, :] = high
-        else:
-            own = field_ref.at[number] if number < 3 else stiff_ref
-            planes = slice(3 * number, 3 * number + 3)
-            low, high = by_parity((gx_ref[0], n_gx), xeven_ref[planes], xodd_ref[planes])
-            target[0:3, :CY, :] = low
-            target[3 : 3 + CX, :CY, :] = own[...]
-            target[3 + CX :, :CY, :] = high
+        target[3 - width : 3, :CY, :] = low
+        target[3 : 3 + CX, :CY, :] = own[...]
+        target[3 + CX : 3 + CX + width, :CY, :] = high
         here = slice(start, start + width)
         low, high = by_parity((gy_ref[0], n_gy), yeven_ref[:, here, :], yodd_ref[:, here, :])
         target[1 : EXT_X - 1, CY : CY + width, :] = high
         target[1 : EXT_X - 1, EXT_Y - width :, :] = low
-        shift = jnp.where(side == 0, (3 * number + 3) % LANES, 3 * number)
-        turned = pltpu.roll(target[1 : EXT_X - 1].reshape((EXT_X - 2) * EXT_Y, LANES), shift, 1)
-        turned = turned.reshape(EXT_X - 2, EXT_Y, LANES)
-        total = jnp.where((lane >= 3 * number) & (lane < 3 * number + 3), turned, total)
-    flipped = jnp.transpose(total.reshape((EXT_X - 2) * EXT_Y, LANES))
-    z_ref[...] = flipped[:Z_ROWS]
-
-
-def relax_and_gather(
-    side_ref, ext_ref, z_ref, where_ref, ids_ref, out_ref, message_ref, first_s, second_s, stiff_s, weight_s, keep_s, couple_s, push_s, turned_s
-):
-    side = side_ref[0]
-    wide = 2 * LANES
-    rows = (EXT_X - 2) * EXT_Y
-    lane = iota((1, 1, LANES), 2)
-    padded = jnp.concatenate([z_ref[...], jnp.zeros((LANES - Z_ROWS, rows), f32)], axis=0)
-    columns = jnp.transpose(padded)
-    first_lane = jnp.where(side == 0, 0, LANES - 3)
-    near = (lane >= first_lane) & (lane < first_lane + 3)
-
-    def beyond(number):
-        shift = jnp.where(side == 0, (LANES - 3 * number) % LANES, (2 * LANES - 3 - 3 * number) % LANES)
-        return jnp.where(near, pltpu.roll(columns, shift, 1).reshape(EXT_X - 2, EXT_Y, LANES), 0.0)
-
+    pack_z(side_ref[0], [ext_ref[number, 1 : EXT_X - 1] for number in range(5)], z_ref)
+
+
+def widen_source(n_gy, gy_ref, side_ref, source_ref, yeven_ref, yodd_ref, ext_ref, z_ref):
+    zeros = jnp.zeros((EXT_X - 2, EXT_Y - CY, LANES), f32)
+    for c in range(3):
+        here = slice(2 * c, 2 * c + 2)
+        low, high = by_parity((gy_ref[0], n_gy), yeven_ref[:, here, :], yodd_ref[:, here, :])
+        ext_ref[c, :, CY:, :] = zeros
+        ext_ref[c, :, :CY, :] = source_ref[c]
+        ext_ref[c, :, CY : CY + 2, :] = high
+        ext_ref[c, :, EXT_Y - 2 :, :] = low
+    pack_z(side_ref[0], [ext_ref[c] for c in range(3)], z_ref)
+
+
+def around(ref_at, x):
+    middle = ref_at(x)
+    return middle, (
+        ref_at(x + 1),
+        ref_at(x - 1),
+        pltpu.roll(middle, EXT_Y - 1, 0),
+        pltpu.roll(middle, 1, 0),
+        pltpu.roll(middle, 2 * LANES - 1, 1),
+        pltpu.roll(middle, 1, 1),
+    )
+
+
+def prepare(side_ref, ext_ref, z_ref, start_ref, weight_ref, keep_ref, couple_ref, rate_ref, stiff_s, mass_s):
+    beyond = unpack_z(side_ref[0], z_ref)
     empty = jnp.zeros((EXT_Y, LANES), f32)
     for c in range(3):
-        first_s[c, :, :, :LANES] = ext_ref[c]
-        first_s[c, 1 : EXT_X - 1, :, LANES:] = beyond(c)
-        first_s[c, 0, :, LANES:] = empty
-        first_s[c, EXT_X - 1, :, LANES:] = empty
+        start_ref[c, :, :, :LANES] = ext_ref[c]
+        start_ref[c, 1 : EXT_X - 1, :, LANES:] = beyond(c)
+        start_ref[c, 0, :, LANES:] = empty
+        start_ref[c, EXT_X - 1, :, LANES:] = empty
     stiff_s[:, :, :LANES] = ext_ref[3]
     stiff_s[1 : EXT_X - 1, :, LANES:] = beyond(3)
     stiff_s[0, :, LANES:] = empty
     stiff_s[EXT_X - 1, :, LANES:] = empty
-    keep_s[:, :, :LANES] = ext_ref[4, 1 : EXT_X - 1]
-    keep_s[:, :, LANES:] = beyond(4)
-    for c in range(3):
-        push_s[c, :, :, :LANES] = ext_ref[5 + c, 1 : EXT_X - 1]
-        push_s[c, :, :, LANES:] = beyond(5 + c)
-
-    def around(ref_at, x):
-        middle = ref_at(x)
-        return middle, (
-            ref_at(x + 1),
-            ref_at(x - 1),
-            pltpu.roll(middle, EXT_Y - 1, 0),
-            pltpu.roll(middle, 1, 0),
-            pltpu.roll(middle, wide - 1, 1),
-            pltpu.roll(middle, 1, 1),
-        )
-
-    def prepare(i, carry):
+    mass_s[:, :, :LANES] = ext_ref[4, 1 : EXT_X - 1]
+    mass_s[:, :, LANES:] = beyond(4)
+
+    def one(i, carry):
         middle, others = around(lambda x: stiff_s[x], i + 1)
         weights = [0.5 * (middle + other) for other in others]
         weight_sum = weights[0] + weights[1] + weights[2] + weights[3] + weights[4] + weights[5]
-        mass = keep_s[i]
+        mass = mass_s[i]
         inside = middle > 0.0
         rate = jnp.where(inside, RELAX / jnp.where(inside, weight_sum + 1.25 * mass, 1.0), 0.0)
         for n in range(6):
-            weight_s[n, i] = rate * weights[n]
-        keep_s[i] = jnp.where(inside, 1.0 - rate * (weight_sum + mass), 0.0)
-        couple_s[i] = 0.25 * rate * mass
-        for c in range(3):
-            push_s[c, i] = rate * push_s[c, i]
+            weight_ref[n, i] = rate * weights[n]
+        keep_ref[i] = jnp.where(inside, 1.0 - rate * (weight_sum + mass), 0.0)
+        couple_ref[i] = 0.25 * rate * mass
+        rate_ref[i] = rate
         return carry
 
-    lax.fori_loop(0, EXT_X - 2, prepare, 0)
+    lax.fori_loop(0, EXT_X - 2, one, 0)
+
+
+def relax_and_gather(
+    side_ref,
+    start_ref,
+    weight_s,
+    keep_s,
+    couple_s,
+    rate_ref,
+    ext_ref,
+    z_ref,
+    stiff_ref,
+    where_ref,
+    ids_ref,
+    out_ref,
+    message_ref,
+    first_s,
+    second_s,
+    push_s,
+    turned_s,
+):
+    beyond = unpack_z(side_ref[0], z_ref)
+    for c in range(3):
+        push_s[c, :, :, :LANES] = rate_ref[:, :, :LANES] * ext_ref[c]
+        push_s[c, :, :, LANES:] = rate_ref[:, :, LANES:] * beyond(c)
 
     def sweep(source, target, lowest, highest):
         def one(x, carry):
@@ -310,7 +348,7 @@
 
         lax.fori_loop(lowest, highest, one, 0)
 
-    sweep(first_s, second_s, 1, EXT_X - 1)
+    sweep(start_ref, second_s, 1, EXT_X - 1)
     sweep(second_s, first_s, 2, EXT_X - 2)
 
     def finish(x, carry):
@@ -341,7 +379,7 @@
     blank = jnp.zeros((2 * LANES - own_rows, LANES), f32)
     for c in range(3):
         result = out_ref[c]
-        scaled = (result * stiff_s[3 : 3 + CX, :CY, :LANES]).reshape(own_rows, LANES)
+        scaled = (result * stiff_ref[...]).reshape(own_rows, LANES)
         high, low = halves(scaled)
         cut = slice(c * LANES, (c + 1) * LANES)
         turned_s[cut, : 2 * LANES] = jnp.transpose(jnp.concatenate([high, blank], axis=0)).astype(bf16)
@@ -466,36 +504,40 @@
         hull_cells.reshape(SLOT_ROWS, LANES),
         hull_patches.reshape(SLOT_ROWS, LANES),
     )
-    arrived = arrived.reshape(3 * BLOCKS, LANES)
-    source = call(
-        scatter_slots,
-        shaped(3, CX + 4, CY, CZ),
-        [pltpu.VMEM((rows, SLOTS), bf16) for rows in (2 * LANES, 6 * LANES, 12 * CY, LANES)],
-        1 << 32,
-        arrived,
-    )
+    n_gx, n_gy = lax.axis_size("gx"), lax.axis_size("gy")
     y_message = shaped(CX + 4, Y_ROWS, CZ)
-    n_gx, n_gy = lax.axis_size("gx"), lax.axis_size("gy")
     even, odd = call(
         functools.partial(pack_y, n_gx),
         (y_message, y_message),
-        [],
-        1 << 20,
+        [pltpu.VMEM((5, 2, CX, 8, CZ), f32), pltpu.SemaphoreType.DMA((10,))],
+        1 << 34,
         gx,
         gy,
-        source,
         start_field,
         stiffness,
         mass,
         xeven,
         xodd,
-        places="SS",
+        places="SSHHH",
     )
     yeven, yodd = pair_exchange("gy", even, odd)
+    arrived, yeven, yodd = lax.optimization_barrier((arrived, yeven, yodd))
+    y_message = shaped(CX + 4, 6, CZ)
+    source, even, odd = call(
+        scatter_slots,
+        (shaped(3, CX + 4, CY, CZ), y_message, y_message),
+        [pltpu.VMEM((rows, SLOTS), bf16) for rows in (2 * LANES, 6 * LANES, 12 * CY, LANES)],
+        1 << 32,
+        gy,
+        arrived.reshape(3 * BLOCKS, LANES),
+        places="S",
+    )
     rows = (EXT_X - 2) * EXT_Y
+    z_message = shaped(Z_ROWS, rows)
+    source_even, source_odd = pair_exchange("gy", even, odd)
     ext, faces = call(
-        functools.partial(widen, n_gx, n_gy),
-        (shaped(8, EXT_X, EXT_Y, CZ), shaped(Z_ROWS, rows)),
+        functools.partial(widen_fixed, n_gx, n_gy),
+        (shaped(5, EXT_X, EXT_Y, CZ), z_message),
         [],
         1 << 20,
         gx,
@@ -504,7 +546,6 @@
         start_field,
         stiffness,
         mass,
-        source,
         xeven,
         xodd,
         yeven,
@@ -512,25 +553,46 @@
         places="SSS",
     )
     faces = lax.ppermute(faces, "gz", [(0, 1), (1, 0)])
+    source_ext, source_faces = call(
+        functools.partial(widen_source, n_gy),
+        (shaped(3, EXT_X - 2, EXT_Y, CZ), z_message),
+        [],
+        1 << 20,
+        gy,
+        side,
+        source,
+        source_even,
+        source_odd,
+        places="SS",
+    )
+    source_faces = lax.ppermute(source_faces, "gz", [(0, 1), (1, 0)])
     wide = (EXT_X - 2, EXT_Y, 2 * CZ)
     full = (EXT_X, EXT_Y, 2 * CZ)
+    prepared = call(
+        prepare,
+        (shaped(3, *full), shaped(6, *wide), shaped(*wide), shaped(*wide), shaped(*wide)),
+        [pltpu.VMEM(full, f32), pltpu.VMEM(wide, f32)],
+        1 << 30,
+        side,
+        ext,
+        faces,
+        places="S",
+    )
     field, outgoing = call(
         relax_and_gather,
         (shaped(3, CX, CY, CZ), shaped(4 * count, LANES)),
         [
             pltpu.VMEM((3,) + full, f32),
             pltpu.VMEM((3,) + full, f32),
-            pltpu.VMEM(full, f32),
-            pltpu.VMEM((6,) + wide, f32),
-            pltpu.VMEM(wide, f32),
-            pltpu.VMEM(wide, f32),
             pltpu.VMEM((3,) + wide, f32),
             pltpu.VMEM((3 * LANES, 4 * LANES), bf16),
         ],
         1 << 32,
         side,
-        ext,
-        faces,
+        *prepared,
+        source_ext,
+        source_faces,
+        stiffness,
         where,
         ids,
         places="S",

time: 74.2 us -> 72.1 us (0.972)
  starting transfers between devices: 30.1 us -> 27.8 us
  Pallas kernels: 22 us -> 23.1 us
  waiting for transfers between devices: 20.2 us -> 19.2 us
    all_to_all x1, starting transfers between devices: 16.4 us -> 8.23 us  [per_device(): lax.all_to_all(packed, ('gx', 'gy'), split_axis=0, concat_axis=0, tiled=T...]
    ppermute x4 -> x6, starting transfers between devices: 7.61 us -> 12.5 us  [pair_exchange(): lax.ppermute(values, axis, pairs + [(b, a) for a, b in pairs])]
    pallas_call x7 -> x9, Pallas kernels: 22 us -> 23.1 us  [call(): pl.pallas_call(kernel, out_shape=outs, in_specs=specs(len(args), places),...]
    ppermute x4 -> x6, waiting for transfers between devices: 4.67 us -> 4.67 us  [pair_exchange(): lax.ppermute(values, axis, pairs + [(b, a) for a, b in pairs])]
  transfers between devices with their start and end apart: 7 -> 10, of which waited for: 5 -> 6; matrix products, arithmetic and copies ran while one was open for 0% -> 0% of each run, Pallas kernels for 9% -> 7%
where the time goes in v3:
time: 72.1 us; the launch traced here: 71.8 us
  starting transfers between devices  27.8 us (39%)
  Pallas kernels  23.1 us (32%)
  waiting for transfers between devices  19.2 us (27%)
  between operations  1.6 us (2%)
    pallas_call x9, Pallas kernels, call(): pl.pallas_call(kernel, out_shape=outs, in_specs=specs(len(args), places),...  23.1 us
    ppermute x6, starting transfers between devices, pair_exchange(): lax.ppermute(values, axis, pairs + [(b, a) for a, b in pairs])  12.5 us
    all_to_all x1, starting transfers between devices, per_device(): lax.all_to_all(packed, ('gx', 'gy'), split_axis=0, concat_axis=0, tiled=T...  8.23 us
    all_to_all x1, waiting for transfers between devices, per_device(): lax.all_to_all(packed, ('gx', 'gy'), split_axis=0, concat_axis=0, tiled=T...  8.03 us
    all_to_all x1, waiting for transfers between devices, per_device(): lax.all_to_all(outgoing, ('gy', 'gz'), split_axis=0, concat_axis=0, tiled...  6.28 us
    all_to_all x1, starting transfers between devices, per_device(): lax.all_to_all(outgoing, ('gy', 'gz'), split_axis=0, concat_axis=0, tiled...  5.78 us
    ppermute x6, waiting for transfers between devices, pair_exchange(): lax.ppermute(values, axis, pairs + [(b, a) for a, b in pairs])  4.67 us
  transfers between devices with their start and end apart: 10, of which 6 were waited for; matrix products, arithmetic and copies ran while one was open for 0% of the time, Pallas kernels for 7%

profile of v3, /device:TPU:1, one launch (start us, length us, event | category | flops | bytes accessed | tf_op | source)
XLA Modules:
  0.0 71.8 jit_solution(6428345429020960461)
XLA Ops:
  0.6 1.9 %pack_slots.1 = (f32[384,128]{1,0:T(8,128)}, f32[14,24,128]{2,1,0:T(8,128)S(1)}, f32[14,24,128]{2,1,0:T(8,128)S(1)}) custom-call(s32[1]{0:T(128)} %bitcast.13.gx_ref, f32[3,32,128]{2,1,0:T(8,128)} %bitcast.44, s32[32,128]{1,0:T(8,128)} %bitcast.45, s32[1,128]{1,0:T(1,128)} %bitcast.48, f32[3,8,24,128]{3,2,1,0:T(8,128)} %field_ref.1, ...), custom_call_target="tpu_custom_call" | custom-call | flops 1048576 | bytes 1048576 | tf_op jit(solution)/shard_map/pack_slots/pallas_call | solution.py:452
  2.5 2.6 %collective-permute-start = (f32[14,24,128]{2,1,0:T(8,128)S(1)}, f32[14,24,128]{2,1,0:T(8,128)S(1)}, u32[]{:S(2)}, u32[]{:S(2)}) collective-permute-start(f32[14,24,128]{2,1,0:T(8,128)S(1)} %get-tuple-element.44), channel_id=1, source_target_pairs={{0,16},{32,48},{64,80},{96,112},{128,144},{160,176},{192,208},{224... | collective-permute-start | bytes 516104 | tf_op jit(solution)/shard_map/ppermute | solution.py:469
  5.1 7.3 %collective-permute-start.1 = (f32[14,24,128]{2,1,0:T(8,128)S(1)}, f32[14,24,128]{2,1,0:T(8,128)S(1)}, u32[]{:S(2)}, u32[]{:S(2)}) collective-permute-start(f32[14,24,128]{2,1,0:T(8,128)S(1)} %get-tuple-element.45), channel_id=1, source_target_pairs={{16,32},{48,64},{80,96},{112,128},{144,160},{176,192},{208,224},{2... | collective-permute-start | bytes 516104 | tf_op jit(solution)/shard_map/ppermute | solution.py:469
  12.4 8.2 %all-to-all-start.1 = ((f32[128,1,384]{2,1,0:T(1,128)}), f32[128,1,384]{2,1,0:T(1,128)S(1)}, u32[]{:S(2)}, u32[]{:S(2)}) async-start(f32[128,1,384]{2,1,0:T(1,128)} %bitcast.18), calls=%async_computation.1 | async-start | bytes 393216 | tf_op jit(solution)/shard_map/all_to_all | solution.py:496
  20.6 0.0 collective-permute-done.xeven_ref
  20.6 0.0 collective-permute-done.1.xodd_ref
  20.6 1.1 %pack_y.1 = (f32[12,14,128]{2,1,0:T(8,128)S(1)}, f32[12,14,128]{2,1,0:T(8,128)S(1)}) custom-call(s32[1]{0:T(128)} %bitcast.13.gx_ref, s32[1]{0:T(128)} %bitcast.14.gy_ref, f32[3,8,24,128]{3,2,1,0:T(8,128)} %field_ref.1, f32[8,24,128]{2,1,0:T(8,128)} %stiff_ref.3, f32[8,24,128]{2,1,0:T(8,128)} %mass_ref.1, f32[14,24,128]{2,1,0:T(8,128)S(1)} %collective-permute-done.xeven_ref, ...), custom_call_target="tpu_custom_call" | custom-call | flops 17179869184 | bytes 1048576 | tf_op jit(solution)/shard_map/pack_y/pallas_call | solution.py:452
  21.7 0.0 copy-start
  21.7 0.0 copy-start.1
  21.7 0.0 copy-start.2
  21.7 1.0 %collective-permute-start.2 = (f32[12,14,128]{2,1,0:T(8,128)S(1)}, f32[12,14,128]{2,1,0:T(8,128)S(1)}, u32[]{:S(2)}, u32[]{:S(2)}) collective-permute-start(f32[12,14,128]{2,1,0:T(8,128)S(1)} %get-tuple-element.47), channel_id=1, source_target_pairs={{0,2},{4,6},{8,10},{12,14},{2,0},{6,4},{10,8},{14,12},{1,3},{5,7},... | collective-permute-start | bytes 258056 | tf_op jit(solution)/shard_map/ppermute | solution.py:469
  22.7 0.9 %collective-permute-start.3 = (f32[12,14,128]{2,1,0:T(8,128)S(1)}, f32[12,14,128]{2,1,0:T(8,128)S(1)}, u32[]{:S(2)}, u32[]{:S(2)}) collective-permute-start(f32[12,14,128]{2,1,0:T(8,128)S(1)} %get-tuple-element.48), channel_id=1, source_target_pairs={{2,4},{6,8},{10,12},{14,0},{4,2},{8,6},{12,10},{0,14},{3,5},{7,9},... | collective-permute-start | bytes 258056 | tf_op jit(solution)/shard_map/ppermute | solution.py:469
  23.6 0.1 collective-permute-done.2.yeven_ref
  23.7 4.2 %collective-permute-done.3.yodd_ref = f32[12,14,128]{2,1,0:T(8,128)S(1)} collective-permute-done((f32[12,14,128]{2,1,0:T(8,128)S(1)}, f32[12,14,128]{2,1,0:T(8,128)S(1)}, u32[]{:S(2)}, u32[]{:S(2)}) %collective-permute-start.3) | collective-permute-done | bytes 86048 | tf_op jit(solution)/shard_map/ppermute | solution.py:469
  27.9 8.0 %all-to-all-done.1 = f32[128,1,384]{2,1,0:T(1,128)S(1)} async-done(((f32[128,1,384]{2,1,0:T(1,128)}), f32[128,1,384]{2,1,0:T(1,128)S(1)}, u32[]{:S(2)}, u32[]{:S(2)}) %all-to-all-start.1) | async-done | bytes 196640 | tf_op jit(solution)/shard_map/all_to_all | solution.py:496
  35.9 0.0 copy-start.3
  35.9 0.0 copy-start.4
  35.9 5.2 %scatter_slots.1 = (f32[3,12,24,128]{3,2,1,0:T(8,128)S(1)}, f32[12,6,128]{2,1,0:T(8,128)S(1)}, f32[12,6,128]{2,1,0:T(8,128)S(1)}) custom-call(s32[1]{0:T(128)} %bitcast.14.gy_ref, f32[384,128]{1,0:T(8,128)S(1)} %bitcast.32), custom_call_target="tpu_custom_call" | custom-call | flops 4294967296 | bytes 1048576 | tf_op jit(solution)/shard_map/scatter_slots/pallas_call | solution.py:452
  41.1 0.5 collective-permute-start.5
  41.6 0.3 collective-permute-start.6
  41.9 0.0 copy-done
  41.9 0.0 copy-done.1
  41.9 0.0 copy-done.2
  41.9 0.4 widen_fixed.1
  42.3 0.6 collective-permute-start.4
  43.0 0.0 copy-done.3
  43.0 0.0 copy-done.4
  43.0 1.7 %route_hull.1 = (s32[96,128]{1,0:T(8,128)S(1)}, f32[48,128]{1,0:T(8,128)S(1)}) custom-call(s32[32,128]{1,0:T(8,128)S(1)} %bitcast.46, s32[32,128]{1,0:T(8,128)S(1)} %bitcast.47), custom_call_target="tpu_custom_call" | custom-call | flops 2147483648 | bytes 1048576 | tf_op jit(solution)/shard_map/route_hull/pallas_call | solution.py:452
  44.7 0.0 collective-permute-done.5.yeven_ref
  44.7 0.4 collective-permute-done.6.yodd_ref
  45.1 0.3 widen_source.1
  45.4 0.7 %collective-permute-start.7 = (f32[16,384]{1,0:T(8,128)S(1)}, f32[16,384]{1,0:T(8,128)S(1)}, u32[]{:S(2)}, u32[]{:S(2)}) collective-permute-start(f32[16,384]{1,0:T(8,128)S(1)} %get-tuple-element.63), channel_id=1, source_target_pairs={{0,1},{1,0},{2,3},{3,2},{4,5},{5,4},{6,7},{7,6},{8,9},{9,8},{10,11... | collective-permute-start | bytes 73736 | tf_op jit(solution)/shard_map/ppermute | solution.py:568
  46.2 0.0 collective-permute-done.4.z_ref
  46.2 1.8 %prepare.1 = (f32[3,14,32,256]{3,2,1,0:T(8,128)S(1)}, f32[6,12,32,256]{3,2,1,0:T(8,128)S(1)}, f32[12,32,256]{2,1,0:T(8,128)S(1)}, f32[12,32,256]{2,1,0:T(8,128)S(1)}, f32[12,32,256]{2,1,0:T(8,128)S(1)}) custom-call(s32[1]{0:T(128)} %bitcast.12.side_ref, f32[5,14,32,128]{3,2,1,0:T(8,128)S(1)} %get-tuple-element.51.ext_ref, ...), custom_call_target="tpu_custom_call" | custom-call | flops 1073741824 | bytes 1048576 | tf_op jit(solution)/shard_map/prepare/pallas_call | solution.py:452
  48.0 0.2 collective-permute-done.7.z_ref
  48.2 8.0 %relax_and_gather.1 = (f32[3,8,24,128]{3,2,1,0:T(8,128)}, f32[192,128]{1,0:T(8,128)}) custom-call(s32[1]{0:T(128)} %bitcast.12.side_ref, f32[3,14,32,256]{3,2,1,0:T(8,128)S(1)} %get-tuple-element.53.start_ref, f32[6,12,32,256]{3,2,1,0:T(8,128)S(1)} %get-tuple-element.54.weight_s, f32[12,32,256]{2,1,0:T(8,128)S(1)} %get-tuple-element.55.keep_s, ...), custom_call_target="tpu_custom_call" | custom-call | flops 4294967296 | bytes 1048576 | tf_op jit(solution)/shard_map/relax_and_gather/pallas_call | solution.py:452
  56.2 5.8 %all-to-all-start.2 = ((f32[16,1,1536]{2,1,0:T(1,128)}), f32[16,1,1536]{2,1,0:T(1,128)S(1)}, u32[]{:S(2)}, u32[]{:S(2)}) async-start(f32[16,1,1536]{2,1,0:T(1,128)} %bitcast.22), calls=%async_computation.2 | async-start | bytes 196608 | tf_op jit(solution)/shard_map/all_to_all | solution.py:601
  62.0 6.3 %all-to-all-done.2 = f32[16,1,1536]{2,1,0:T(1,128)S(1)} async-done(((f32[16,1,1536]{2,1,0:T(1,128)}), f32[16,1,1536]{2,1,0:T(1,128)S(1)}, u32[]{:S(2)}, u32[]{:S(2)}) %all-to-all-start.2) | async-done | bytes 98336 | tf_op jit(solution)/shard_map/all_to_all | solution.py:601
  68.3 2.6 %scatter_hull.1 = (f32[3,64,256]{2,1,0:T(8,128)}, s32[1]{0:T(128)}) custom-call(f32[192,128]{1,0:T(8,128)S(1)} %bitcast.33), custom_call_target="tpu_custom_call" | custom-call | flops 4294967296 | bytes 1048576 | tf_op jit(solution)/shard_map/scatter_hull/pallas_call | solution.py:452
  (1 shorter events, 0.0 us)
Async XLA Ops:
  2.5 18.1 %collective-permute-start = (f32[14,24,128]{2,1,0:T(8,128)S(1)}, f32[14,24,128]{2,1,0:T(8,128)S(1)}, u32[]{:S(2)}, u32[]{:S(2)}) collective-permute-start(f32[14,24,128]{2,1,0:T(8,128)S(1)} %get-tuple-element.44), channel_id=1, source_target_pairs={{0,16},{32,48},{64,80},{96,112},{128,144},{160,176},{192,208},{224... | collective-permute-start | bytes 516104 | tf_op jit(solution)/shard_map/ppermute | solution.py:469
  5.1 15.6 %collective-permute-start.1 = (f32[14,24,128]{2,1,0:T(8,128)S(1)}, f32[14,24,128]{2,1,0:T(8,128)S(1)}, u32[]{:S(2)}, u32[]{:S(2)}) collective-permute-start(f32[14,24,128]{2,1,0:T(8,128)S(1)} %get-tuple-element.45), channel_id=1, source_target_pairs={{16,32},{48,64},{80,96},{112,128},{144,160},{176,192},{208,224},{2... | collective-permute-start | bytes 516104 | tf_op jit(solution)/shard_map/ppermute | solution.py:469
  12.4 23.5 %all-to-all-start.1 = ((f32[128,1,384]{2,1,0:T(1,128)}), f32[128,1,384]{2,1,0:T(1,128)S(1)}, u32[]{:S(2)}, u32[]{:S(2)}) async-start(f32[128,1,384]{2,1,0:T(1,128)} %bitcast.18), calls=%async_computation.1 | async-start | bytes 393216 | tf_op jit(solution)/shard_map/all_to_all | solution.py:496
  21.7 20.2 %copy-start = (f32[3,8,24,128]{3,2,1,0:T(8,128)S(1)}, f32[3,8,24,128]{3,2,1,0:T(8,128)}, u32[]{:S(2)}) copy-start(f32[3,8,24,128]{3,2,1,0:T(8,128)} %field_ref.1) | copy-start | bytes 884740
  21.7 20.2 %copy-start.1 = (f32[8,24,128]{2,1,0:T(8,128)S(1)}, f32[8,24,128]{2,1,0:T(8,128)}, u32[]{:S(2)}) copy-start(f32[8,24,128]{2,1,0:T(8,128)} %mass_ref.1) | copy-start | bytes 294916
  21.7 20.2 %copy-start.2 = (f32[8,24,128]{2,1,0:T(8,128)S(1)}, f32[8,24,128]{2,1,0:T(8,128)}, u32[]{:S(2)}) copy-start(f32[8,24,128]{2,1,0:T(8,128)} %stiff_ref.3) | copy-start | bytes 294916
  21.7 1.9 %collective-permute-start.2 = (f32[12,14,128]{2,1,0:T(8,128)S(1)}, f32[12,14,128]{2,1,0:T(8,128)S(1)}, u32[]{:S(2)}, u32[]{:S(2)}) collective-permute-start(f32[12,14,128]{2,1,0:T(8,128)S(1)} %get-tuple-element.47), channel_id=1, source_target_pairs={{0,2},{4,6},{8,10},{12,14},{2,0},{6,4},{10,8},{14,12},{1,3},{5,7},... | collective-permute-start | bytes 258056 | tf_op jit(solution)/shard_map/ppermute | solution.py:469
  22.7 5.1 %collective-permute-start.3 = (f32[12,14,128]{2,1,0:T(8,128)S(1)}, f32[12,14,128]{2,1,0:T(8,128)S(1)}, u32[]{:S(2)}, u32[]{:S(2)}) collective-permute-start(f32[12,14,128]{2,1,0:T(8,128)S(1)} %get-tuple-element.48), channel_id=1, source_target_pairs={{2,4},{6,8},{10,12},{14,0},{4,2},{8,6},{12,10},{0,14},{3,5},{7,9},... | collective-permute-start | bytes 258056 | tf_op jit(solution)/shard_map/ppermute | solution.py:469
  35.9 7.1 %copy-start.3 = (s32[1,1,4096]{2,1,0:T(1,128)S(1)}, s32[1,1,4096]{2,1,0:T(1,128)}, u32[]{:S(2)}) copy-start(s32[1,1,4096]{2,1,0:T(1,128)} %param.16) | copy-start | bytes 49156
  35.9 7.1 %copy-start.4 = (s32[1,1,4096]{2,1,0:T(1,128)S(1)}, s32[1,1,4096]{2,1,0:T(1,128)}, u32[]{:S(2)}) copy-start(s32[1,1,4096]{2,1,0:T(1,128)} %param.17) | copy-start | bytes 49156
  41.1 3.6 %collective-permute-start.5 = (f32[12,6,128]{2,1,0:T(8,128)S(1)}, f32[12,6,128]{2,1,0:T(8,128)S(1)}, u32[]{:S(2)}, u32[]{:S(2)}) collective-permute-start(f32[12,6,128]{2,1,0:T(8,128)S(1)} %get-tuple-element.60), channel_id=1, source_target_pairs={{0,2},{4,6},{8,10},{12,14},{2,0},{6,4},{10,8},{14,12},{1,3},{5,7},... | collective-permute-start | bytes 110600 | tf_op jit(solution)/shard_map/ppermute | solution.py:469
  41.6 3.5 %collective-permute-start.6 = (f32[12,6,128]{2,1,0:T(8,128)S(1)}, f32[12,6,128]{2,1,0:T(8,128)S(1)}, u32[]{:S(2)}, u32[]{:S(2)}) collective-permute-start(f32[12,6,128]{2,1,0:T(8,128)S(1)} %get-tuple-element.61), channel_id=1, source_target_pairs={{2,4},{6,8},{10,12},{14,0},{4,2},{8,6},{12,10},{0,14},{3,5},{7,9},... | collective-permute-start | bytes 110600 | tf_op jit(solution)/shard_map/ppermute | solution.py:469
  42.3 3.8 %collective-permute-start.4 = (f32[16,384]{1,0:T(8,128)S(1)}, f32[16,384]{1,0:T(8,128)S(1)}, u32[]{:S(2)}, u32[]{:S(2)}) collective-permute-start(f32[16,384]{1,0:T(8,128)S(1)} %get-tuple-element.52), channel_id=1, source_target_pairs={{0,1},{1,0},{2,3},{3,2},{4,5},{5,4},{6,7},{7,6},{8,9},{9,8},{10,11... | collective-permute-start | bytes 73736 | tf_op jit(solution)/shard_map/ppermute | solution.py:555
  45.4 2.7 %collective-permute-start.7 = (f32[16,384]{1,0:T(8,128)S(1)}, f32[16,384]{1,0:T(8,128)S(1)}, u32[]{:S(2)}, u32[]{:S(2)}) collective-permute-start(f32[16,384]{1,0:T(8,128)S(1)} %get-tuple-element.63), channel_id=1, source_target_pairs={{0,1},{1,0},{2,3},{3,2},{4,5},{5,4},{6,7},{7,6},{8,9},{9,8},{10,11... | collective-permute-start | bytes 73736 | tf_op jit(solution)/shard_map/ppermute | solution.py:568
  56.2 12.1 %all-to-all-start.2 = ((f32[16,1,1536]{2,1,0:T(1,128)}), f32[16,1,1536]{2,1,0:T(1,128)S(1)}, u32[]{:S(2)}, u32[]{:S(2)}) async-start(f32[16,1,1536]{2,1,0:T(1,128)} %bitcast.22), calls=%async_computation.2 | async-start | bytes 196608 | tf_op jit(solution)/shard_map/all_to_all | solution.py:601

commit v4 on v3

--- a/solution.py
+++ b/solution.py
@@ -91,7 +91,7 @@
         copy.wait()
 
 
-def scatter_slots(gy_ref, slots_ref, source_ref, even_ref, odd_ref, rows_s, lanes_s, left_s, right_s):
+def scatter_slots(gy_ref, slots_ref, source_ref, even_ref, odd_ref):
     lane = iota((SLOT_ROWS, LANES), 1)
     quarter = lane // CAP
     own_rows = CY * CX
@@ -113,26 +113,29 @@
     lane_number = iota((LANES, LANES), 0)
     row_number = iota((2 * LANES, LANES), 0)
     side_number = iota((side_rows, LANES), 0)
+    batch = 8
     rows, lanes, pieces = unpack(1)
-    for r in range(SLOT_ROWS):
-        cut = slice(r * LANES, (r + 1) * LANES)
-        rows_s[:, cut] = jnp.where(row_number == rows[r : r + 1, :], 1.0, 0.0).astype(bf16)
-        here = lane_number == lanes[r : r + 1, :]
-        for n in range(6):
-            lanes_s[n * LANES : (n + 1) * LANES, cut] = jnp.where(here, pieces[n][r : r + 1, :], 0.0).astype(bf16)
-    sums = dot_last(lanes_s[...], rows_s[...])
+    sums = jnp.zeros((6 * LANES, 2 * LANES), f32)
+    for start in range(0, SLOT_ROWS, batch):
+        lefts, rights = [], []
+        for r in range(start, start + batch):
+            here = lane_number == lanes[r : r + 1, :]
+            lefts.append(jnp.concatenate([jnp.where(here, piece[r : r + 1, :], 0.0).astype(bf16) for piece in pieces], axis=0))
+            rights.append(jnp.where(row_number == rows[r : r + 1, :], 1.0, 0.0).astype(bf16))
+        sums = sums + dot_last(jnp.concatenate(lefts, axis=1), jnp.concatenate(rights, axis=1))
     for c in range(3):
         one = sums[2 * c * LANES : (2 * c + 1) * LANES] + sums[(2 * c + 1) * LANES : (2 * c + 2) * LANES]
         source_ref[c, 2 : 2 + CX] = jnp.transpose(one)[:own_rows].reshape(CX, CY, LANES)
     for k, first, target in ((0, own_rows - side_rows, 0), (2, 0, 2 + CX)):
         rows, lanes, pieces = unpack(k)
-        for r in range(SLOT_ROWS):
-            cut = slice(r * LANES, (r + 1) * LANES)
-            here = side_number == rows[r : r + 1, :] - first
-            for n in range(6):
-                left_s[n * side_rows : (n + 1) * side_rows, cut] = jnp.where(here, pieces[n][r : r + 1, :], 0.0).astype(bf16)
-            right_s[:, cut] = jnp.where(lane_number == lanes[r : r + 1, :], 1.0, 0.0).astype(bf16)
-        sums = dot_last(left_s[...], right_s[...])
+        sums = jnp.zeros((6 * side_rows, LANES), f32)
+        for start in range(0, SLOT_ROWS, batch):
+            lefts, rights = [], []
+            for r in range(start, start + batch):
+                here = side_number == rows[r : r + 1, :] - first
+                lefts.append(jnp.concatenate([jnp.where(here, piece[r : r + 1, :], 0.0).astype(bf16) for piece in pieces], axis=0))
+                rights.append(jnp.where(lane_number == lanes[r : r + 1, :], 1.0, 0.0).astype(bf16))
+            sums = sums + dot_last(jnp.concatenate(lefts, axis=1), jnp.concatenate(rights, axis=1))
         for c in range(3):
             one = sums[2 * c * side_rows : (2 * c + 1) * side_rows] + sums[(2 * c + 1) * side_rows : (2 * c + 2) * side_rows]
             source_ref[c, target : target + 2] = one.reshape(2, CY, LANES)
@@ -326,7 +329,7 @@
     first_s,
     second_s,
     push_s,
-    turned_s,
+    pieces_s,
 ):
     beyond = unpack_z(side_ref[0], z_ref)
     for c in range(3):
@@ -376,31 +379,26 @@
     lax.fori_loop(3, 3 + CX, finish, 0)
 
     own_rows = CX * CY
-    blank = jnp.zeros((2 * LANES - own_rows, LANES), f32)
     for c in range(3):
-        result = out_ref[c]
-        scaled = (result * stiff_ref[...]).reshape(own_rows, LANES)
-        high, low = halves(scaled)
-        cut = slice(c * LANES, (c + 1) * LANES)
-        turned_s[cut, : 2 * LANES] = jnp.transpose(jnp.concatenate([high, blank], axis=0)).astype(bf16)
-        turned_s[cut, 2 * LANES :] = jnp.transpose(jnp.concatenate([low, blank], axis=0)).astype(bf16)
+        scaled = (out_ref[c] * stiff_ref[...]).reshape(own_rows, LANES)
+        for n, piece in enumerate(halves(scaled)):
+            pieces_s[c * own_rows : (c + 1) * own_rows, n * LANES : (n + 1) * LANES] = piece.astype(bf16)
     count = HULL_DESTS * HULL_ROWS
-    row_number = iota((2 * LANES, LANES), 0)
+    row_number = iota((own_rows, LANES), 0)
     lane_number = iota((LANES, LANES), 0)
     group = 2 * HULL_ROWS
     for g in range(count // group):
         chosen = []
+        for r in range(g * group, (g + 1) * group):
+            chosen.append(jnp.where(lane_number == where_ref[count + r : count + r + 1, :], 1.0, 0.0).astype(bf16))
+        chosen = jnp.concatenate(chosen, axis=1)
+        found = jnp.dot(pieces_s[...], jnp.concatenate([chosen, chosen], axis=0), preferred_element_type=f32)
         for i in range(group):
             r = g * group + i
-            chosen.append(jnp.where(row_number == where_ref[r : r + 1, :], 1.0, 0.0).astype(bf16))
-        chosen = jnp.concatenate(chosen, axis=1)
-        found = jnp.dot(turned_s[...], jnp.concatenate([chosen, chosen], axis=0), preferred_element_type=f32)
-        for i in range(group):
-            r = g * group + i
-            here = lane_number == where_ref[count + r : count + r + 1, :]
+            here = row_number == where_ref[r : r + 1, :]
             base = r // HULL_ROWS * 4 * HULL_ROWS + r % HULL_ROWS
             for c in range(3):
-                part = found[c * LANES : (c + 1) * LANES, i * LANES : (i + 1) * LANES]
+                part = found[c * own_rows : (c + 1) * own_rows, i * LANES : (i + 1) * LANES]
                 spot = base + c * HULL_ROWS
                 message_ref[spot : spot + 1, :] = jnp.sum(jnp.where(here, part, 0.0), axis=0, keepdims=True)
             spot = base + 3 * HULL_ROWS
@@ -526,7 +524,7 @@
     source, even, odd = call(
         scatter_slots,
         (shaped(3, CX + 4, CY, CZ), y_message, y_message),
-        [pltpu.VMEM((rows, SLOTS), bf16) for rows in (2 * LANES, 6 * LANES, 12 * CY, LANES)],
+        [],
         1 << 32,
         gy,
         arrived.reshape(3 * BLOCKS, LANES),
@@ -585,7 +583,7 @@
             pltpu.VMEM((3,) + full, f32),
             pltpu.VMEM((3,) + full, f32),
             pltpu.VMEM((3,) + wide, f32),
-            pltpu.VMEM((3 * LANES, 4 * LANES), bf16),
+            pltpu.VMEM((3 * CX * CY, 2 * LANES), bf16),
         ],
         1 << 32,
         side,

time: 72.1 us -> 69.4 us (0.963)
  Pallas kernels: 23.1 us -> 20.2 us
    pallas_call x9, Pallas kernels: 23.1 us -> 20.2 us  [call(): pl.pallas_call(kernel, out_shape=outs, in_specs=specs(len(args), places),...]
  transfers between devices with their start and end apart: 10 -> 10, of which waited for: 6 -> 6; matrix products, arithmetic and copies ran while one was open for 0% -> 0% of each run, Pallas kernels for 7% -> 8%
where the time goes in v4:
time: 69.4 us; the launch traced here: 69.1 us
  starting transfers between devices  27.3 us (39%)
  Pallas kernels  20.2 us (29%)
  waiting for transfers between devices  19.9 us (29%)
  between operations  1.6 us (2%)
    pallas_call x9, Pallas kernels, call(): pl.pallas_call(kernel, out_shape=outs, in_specs=specs(len(args), places),...  20.2 us
    ppermute x6, starting transfers between devices, pair_exchange(): lax.ppermute(values, axis, pairs + [(b, a) for a, b in pairs])  12.5 us
    all_to_all x1, starting transfers between devices, per_device(): lax.all_to_all(packed, ('gx', 'gy'), split_axis=0, concat_axis=0, tiled=T...  8.23 us
    all_to_all x1, waiting for transfers between devices, per_device(): lax.all_to_all(packed, ('gx', 'gy'), split_axis=0, concat_axis=0, tiled=T...  8.03 us
    all_to_all x1, waiting for transfers between devices, per_device(): lax.all_to_all(outgoing, ('gy', 'gz'), split_axis=0, concat_axis=0, tiled...  6.28 us
    all_to_all x1, starting transfers between devices, per_device(): lax.all_to_all(outgoing, ('gy', 'gz'), split_axis=0, concat_axis=0, tiled...  5.48 us
    ppermute x6, waiting for transfers between devices, pair_exchange(): lax.ppermute(values, axis, pairs + [(b, a) for a, b in pairs])  5.14 us
  transfers between devices with their start and end apart: 10, of which 6 were waited for; matrix products, arithmetic and copies ran while one was open for 0% of the time, Pallas kernels for 8%

profile of v4, /device:TPU:1, one launch (start us, length us, event | category | flops | bytes accessed | tf_op | source)
XLA Modules:
  0.0 69.1 jit_solution(8704613371165360822)
XLA Ops:
  0.6 1.9 %pack_slots.1 = (f32[384,128]{1,0:T(8,128)}, f32[14,24,128]{2,1,0:T(8,128)S(1)}, f32[14,24,128]{2,1,0:T(8,128)S(1)}) custom-call(s32[1]{0:T(128)} %bitcast.13.gx_ref, f32[3,32,128]{2,1,0:T(8,128)} %bitcast.44, s32[32,128]{1,0:T(8,128)} %bitcast.45, s32[1,128]{1,0:T(1,128)} %bitcast.48, f32[3,8,24,128]{3,2,1,0:T(8,128)} %field_ref.1, ...), custom_call_target="tpu_custom_call" | custom-call | flops 1048576 | bytes 1048576 | tf_op jit(solution)/shard_map/pack_slots/pallas_call | solution.py:450
  2.5 2.6 %collective-permute-start = (f32[14,24,128]{2,1,0:T(8,128)S(1)}, f32[14,24,128]{2,1,0:T(8,128)S(1)}, u32[]{:S(2)}, u32[]{:S(2)}) collective-permute-start(f32[14,24,128]{2,1,0:T(8,128)S(1)} %get-tuple-element.44), channel_id=1, source_target_pairs={{0,16},{32,48},{64,80},{96,112},{128,144},{160,176},{192,208},{224... | collective-permute-start | bytes 516104 | tf_op jit(solution)/shard_map/ppermute | solution.py:467
  5.1 7.3 %collective-permute-start.1 = (f32[14,24,128]{2,1,0:T(8,128)S(1)}, f32[14,24,128]{2,1,0:T(8,128)S(1)}, u32[]{:S(2)}, u32[]{:S(2)}) collective-permute-start(f32[14,24,128]{2,1,0:T(8,128)S(1)} %get-tuple-element.45), channel_id=1, source_target_pairs={{16,32},{48,64},{80,96},{112,128},{144,160},{176,192},{208,224},{2... | collective-permute-start | bytes 516104 | tf_op jit(solution)/shard_map/ppermute | solution.py:467
  12.4 8.2 %all-to-all-start.1 = ((f32[128,1,384]{2,1,0:T(1,128)}), f32[128,1,384]{2,1,0:T(1,128)S(1)}, u32[]{:S(2)}, u32[]{:S(2)}) async-start(f32[128,1,384]{2,1,0:T(1,128)} %bitcast.18), calls=%async_computation.1 | async-start | bytes 393216 | tf_op jit(solution)/shard_map/all_to_all | solution.py:494
  20.6 0.0 collective-permute-done.xeven_ref
  20.6 0.0 collective-permute-done.1.xodd_ref
  20.6 1.1 %pack_y.1 = (f32[12,14,128]{2,1,0:T(8,128)S(1)}, f32[12,14,128]{2,1,0:T(8,128)S(1)}) custom-call(s32[1]{0:T(128)} %bitcast.13.gx_ref, s32[1]{0:T(128)} %bitcast.14.gy_ref, f32[3,8,24,128]{3,2,1,0:T(8,128)} %field_ref.1, f32[8,24,128]{2,1,0:T(8,128)} %stiff_ref.3, f32[8,24,128]{2,1,0:T(8,128)} %mass_ref.1, f32[14,24,128]{2,1,0:T(8,128)S(1)} %collective-permute-done.xeven_ref, ...), custom_call_target="tpu_custom_call" | custom-call | flops 17179869184 | bytes 1048576 | tf_op jit(solution)/shard_map/pack_y/pallas_call | solution.py:450
  21.7 0.0 copy-start
  21.7 0.0 copy-start.1
  21.7 0.0 copy-start.2
  21.7 1.0 %collective-permute-start.2 = (f32[12,14,128]{2,1,0:T(8,128)S(1)}, f32[12,14,128]{2,1,0:T(8,128)S(1)}, u32[]{:S(2)}, u32[]{:S(2)}) collective-permute-start(f32[12,14,128]{2,1,0:T(8,128)S(1)} %get-tuple-element.47), channel_id=1, source_target_pairs={{0,2},{4,6},{8,10},{12,14},{2,0},{6,4},{10,8},{14,12},{1,3},{5,7},... | collective-permute-start | bytes 258056 | tf_op jit(solution)/shard_map/ppermute | solution.py:467
  22.7 0.9 %collective-permute-start.3 = (f32[12,14,128]{2,1,0:T(8,128)S(1)}, f32[12,14,128]{2,1,0:T(8,128)S(1)}, u32[]{:S(2)}, u32[]{:S(2)}) collective-permute-start(f32[12,14,128]{2,1,0:T(8,128)S(1)} %get-tuple-element.48), channel_id=1, source_target_pairs={{2,4},{6,8},{10,12},{14,0},{4,2},{8,6},{12,10},{0,14},{3,5},{7,9},... | collective-permute-start | bytes 258056 | tf_op jit(solution)/shard_map/ppermute | solution.py:467
  23.6 0.1 collective-permute-done.2.yeven_ref
  23.7 4.2 %collective-permute-done.3.yodd_ref = f32[12,14,128]{2,1,0:T(8,128)S(1)} collective-permute-done((f32[12,14,128]{2,1,0:T(8,128)S(1)}, f32[12,14,128]{2,1,0:T(8,128)S(1)}, u32[]{:S(2)}, u32[]{:S(2)}) %collective-permute-start.3) | collective-permute-done | bytes 86048 | tf_op jit(solution)/shard_map/ppermute | solution.py:467
  27.9 8.0 %all-to-all-done.1 = f32[128,1,384]{2,1,0:T(1,128)S(1)} async-done(((f32[128,1,384]{2,1,0:T(1,128)}), f32[128,1,384]{2,1,0:T(1,128)S(1)}, u32[]{:S(2)}, u32[]{:S(2)}) %all-to-all-start.1) | async-done | bytes 196640 | tf_op jit(solution)/shard_map/all_to_all | solution.py:494
  35.9 0.0 copy-start.3
  35.9 0.0 copy-start.4
  35.9 3.2 %scatter_slots.1 = (f32[3,12,24,128]{3,2,1,0:T(8,128)S(1)}, f32[12,6,128]{2,1,0:T(8,128)S(1)}, f32[12,6,128]{2,1,0:T(8,128)S(1)}) custom-call(s32[1]{0:T(128)} %bitcast.14.gy_ref, f32[384,128]{1,0:T(8,128)S(1)} %bitcast.32), custom_call_target="tpu_custom_call" | custom-call | flops 4294967296 | bytes 1048576 | tf_op jit(solution)/shard_map/scatter_slots/pallas_call | solution.py:450
  39.1 0.5 collective-permute-start.5
  39.6 0.3 collective-permute-start.6
  39.9 0.0 copy-done
  39.9 0.0 copy-done.1
  39.9 0.0 copy-done.2
  39.9 0.4 widen_fixed.1
  40.3 0.5 collective-permute-start.4
  40.8 0.0 copy-done.3
  40.8 0.0 copy-done.4
  40.8 1.7 %route_hull.1 = (s32[96,128]{1,0:T(8,128)S(1)}, f32[48,128]{1,0:T(8,128)S(1)}) custom-call(s32[32,128]{1,0:T(8,128)S(1)} %bitcast.46, s32[32,128]{1,0:T(8,128)S(1)} %bitcast.47), custom_call_target="tpu_custom_call" | custom-call | flops 2147483648 | bytes 1048576 | tf_op jit(solution)/shard_map/route_hull/pallas_call | solution.py:450
  42.5 0.0 collective-permute-done.5.yeven_ref
  42.5 0.9 %collective-permute-done.6.yodd_ref = f32[12,6,128]{2,1,0:T(8,128)S(1)} collective-permute-done((f32[12,6,128]{2,1,0:T(8,128)S(1)}, f32[12,6,128]{2,1,0:T(8,128)S(1)}, u32[]{:S(2)}, u32[]{:S(2)}) %collective-permute-start.6) | collective-permute-done | bytes 36896 | tf_op jit(solution)/shard_map/ppermute | solution.py:467
  43.4 0.3 widen_source.1
  43.7 0.6 collective-permute-start.7
  44.4 0.0 collective-permute-done.4.z_ref
  44.4 1.8 %prepare.1 = (f32[3,14,32,256]{3,2,1,0:T(8,128)S(1)}, f32[6,12,32,256]{3,2,1,0:T(8,128)S(1)}, f32[12,32,256]{2,1,0:T(8,128)S(1)}, f32[12,32,256]{2,1,0:T(8,128)S(1)}, f32[12,32,256]{2,1,0:T(8,128)S(1)}) custom-call(s32[1]{0:T(128)} %bitcast.12.side_ref, f32[5,14,32,128]{3,2,1,0:T(8,128)S(1)} %get-tuple-element.51.ext_ref, ...), custom_call_target="tpu_custom_call" | custom-call | flops 1073741824 | bytes 1048576 | tf_op jit(solution)/shard_map/prepare/pallas_call | solution.py:450
  46.2 0.5 collective-permute-done.7.z_ref
  46.6 7.2 %relax_and_gather.1 = (f32[3,8,24,128]{3,2,1,0:T(8,128)}, f32[192,128]{1,0:T(8,128)}) custom-call(s32[1]{0:T(128)} %bitcast.12.side_ref, f32[3,14,32,256]{3,2,1,0:T(8,128)S(1)} %get-tuple-element.53.start_ref, f32[6,12,32,256]{3,2,1,0:T(8,128)S(1)} %get-tuple-element.54.weight_s, f32[12,32,256]{2,1,0:T(8,128)S(1)} %get-tuple-element.55.keep_s, ...), custom_call_target="tpu_custom_call" | custom-call | flops 4294967296 | bytes 1048576 | tf_op jit(solution)/shard_map/relax_and_gather/pallas_call | solution.py:450
  53.8 5.5 %all-to-all-start.2 = ((f32[16,1,1536]{2,1,0:T(1,128)}), f32[16,1,1536]{2,1,0:T(1,128)S(1)}, u32[]{:S(2)}, u32[]{:S(2)}) async-start(f32[16,1,1536]{2,1,0:T(1,128)} %bitcast.22), calls=%async_computation.2 | async-start | bytes 196608 | tf_op jit(solution)/shard_map/all_to_all | solution.py:599
  59.3 6.3 %all-to-all-done.2 = f32[16,1,1536]{2,1,0:T(1,128)S(1)} async-done(((f32[16,1,1536]{2,1,0:T(1,128)}), f32[16,1,1536]{2,1,0:T(1,128)S(1)}, u32[]{:S(2)}, u32[]{:S(2)}) %all-to-all-start.2) | async-done | bytes 98336 | tf_op jit(solution)/shard_map/all_to_all | solution.py:599
  65.6 2.6 %scatter_hull.1 = (f32[3,64,256]{2,1,0:T(8,128)}, s32[1]{0:T(128)}) custom-call(f32[192,128]{1,0:T(8,128)S(1)} %bitcast.33), custom_call_target="tpu_custom_call" | custom-call | flops 4294967296 | bytes 1048576 | tf_op jit(solution)/shard_map/scatter_hull/pallas_call | solution.py:450
  (1 shorter events, 0.0 us)
Async XLA Ops:
  2.5 18.1 %collective-permute-start = (f32[14,24,128]{2,1,0:T(8,128)S(1)}, f32[14,24,128]{2,1,0:T(8,128)S(1)}, u32[]{:S(2)}, u32[]{:S(2)}) collective-permute-start(f32[14,24,128]{2,1,0:T(8,128)S(1)} %get-tuple-element.44), channel_id=1, source_target_pairs={{0,16},{32,48},{64,80},{96,112},{128,144},{160,176},{192,208},{224... | collective-permute-start | bytes 516104 | tf_op jit(solution)/shard_map/ppermute | solution.py:467
  5.1 15.6 %collective-permute-start.1 = (f32[14,24,128]{2,1,0:T(8,128)S(1)}, f32[14,24,128]{2,1,0:T(8,128)S(1)}, u32[]{:S(2)}, u32[]{:S(2)}) collective-permute-start(f32[14,24,128]{2,1,0:T(8,128)S(1)} %get-tuple-element.45), channel_id=1, source_target_pairs={{16,32},{48,64},{80,96},{112,128},{144,160},{176,192},{208,224},{2... | collective-permute-start | bytes 516104 | tf_op jit(solution)/shard_map/ppermute | solution.py:467
  12.4 23.5 %all-to-all-start.1 = ((f32[128,1,384]{2,1,0:T(1,128)}), f32[128,1,384]{2,1,0:T(1,128)S(1)}, u32[]{:S(2)}, u32[]{:S(2)}) async-start(f32[128,1,384]{2,1,0:T(1,128)} %bitcast.18), calls=%async_computation.1 | async-start | bytes 393216 | tf_op jit(solution)/shard_map/all_to_all | solution.py:494
  21.7 18.2 %copy-start = (f32[3,8,24,128]{3,2,1,0:T(8,128)S(1)}, f32[3,8,24,128]{3,2,1,0:T(8,128)}, u32[]{:S(2)}) copy-start(f32[3,8,24,128]{3,2,1,0:T(8,128)} %field_ref.1) | copy-start | bytes 884740
  21.7 18.2 %copy-start.1 = (f32[8,24,128]{2,1,0:T(8,128)S(1)}, f32[8,24,128]{2,1,0:T(8,128)}, u32[]{:S(2)}) copy-start(f32[8,24,128]{2,1,0:T(8,128)} %mass_ref.1) | copy-start | bytes 294916
  21.7 18.1 %copy-start.2 = (f32[8,24,128]{2,1,0:T(8,128)S(1)}, f32[8,24,128]{2,1,0:T(8,128)}, u32[]{:S(2)}) copy-start(f32[8,24,128]{2,1,0:T(8,128)} %stiff_ref.3) | copy-start | bytes 294916
  21.7 1.9 %collective-permute-start.2 = (f32[12,14,128]{2,1,0:T(8,128)S(1)}, f32[12,14,128]{2,1,0:T(8,128)S(1)}, u32[]{:S(2)}, u32[]{:S(2)}) collective-permute-start(f32[12,14,128]{2,1,0:T(8,128)S(1)} %get-tuple-element.47), channel_id=1, source_target_pairs={{0,2},{4,6},{8,10},{12,14},{2,0},{6,4},{10,8},{14,12},{1,3},{5,7},... | collective-permute-start | bytes 258056 | tf_op jit(solution)/shard_map/ppermute | solution.py:467
  22.7 5.1 %collective-permute-start.3 = (f32[12,14,128]{2,1,0:T(8,128)S(1)}, f32[12,14,128]{2,1,0:T(8,128)S(1)}, u32[]{:S(2)}, u32[]{:S(2)}) collective-permute-start(f32[12,14,128]{2,1,0:T(8,128)S(1)} %get-tuple-element.48), channel_id=1, source_target_pairs={{2,4},{6,8},{10,12},{14,0},{4,2},{8,6},{12,10},{0,14},{3,5},{7,9},... | collective-permute-start | bytes 258056 | tf_op jit(solution)/shard_map/ppermute | solution.py:467
  35.9 4.9 %copy-start.3 = (s32[1,1,4096]{2,1,0:T(1,128)S(1)}, s32[1,1,4096]{2,1,0:T(1,128)}, u32[]{:S(2)}) copy-start(s32[1,1,4096]{2,1,0:T(1,128)} %param.16) | copy-start | bytes 49156
  35.9 4.9 %copy-start.4 = (s32[1,1,4096]{2,1,0:T(1,128)S(1)}, s32[1,1,4096]{2,1,0:T(1,128)}, u32[]{:S(2)}) copy-start(s32[1,1,4096]{2,1,0:T(1,128)} %param.17) | copy-start | bytes 49156
  39.1 3.4 %collective-permute-start.5 = (f32[12,6,128]{2,1,0:T(8,128)S(1)}, f32[12,6,128]{2,1,0:T(8,128)S(1)}, u32[]{:S(2)}, u32[]{:S(2)}) collective-permute-start(f32[12,6,128]{2,1,0:T(8,128)S(1)} %get-tuple-element.60), channel_id=1, source_target_pairs={{0,2},{4,6},{8,10},{12,14},{2,0},{6,4},{10,8},{14,12},{1,3},{5,7},... | collective-permute-start | bytes 110600 | tf_op jit(solution)/shard_map/ppermute | solution.py:467
  39.6 3.8 %collective-permute-start.6 = (f32[12,6,128]{2,1,0:T(8,128)S(1)}, f32[12,6,128]{2,1,0:T(8,128)S(1)}, u32[]{:S(2)}, u32[]{:S(2)}) collective-permute-start(f32[12,6,128]{2,1,0:T(8,128)S(1)} %get-tuple-element.61), channel_id=1, source_target_pairs={{2,4},{6,8},{10,12},{14,0},{4,2},{8,6},{12,10},{0,14},{3,5},{7,9},... | collective-permute-start | bytes 110600 | tf_op jit(solution)/shard_map/ppermute | solution.py:467
  40.3 4.1 %collective-permute-start.4 = (f32[16,384]{1,0:T(8,128)S(1)}, f32[16,384]{1,0:T(8,128)S(1)}, u32[]{:S(2)}, u32[]{:S(2)}) collective-permute-start(f32[16,384]{1,0:T(8,128)S(1)} %get-tuple-element.52), channel_id=1, source_target_pairs={{0,1},{1,0},{2,3},{3,2},{4,5},{5,4},{6,7},{7,6},{8,9},{9,8},{10,11... | collective-permute-start | bytes 73736 | tf_op jit(solution)/shard_map/ppermute | solution.py:553
  43.7 2.9 %collective-permute-start.7 = (f32[16,384]{1,0:T(8,128)S(1)}, f32[16,384]{1,0:T(8,128)S(1)}, u32[]{:S(2)}, u32[]{:S(2)}) collective-permute-start(f32[16,384]{1,0:T(8,128)S(1)} %get-tuple-element.63), channel_id=1, source_target_pairs={{0,1},{1,0},{2,3},{3,2},{4,5},{5,4},{6,7},{7,6},{8,9},{9,8},{10,11... | collective-permute-start | bytes 73736 | tf_op jit(solution)/shard_map/ppermute | solution.py:566
  53.8 11.8 %all-to-all-start.2 = ((f32[16,1,1536]{2,1,0:T(1,128)}), f32[16,1,1536]{2,1,0:T(1,128)S(1)}, u32[]{:S(2)}, u32[]{:S(2)}) async-start(f32[16,1,1536]{2,1,0:T(1,128)} %bitcast.22), calls=%async_computation.2 | async-start | bytes 196608 | tf_op jit(solution)/shard_map/all_to_all | solution.py:599

commit v5 on v4

--- a/solution.py
+++ b/solution.py
@@ -295,7 +295,7 @@
     mass_s[:, :, :LANES] = ext_ref[4, 1 : EXT_X - 1]
     mass_s[:, :, LANES:] = beyond(4)
 
-    def one(i, carry):
+    def one(i):
         middle, others = around(lambda x: stiff_s[x], i + 1)
         weights = [0.5 * (middle + other) for other in others]
         weight_sum = weights[0] + weights[1] + weights[2] + weights[3] + weights[4] + weights[5]
@@ -307,9 +307,9 @@
         keep_ref[i] = jnp.where(inside, 1.0 - rate * (weight_sum + mass), 0.0)
         couple_ref[i] = 0.25 * rate * mass
         rate_ref[i] = rate
-        return carry
-
-    lax.fori_loop(0, EXT_X - 2, one, 0)
+
+    for i in range(EXT_X - 2):
+        one(i)
 
 
 def relax_and_gather(
@@ -337,7 +337,7 @@
         push_s[c, :, :, LANES:] = rate_ref[:, :, LANES:] * beyond(c)
 
     def sweep(source, target, lowest, highest):
-        def one(x, carry):
+        def one(x):
             i = x - 1
             gathered = [around(lambda y, c=c: source[c, y], x) for c in range(3)]
             shared = couple_s[i] * (gathered[0][0] + gathered[1][0] + gathered[2][0])
@@ -347,14 +347,14 @@
                 for n in range(6):
                     value = value + weight_s[n, i] * others[n]
                 target[c, x] = value
-            return carry
-
-        lax.fori_loop(lowest, highest, one, 0)
+
+        for x in range(lowest, highest):
+            one(x)
 
     sweep(start_ref, second_s, 1, EXT_X - 1)
     sweep(second_s, first_s, 2, EXT_X - 2)
 
-    def finish(x, carry):
+    def finish(x):
         i = x - 1
         middles = [first_s[c, x, :CY, :LANES] for c in range(3)]
         shared = couple_s[i, :CY, :LANES] * (middles[0] + middles[1] + middles[2])
@@ -373,10 +373,10 @@
             for n in range(6):
                 value = value + weight_s[n, i, :CY, :LANES] * others[n]
             out_ref[c, x - 3] = value
-        return carry
 
     last_lane = iota((CY, LANES), 1)
-    lax.fori_loop(3, 3 + CX, finish, 0)
+    for x in range(3, 3 + CX):
+        finish(x)
 
     own_rows = CX * CY
     for c in range(3):

time: 69.4 us -> 67.8 us (0.977)
  Pallas kernels: 20.2 us -> 17.8 us
  waiting for transfers between devices: 19.9 us -> 20.7 us
    pallas_call x9, Pallas kernels: 20.2 us -> 17.8 us  [call(): pl.pallas_call(kernel, out_shape=outs, in_specs=specs(len(args), places),...]
    ppermute x1, waiting for transfers between devices: 0.47 us -> 1.26 us  [per_device(): source_faces = lax.ppermute(source_faces, 'gz', [(0, 1), (1, 0)])]
  transfers between devices with their start and end apart: 10 -> 10, of which waited for: 6 -> 6; matrix products, arithmetic and copies ran while one was open for 0% -> 0% of each run, Pallas kernels for 8% -> 7%
where the time goes in v5:
time: 67.8 us; the launch traced here: 67.4 us
  starting transfers between devices  27.3 us (40%)
  waiting for transfers between devices  20.7 us (31%)
  Pallas kernels  17.8 us (26%)
  between operations  1.6 us (2%)
    pallas_call x9, Pallas kernels, call(): pl.pallas_call(kernel, out_shape=outs, in_specs=specs(len(args), places),...  17.8 us
    ppermute x6, starting transfers between devices, pair_exchange(): lax.ppermute(values, axis, pairs + [(b, a) for a, b in pairs])  12.5 us
    all_to_all x1, starting transfers between devices, per_device(): lax.all_to_all(packed, ('gx', 'gy'), split_axis=0, concat_axis=0, tiled=T...  8.23 us
    all_to_all x1, waiting for transfers between devices, per_device(): lax.all_to_all(packed, ('gx', 'gy'), split_axis=0, concat_axis=0, tiled=T...  8.03 us
    all_to_all x1, waiting for transfers between devices, per_device(): lax.all_to_all(outgoing, ('gy', 'gz'), split_axis=0, concat_axis=0, tiled...  6.28 us
    all_to_all x1, starting transfers between devices, per_device(): lax.all_to_all(outgoing, ('gy', 'gz'), split_axis=0, concat_axis=0, tiled...  5.49 us
    ppermute x6, waiting for transfers between devices, pair_exchange(): lax.ppermute(values, axis, pairs + [(b, a) for a, b in pairs])  5.14 us
  transfers between devices with their start and end apart: 10, of which 6 were waited for; matrix products, arithmetic and copies ran while one was open for 0% of the time, Pallas kernels for 7%

profile of v5, /device:TPU:1, one launch (start us, length us, event | category | flops | bytes accessed | tf_op | source)
XLA Modules:
  0.0 67.4 jit_solution(10927028594552440867)
XLA Ops:
  0.6 1.9 %pack_slots.1 = (f32[384,128]{1,0:T(8,128)}, f32[14,24,128]{2,1,0:T(8,128)S(1)}, f32[14,24,128]{2,1,0:T(8,128)S(1)}) custom-call(s32[1]{0:T(128)} %bitcast.13.gx_ref, f32[3,32,128]{2,1,0:T(8,128)} %bitcast.44, s32[32,128]{1,0:T(8,128)} %bitcast.45, s32[1,128]{1,0:T(1,128)} %bitcast.48, f32[3,8,24,128]{3,2,1,0:T(8,128)} %field_ref.1, ...), custom_call_target="tpu_custom_call" | custom-call | flops 1048576 | bytes 1048576 | tf_op jit(solution)/shard_map/pack_slots/pallas_call | solution.py:450
  2.5 2.6 %collective-permute-start = (f32[14,24,128]{2,1,0:T(8,128)S(1)}, f32[14,24,128]{2,1,0:T(8,128)S(1)}, u32[]{:S(2)}, u32[]{:S(2)}) collective-permute-start(f32[14,24,128]{2,1,0:T(8,128)S(1)} %get-tuple-element.44), channel_id=1, source_target_pairs={{0,16},{32,48},{64,80},{96,112},{128,144},{160,176},{192,208},{224... | collective-permute-start | bytes 516104 | tf_op jit(solution)/shard_map/ppermute | solution.py:467
  5.1 7.3 %collective-permute-start.1 = (f32[14,24,128]{2,1,0:T(8,128)S(1)}, f32[14,24,128]{2,1,0:T(8,128)S(1)}, u32[]{:S(2)}, u32[]{:S(2)}) collective-permute-start(f32[14,24,128]{2,1,0:T(8,128)S(1)} %get-tuple-element.45), channel_id=1, source_target_pairs={{16,32},{48,64},{80,96},{112,128},{144,160},{176,192},{208,224},{2... | collective-permute-start | bytes 516104 | tf_op jit(solution)/shard_map/ppermute | solution.py:467
  12.4 8.2 %all-to-all-start.1 = ((f32[128,1,384]{2,1,0:T(1,128)}), f32[128,1,384]{2,1,0:T(1,128)S(1)}, u32[]{:S(2)}, u32[]{:S(2)}) async-start(f32[128,1,384]{2,1,0:T(1,128)} %bitcast.18), calls=%async_computation.1 | async-start | bytes 393216 | tf_op jit(solution)/shard_map/all_to_all | solution.py:494
  20.6 0.0 collective-permute-done.xeven_ref
  20.6 0.0 collective-permute-done.1.xodd_ref
  20.6 1.1 %pack_y.1 = (f32[12,14,128]{2,1,0:T(8,128)S(1)}, f32[12,14,128]{2,1,0:T(8,128)S(1)}) custom-call(s32[1]{0:T(128)} %bitcast.13.gx_ref, s32[1]{0:T(128)} %bitcast.14.gy_ref, f32[3,8,24,128]{3,2,1,0:T(8,128)} %field_ref.1, f32[8,24,128]{2,1,0:T(8,128)} %stiff_ref.3, f32[8,24,128]{2,1,0:T(8,128)} %mass_ref.1, f32[14,24,128]{2,1,0:T(8,128)S(1)} %collective-permute-done.xeven_ref, ...), custom_call_target="tpu_custom_call" | custom-call | flops 17179869184 | bytes 1048576 | tf_op jit(solution)/shard_map/pack_y/pallas_call | solution.py:450
  21.7 0.0 copy-start
  21.7 0.0 copy-start.1
  21.7 0.0 copy-start.2
  21.7 1.0 %collective-permute-start.2 = (f32[12,14,128]{2,1,0:T(8,128)S(1)}, f32[12,14,128]{2,1,0:T(8,128)S(1)}, u32[]{:S(2)}, u32[]{:S(2)}) collective-permute-start(f32[12,14,128]{2,1,0:T(8,128)S(1)} %get-tuple-element.47), channel_id=1, source_target_pairs={{0,2},{4,6},{8,10},{12,14},{2,0},{6,4},{10,8},{14,12},{1,3},{5,7},... | collective-permute-start | bytes 258056 | tf_op jit(solution)/shard_map/ppermute | solution.py:467
  22.7 0.9 %collective-permute-start.3 = (f32[12,14,128]{2,1,0:T(8,128)S(1)}, f32[12,14,128]{2,1,0:T(8,128)S(1)}, u32[]{:S(2)}, u32[]{:S(2)}) collective-permute-start(f32[12,14,128]{2,1,0:T(8,128)S(1)} %get-tuple-element.48), channel_id=1, source_target_pairs={{2,4},{6,8},{10,12},{14,0},{4,2},{8,6},{12,10},{0,14},{3,5},{7,9},... | collective-permute-start | bytes 258056 | tf_op jit(solution)/shard_map/ppermute | solution.py:467
  23.6 0.1 collective-permute-done.2.yeven_ref
  23.7 4.2 %collective-permute-done.3.yodd_ref = f32[12,14,128]{2,1,0:T(8,128)S(1)} collective-permute-done((f32[12,14,128]{2,1,0:T(8,128)S(1)}, f32[12,14,128]{2,1,0:T(8,128)S(1)}, u32[]{:S(2)}, u32[]{:S(2)}) %collective-permute-start.3) | collective-permute-done | bytes 86048 | tf_op jit(solution)/shard_map/ppermute | solution.py:467
  27.9 8.0 %all-to-all-done.1 = f32[128,1,384]{2,1,0:T(1,128)S(1)} async-done(((f32[128,1,384]{2,1,0:T(1,128)}), f32[128,1,384]{2,1,0:T(1,128)S(1)}, u32[]{:S(2)}, u32[]{:S(2)}) %all-to-all-start.1) | async-done | bytes 196640 | tf_op jit(solution)/shard_map/all_to_all | solution.py:494
  35.9 0.0 copy-start.3
  35.9 0.0 copy-start.4
  35.9 3.2 %scatter_slots.1 = (f32[3,12,24,128]{3,2,1,0:T(8,128)S(1)}, f32[12,6,128]{2,1,0:T(8,128)S(1)}, f32[12,6,128]{2,1,0:T(8,128)S(1)}) custom-call(s32[1]{0:T(128)} %bitcast.14.gy_ref, f32[384,128]{1,0:T(8,128)S(1)} %bitcast.32), custom_call_target="tpu_custom_call" | custom-call | flops 4294967296 | bytes 1048576 | tf_op jit(solution)/shard_map/scatter_slots/pallas_call | solution.py:450
  39.1 0.5 collective-permute-start.5
  39.6 0.3 collective-permute-start.6
  39.9 0.0 copy-done
  39.9 0.0 copy-done.1
  39.9 0.0 copy-done.2
  39.9 0.4 widen_fixed.1
  40.3 0.5 collective-permute-start.4
  40.8 0.0 copy-done.3
  40.8 0.0 copy-done.4
  40.8 1.7 %route_hull.1 = (s32[96,128]{1,0:T(8,128)S(1)}, f32[48,128]{1,0:T(8,128)S(1)}) custom-call(s32[32,128]{1,0:T(8,128)S(1)} %bitcast.46, s32[32,128]{1,0:T(8,128)S(1)} %bitcast.47), custom_call_target="tpu_custom_call" | custom-call | flops 2147483648 | bytes 1048576 | tf_op jit(solution)/shard_map/route_hull/pallas_call | solution.py:450
  42.5 0.0 collective-permute-done.5.yeven_ref
  42.5 0.9 %collective-permute-done.6.yodd_ref = f32[12,6,128]{2,1,0:T(8,128)S(1)} collective-permute-done((f32[12,6,128]{2,1,0:T(8,128)S(1)}, f32[12,6,128]{2,1,0:T(8,128)S(1)}, u32[]{:S(2)}, u32[]{:S(2)}) %collective-permute-start.6) | collective-permute-done | bytes 36896 | tf_op jit(solution)/shard_map/ppermute | solution.py:467
  43.4 0.3 widen_source.1
  43.7 0.6 collective-permute-start.7
  44.4 0.0 collective-permute-done.4.z_ref
  44.4 1.0 %prepare.1 = (f32[3,14,32,256]{3,2,1,0:T(8,128)S(1)}, f32[6,12,32,256]{3,2,1,0:T(8,128)S(1)}, f32[12,32,256]{2,1,0:T(8,128)S(1)}, f32[12,32,256]{2,1,0:T(8,128)S(1)}, f32[12,32,256]{2,1,0:T(8,128)S(1)}) custom-call(s32[1]{0:T(128)} %bitcast.12.side_ref, f32[5,14,32,128]{3,2,1,0:T(8,128)S(1)} %get-tuple-element.51.ext_ref, ...), custom_call_target="tpu_custom_call" | custom-call | flops 1073741824 | bytes 1048576 | tf_op jit(solution)/shard_map/prepare/pallas_call | solution.py:450
  45.4 1.3 %collective-permute-done.7.z_ref = f32[16,384]{1,0:T(8,128)S(1)} collective-permute-done((f32[16,384]{1,0:T(8,128)S(1)}, f32[16,384]{1,0:T(8,128)S(1)}, u32[]{:S(2)}, u32[]{:S(2)}) %collective-permute-start.7) | collective-permute-done | bytes 24608 | tf_op jit(solution)/shard_map/ppermute | solution.py:566
  46.6 5.6 %relax_and_gather.1 = (f32[3,8,24,128]{3,2,1,0:T(8,128)}, f32[192,128]{1,0:T(8,128)}) custom-call(s32[1]{0:T(128)} %bitcast.12.side_ref, f32[3,14,32,256]{3,2,1,0:T(8,128)S(1)} %get-tuple-element.53.start_ref, f32[6,12,32,256]{3,2,1,0:T(8,128)S(1)} %get-tuple-element.54.weight_s, f32[12,32,256]{2,1,0:T(8,128)S(1)} %get-tuple-element.55.keep_s, ...), custom_call_target="tpu_custom_call" | custom-call | flops 4294967296 | bytes 1048576 | tf_op jit(solution)/shard_map/relax_and_gather/pallas_call | solution.py:450
  52.2 5.5 %all-to-all-start.2 = ((f32[16,1,1536]{2,1,0:T(1,128)}), f32[16,1,1536]{2,1,0:T(1,128)S(1)}, u32[]{:S(2)}, u32[]{:S(2)}) async-start(f32[16,1,1536]{2,1,0:T(1,128)} %bitcast.22), calls=%async_computation.2 | async-start | bytes 196608 | tf_op jit(solution)/shard_map/all_to_all | solution.py:599
  57.7 6.3 %all-to-all-done.2 = f32[16,1,1536]{2,1,0:T(1,128)S(1)} async-done(((f32[16,1,1536]{2,1,0:T(1,128)}), f32[16,1,1536]{2,1,0:T(1,128)S(1)}, u32[]{:S(2)}, u32[]{:S(2)}) %all-to-all-start.2) | async-done | bytes 98336 | tf_op jit(solution)/shard_map/all_to_all | solution.py:599
  64.0 2.6 %scatter_hull.1 = (f32[3,64,256]{2,1,0:T(8,128)}, s32[1]{0:T(128)}) custom-call(f32[192,128]{1,0:T(8,128)S(1)} %bitcast.33), custom_call_target="tpu_custom_call" | custom-call | flops 4294967296 | bytes 1048576 | tf_op jit(solution)/shard_map/scatter_hull/pallas_call | solution.py:450
  (1 shorter events, 0.0 us)
Async XLA Ops:
  2.5 18.1 %collective-permute-start = (f32[14,24,128]{2,1,0:T(8,128)S(1)}, f32[14,24,128]{2,1,0:T(8,128)S(1)}, u32[]{:S(2)}, u32[]{:S(2)}) collective-permute-start(f32[14,24,128]{2,1,0:T(8,128)S(1)} %get-tuple-element.44), channel_id=1, source_target_pairs={{0,16},{32,48},{64,80},{96,112},{128,144},{160,176},{192,208},{224... | collective-permute-start | bytes 516104 | tf_op jit(solution)/shard_map/ppermute | solution.py:467
  5.1 15.6 %collective-permute-start.1 = (f32[14,24,128]{2,1,0:T(8,128)S(1)}, f32[14,24,128]{2,1,0:T(8,128)S(1)}, u32[]{:S(2)}, u32[]{:S(2)}) collective-permute-start(f32[14,24,128]{2,1,0:T(8,128)S(1)} %get-tuple-element.45), channel_id=1, source_target_pairs={{16,32},{48,64},{80,96},{112,128},{144,160},{176,192},{208,224},{2... | collective-permute-start | bytes 516104 | tf_op jit(solution)/shard_map/ppermute | solution.py:467
  12.4 23.5 %all-to-all-start.1 = ((f32[128,1,384]{2,1,0:T(1,128)}), f32[128,1,384]{2,1,0:T(1,128)S(1)}, u32[]{:S(2)}, u32[]{:S(2)}) async-start(f32[128,1,384]{2,1,0:T(1,128)} %bitcast.18), calls=%async_computation.1 | async-start | bytes 393216 | tf_op jit(solution)/shard_map/all_to_all | solution.py:494
  21.7 18.2 %copy-start = (f32[3,8,24,128]{3,2,1,0:T(8,128)S(1)}, f32[3,8,24,128]{3,2,1,0:T(8,128)}, u32[]{:S(2)}) copy-start(f32[3,8,24,128]{3,2,1,0:T(8,128)} %field_ref.1) | copy-start | bytes 884740
  21.7 18.2 %copy-start.1 = (f32[8,24,128]{2,1,0:T(8,128)S(1)}, f32[8,24,128]{2,1,0:T(8,128)}, u32[]{:S(2)}) copy-start(f32[8,24,128]{2,1,0:T(8,128)} %mass_ref.1) | copy-start | bytes 294916
  21.7 18.1 %copy-start.2 = (f32[8,24,128]{2,1,0:T(8,128)S(1)}, f32[8,24,128]{2,1,0:T(8,128)}, u32[]{:S(2)}) copy-start(f32[8,24,128]{2,1,0:T(8,128)} %stiff_ref.3) | copy-start | bytes 294916
  21.7 1.9 %collective-permute-start.2 = (f32[12,14,128]{2,1,0:T(8,128)S(1)}, f32[12,14,128]{2,1,0:T(8,128)S(1)}, u32[]{:S(2)}, u32[]{:S(2)}) collective-permute-start(f32[12,14,128]{2,1,0:T(8,128)S(1)} %get-tuple-element.47), channel_id=1, source_target_pairs={{0,2},{4,6},{8,10},{12,14},{2,0},{6,4},{10,8},{14,12},{1,3},{5,7},... | collective-permute-start | bytes 258056 | tf_op jit(solution)/shard_map/ppermute | solution.py:467
  22.7 5.1 %collective-permute-start.3 = (f32[12,14,128]{2,1,0:T(8,128)S(1)}, f32[12,14,128]{2,1,0:T(8,128)S(1)}, u32[]{:S(2)}, u32[]{:S(2)}) collective-permute-start(f32[12,14,128]{2,1,0:T(8,128)S(1)} %get-tuple-element.48), channel_id=1, source_target_pairs={{2,4},{6,8},{10,12},{14,0},{4,2},{8,6},{12,10},{0,14},{3,5},{7,9},... | collective-permute-start | bytes 258056 | tf_op jit(solution)/shard_map/ppermute | solution.py:467
  35.9 4.9 %copy-start.3 = (s32[1,1,4096]{2,1,0:T(1,128)S(1)}, s32[1,1,4096]{2,1,0:T(1,128)}, u32[]{:S(2)}) copy-start(s32[1,1,4096]{2,1,0:T(1,128)} %param.16) | copy-start | bytes 49156
  35.9 4.9 %copy-start.4 = (s32[1,1,4096]{2,1,0:T(1,128)S(1)}, s32[1,1,4096]{2,1,0:T(1,128)}, u32[]{:S(2)}) copy-start(s32[1,1,4096]{2,1,0:T(1,128)} %param.17) | copy-start | bytes 49156
  39.1 3.4 %collective-permute-start.5 = (f32[12,6,128]{2,1,0:T(8,128)S(1)}, f32[12,6,128]{2,1,0:T(8,128)S(1)}, u32[]{:S(2)}, u32[]{:S(2)}) collective-permute-start(f32[12,6,128]{2,1,0:T(8,128)S(1)} %get-tuple-element.60), channel_id=1, source_target_pairs={{0,2},{4,6},{8,10},{12,14},{2,0},{6,4},{10,8},{14,12},{1,3},{5,7},... | collective-permute-start | bytes 110600 | tf_op jit(solution)/shard_map/ppermute | solution.py:467
  39.6 3.8 %collective-permute-start.6 = (f32[12,6,128]{2,1,0:T(8,128)S(1)}, f32[12,6,128]{2,1,0:T(8,128)S(1)}, u32[]{:S(2)}, u32[]{:S(2)}) collective-permute-start(f32[12,6,128]{2,1,0:T(8,128)S(1)} %get-tuple-element.61), channel_id=1, source_target_pairs={{2,4},{6,8},{10,12},{14,0},{4,2},{8,6},{12,10},{0,14},{3,5},{7,9},... | collective-permute-start | bytes 110600 | tf_op jit(solution)/shard_map/ppermute | solution.py:467
  40.3 4.1 %collective-permute-start.4 = (f32[16,384]{1,0:T(8,128)S(1)}, f32[16,384]{1,0:T(8,128)S(1)}, u32[]{:S(2)}, u32[]{:S(2)}) collective-permute-start(f32[16,384]{1,0:T(8,128)S(1)} %get-tuple-element.52), channel_id=1, source_target_pairs={{0,1},{1,0},{2,3},{3,2},{4,5},{5,4},{6,7},{7,6},{8,9},{9,8},{10,11... | collective-permute-start | bytes 73736 | tf_op jit(solution)/shard_map/ppermute | solution.py:553
  43.7 2.9 %collective-permute-start.7 = (f32[16,384]{1,0:T(8,128)S(1)}, f32[16,384]{1,0:T(8,128)S(1)}, u32[]{:S(2)}, u32[]{:S(2)}) collective-permute-start(f32[16,384]{1,0:T(8,128)S(1)} %get-tuple-element.63), channel_id=1, source_target_pairs={{0,1},{1,0},{2,3},{3,2},{4,5},{5,4},{6,7},{7,6},{8,9},{9,8},{10,11... | collective-permute-start | bytes 73736 | tf_op jit(solution)/shard_map/ppermute | solution.py:566
  52.2 11.8 %all-to-all-start.2 = ((f32[16,1,1536]{2,1,0:T(1,128)}), f32[16,1,1536]{2,1,0:T(1,128)S(1)}, u32[]{:S(2)}, u32[]{:S(2)}) async-start(f32[16,1,1536]{2,1,0:T(1,128)} %bitcast.22), calls=%async_computation.2 | async-start | bytes 196608 | tf_op jit(solution)/shard_map/all_to_all | solution.py:599

commit v6 on v5

--- a/solution.py
+++ b/solution.py
@@ -519,7 +519,7 @@
         places="SSHHH",
     )
     yeven, yodd = pair_exchange("gy", even, odd)
-    arrived, yeven, yodd = lax.optimization_barrier((arrived, yeven, yodd))
+    arrived, yeven, yodd, where, ids = lax.optimization_barrier((arrived, yeven, yodd, where, ids))
     y_message = shaped(CX + 4, 6, CZ)
     source, even, odd = call(
         scatter_slots,

time: 67.8 us -> 68.2 us (level)
  transfers between devices with their start and end apart: 10 -> 10, of which waited for: 6 -> 5; matrix products, arithmetic and copies ran while one was open for 0% -> 0% of each run, Pallas kernels for 7% -> 7%
where the time goes in v6:
time: 68.2 us; the launch traced here: 67.9 us
  starting transfers between devices  27.3 us (40%)
  waiting for transfers between devices  20.7 us (30%)
  Pallas kernels  18.2 us (27%)
  between operations  1.62 us (2%)
    pallas_call x9, Pallas kernels, call(): pl.pallas_call(kernel, out_shape=outs, in_specs=specs(len(args), places),...  18.2 us
    ppermute x6, starting transfers between devices, pair_exchange(): lax.ppermute(values, axis, pairs + [(b, a) for a, b in pairs])  12.5 us
    all_to_all x1, starting transfers between devices, per_device(): lax.all_to_all(packed, ('gx', 'gy'), split_axis=0, concat_axis=0, tiled=T...  8.23 us
    all_to_all x1, waiting for transfers between devices, per_device(): lax.all_to_all(packed, ('gx', 'gy'), split_axis=0, concat_axis=0, tiled=T...  8.04 us
    all_to_all x1, waiting for transfers between devices, per_device(): lax.all_to_all(outgoing, ('gy', 'gz'), split_axis=0, concat_axis=0, tiled...  6.28 us
    all_to_all x1, starting transfers between devices, per_device(): lax.all_to_all(outgoing, ('gy', 'gz'), split_axis=0, concat_axis=0, tiled...  5.47 us
    ppermute x6, waiting for transfers between devices, pair_exchange(): lax.ppermute(values, axis, pairs + [(b, a) for a, b in pairs])  5.12 us
  transfers between devices with their start and end apart: 10, of which 5 were waited for; matrix products, arithmetic and copies ran while one was open for 0% of the time, Pallas kernels for 7%

profile of v6, /device:TPU:1, one launch (start us, length us, event | category | flops | bytes accessed | tf_op | source)
XLA Modules:
  0.0 67.9 jit_solution(6878392929736452994)
XLA Ops:
  0.6 1.9 %pack_slots.1 = (f32[384,128]{1,0:T(8,128)}, f32[14,24,128]{2,1,0:T(8,128)S(1)}, f32[14,24,128]{2,1,0:T(8,128)S(1)}) custom-call(s32[1]{0:T(128)} %bitcast.13.gx_ref, f32[3,32,128]{2,1,0:T(8,128)} %bitcast.44, s32[32,128]{1,0:T(8,128)} %bitcast.45, s32[1,128]{1,0:T(1,128)} %bitcast.48, f32[3,8,24,128]{3,2,1,0:T(8,128)} %field_ref.1, ...), custom_call_target="tpu_custom_call" | custom-call | flops 1048576 | bytes 1048576 | tf_op jit(solution)/shard_map/pack_slots/pallas_call | solution.py:450
  2.5 2.6 %collective-permute-start = (f32[14,24,128]{2,1,0:T(8,128)S(1)}, f32[14,24,128]{2,1,0:T(8,128)S(1)}, u32[]{:S(2)}, u32[]{:S(2)}) collective-permute-start(f32[14,24,128]{2,1,0:T(8,128)S(1)} %get-tuple-element.46), channel_id=1, source_target_pairs={{0,16},{32,48},{64,80},{96,112},{128,144},{160,176},{192,208},{224... | collective-permute-start | bytes 516104 | tf_op jit(solution)/shard_map/ppermute | solution.py:467
  5.1 7.3 %collective-permute-start.1 = (f32[14,24,128]{2,1,0:T(8,128)S(1)}, f32[14,24,128]{2,1,0:T(8,128)S(1)}, u32[]{:S(2)}, u32[]{:S(2)}) collective-permute-start(f32[14,24,128]{2,1,0:T(8,128)S(1)} %get-tuple-element.47), channel_id=1, source_target_pairs={{16,32},{48,64},{80,96},{112,128},{144,160},{176,192},{208,224},{2... | collective-permute-start | bytes 516104 | tf_op jit(solution)/shard_map/ppermute | solution.py:467
  12.4 8.2 %all-to-all-start.1 = ((f32[128,1,384]{2,1,0:T(1,128)}), f32[128,1,384]{2,1,0:T(1,128)S(1)}, u32[]{:S(2)}, u32[]{:S(2)}) async-start(f32[128,1,384]{2,1,0:T(1,128)} %bitcast.18), calls=%async_computation.1 | async-start | bytes 393216 | tf_op jit(solution)/shard_map/all_to_all | solution.py:494
  20.6 0.0 collective-permute-done.xeven_ref
  20.6 0.0 collective-permute-done.1.xodd_ref
  20.6 0.0 copy-start.3
  20.6 0.0 copy-start.4
  20.6 1.1 %pack_y.1 = (f32[12,14,128]{2,1,0:T(8,128)S(1)}, f32[12,14,128]{2,1,0:T(8,128)S(1)}) custom-call(s32[1]{0:T(128)} %bitcast.13.gx_ref, s32[1]{0:T(128)} %bitcast.14.gy_ref, f32[3,8,24,128]{3,2,1,0:T(8,128)} %field_ref.1, f32[8,24,128]{2,1,0:T(8,128)} %stiff_ref.3, f32[8,24,128]{2,1,0:T(8,128)} %mass_ref.1, f32[14,24,128]{2,1,0:T(8,128)S(1)} %collective-permute-done.xeven_ref, ...), custom_call_target="tpu_custom_call" | custom-call | flops 17179869184 | bytes 1048576 | tf_op jit(solution)/shard_map/pack_y/pallas_call | solution.py:450
  21.7 1.0 %collective-permute-start.2 = (f32[12,14,128]{2,1,0:T(8,128)S(1)}, f32[12,14,128]{2,1,0:T(8,128)S(1)}, u32[]{:S(2)}, u32[]{:S(2)}) collective-permute-start(f32[12,14,128]{2,1,0:T(8,128)S(1)} %get-tuple-element.49), channel_id=1, source_target_pairs={{0,2},{4,6},{8,10},{12,14},{2,0},{6,4},{10,8},{14,12},{1,3},{5,7},... | collective-permute-start | bytes 258056 | tf_op jit(solution)/shard_map/ppermute | solution.py:467
  22.7 0.9 %collective-permute-start.3 = (f32[12,14,128]{2,1,0:T(8,128)S(1)}, f32[12,14,128]{2,1,0:T(8,128)S(1)}, u32[]{:S(2)}, u32[]{:S(2)}) collective-permute-start(f32[12,14,128]{2,1,0:T(8,128)S(1)} %get-tuple-element.50), channel_id=1, source_target_pairs={{2,4},{6,8},{10,12},{14,0},{4,2},{8,6},{12,10},{0,14},{3,5},{7,9},... | collective-permute-start | bytes 258056 | tf_op jit(solution)/shard_map/ppermute | solution.py:467
  23.6 0.0 copy-done.3
  23.6 0.0 copy-done.4
  23.6 1.7 %route_hull.1 = (s32[96,128]{1,0:T(8,128)S(1)}, f32[48,128]{1,0:T(8,128)S(1)}) custom-call(s32[32,128]{1,0:T(8,128)S(1)} %bitcast.46, s32[32,128]{1,0:T(8,128)S(1)} %bitcast.47), custom_call_target="tpu_custom_call" | custom-call | flops 2147483648 | bytes 1048576 | tf_op jit(solution)/shard_map/route_hull/pallas_call | solution.py:450
  25.4 0.0 copy-start
  25.4 0.0 copy-start.1
  25.4 0.0 copy-start.2
  25.4 0.0 collective-permute-done.2.yeven_ref
  25.4 2.4 %collective-permute-done.3.yodd_ref = f32[12,14,128]{2,1,0:T(8,128)S(1)} collective-permute-done((f32[12,14,128]{2,1,0:T(8,128)S(1)}, f32[12,14,128]{2,1,0:T(8,128)S(1)}, u32[]{:S(2)}, u32[]{:S(2)}) %collective-permute-start.3) | collective-permute-done | bytes 86048 | tf_op jit(solution)/shard_map/ppermute | solution.py:467
  27.9 8.0 %all-to-all-done.1 = f32[128,1,384]{2,1,0:T(1,128)S(1)} async-done(((f32[128,1,384]{2,1,0:T(1,128)}), f32[128,1,384]{2,1,0:T(1,128)S(1)}, u32[]{:S(2)}, u32[]{:S(2)}) %all-to-all-start.1) | async-done | bytes 196640 | tf_op jit(solution)/shard_map/all_to_all | solution.py:494
  35.9 3.2 %scatter_slots.1 = (f32[3,12,24,128]{3,2,1,0:T(8,128)S(1)}, f32[12,6,128]{2,1,0:T(8,128)S(1)}, f32[12,6,128]{2,1,0:T(8,128)S(1)}) custom-call(s32[1]{0:T(128)} %bitcast.14.gy_ref, f32[384,128]{1,0:T(8,128)S(1)} %bitcast.32), custom_call_target="tpu_custom_call" | custom-call | flops 4294967296 | bytes 1048576 | tf_op jit(solution)/shard_map/scatter_slots/pallas_call | solution.py:450
  39.1 0.5 collective-permute-start.5
  39.6 0.3 collective-permute-start.6
  39.9 0.0 copy-done
  39.9 0.0 copy-done.1
  39.9 0.0 copy-done.2
  39.9 0.4 widen_fixed.1
  40.3 0.5 collective-permute-start.4
  40.8 0.0 collective-permute-done.5.yeven_ref
  40.8 2.7 %collective-permute-done.6.yodd_ref = f32[12,6,128]{2,1,0:T(8,128)S(1)} collective-permute-done((f32[12,6,128]{2,1,0:T(8,128)S(1)}, f32[12,6,128]{2,1,0:T(8,128)S(1)}, u32[]{:S(2)}, u32[]{:S(2)}) %collective-permute-start.6) | collective-permute-done | bytes 36896 | tf_op jit(solution)/shard_map/ppermute | solution.py:467
  43.4 0.3 widen_source.1
  43.7 0.6 collective-permute-start.7
  44.3 0.0 collective-permute-done.4.z_ref
  44.3 1.0 %prepare.1 = (f32[3,14,32,256]{3,2,1,0:T(8,128)S(1)}, f32[6,12,32,256]{3,2,1,0:T(8,128)S(1)}, f32[12,32,256]{2,1,0:T(8,128)S(1)}, f32[12,32,256]{2,1,0:T(8,128)S(1)}, f32[12,32,256]{2,1,0:T(8,128)S(1)}) custom-call(s32[1]{0:T(128)} %bitcast.12.side_ref, f32[5,14,32,128]{3,2,1,0:T(8,128)S(1)} %get-tuple-element.55.ext_ref, ...), custom_call_target="tpu_custom_call" | custom-call | flops 1073741824 | bytes 1048576 | tf_op jit(solution)/shard_map/prepare/pallas_call | solution.py:450
  45.4 1.3 %collective-permute-done.7.z_ref = f32[16,384]{1,0:T(8,128)S(1)} collective-permute-done((f32[16,384]{1,0:T(8,128)S(1)}, f32[16,384]{1,0:T(8,128)S(1)}, u32[]{:S(2)}, u32[]{:S(2)}) %collective-permute-start.7) | collective-permute-done | bytes 24608 | tf_op jit(solution)/shard_map/ppermute | solution.py:566
  46.6 6.0 %relax_and_gather.1 = (f32[3,8,24,128]{3,2,1,0:T(8,128)}, f32[192,128]{1,0:T(8,128)}) custom-call(s32[1]{0:T(128)} %bitcast.12.side_ref, f32[3,14,32,256]{3,2,1,0:T(8,128)S(1)} %get-tuple-element.57.start_ref, f32[6,12,32,256]{3,2,1,0:T(8,128)S(1)} %get-tuple-element.58.weight_s, f32[12,32,256]{2,1,0:T(8,128)S(1)} %get-tuple-element.59.keep_s, ...), custom_call_target="tpu_custom_call" | custom-call | flops 4294967296 | bytes 1048576 | tf_op jit(solution)/shard_map/relax_and_gather/pallas_call | solution.py:450
  52.6 5.5 %all-to-all-start.2 = ((f32[16,1,1536]{2,1,0:T(1,128)}), f32[16,1,1536]{2,1,0:T(1,128)S(1)}, u32[]{:S(2)}, u32[]{:S(2)}) async-start(f32[16,1,1536]{2,1,0:T(1,128)} %bitcast.22), calls=%async_computation.2 | async-start | bytes 196608 | tf_op jit(solution)/shard_map/all_to_all | solution.py:599
  58.1 6.3 %all-to-all-done.2 = f32[16,1,1536]{2,1,0:T(1,128)S(1)} async-done(((f32[16,1,1536]{2,1,0:T(1,128)}), f32[16,1,1536]{2,1,0:T(1,128)S(1)}, u32[]{:S(2)}, u32[]{:S(2)}) %all-to-all-start.2) | async-done | bytes 98336 | tf_op jit(solution)/shard_map/all_to_all | solution.py:599
  64.4 2.6 %scatter_hull.1 = (f32[3,64,256]{2,1,0:T(8,128)}, s32[1]{0:T(128)}) custom-call(f32[192,128]{1,0:T(8,128)S(1)} %bitcast.33), custom_call_target="tpu_custom_call" | custom-call | flops 4294967296 | bytes 1048576 | tf_op jit(solution)/shard_map/scatter_hull/pallas_call | solution.py:450
  (1 shorter events, 0.0 us)
Async XLA Ops:
  2.5 18.1 %collective-permute-start = (f32[14,24,128]{2,1,0:T(8,128)S(1)}, f32[14,24,128]{2,1,0:T(8,128)S(1)}, u32[]{:S(2)}, u32[]{:S(2)}) collective-permute-start(f32[14,24,128]{2,1,0:T(8,128)S(1)} %get-tuple-element.46), channel_id=1, source_target_pairs={{0,16},{32,48},{64,80},{96,112},{128,144},{160,176},{192,208},{224... | collective-permute-start | bytes 516104 | tf_op jit(solution)/shard_map/ppermute | solution.py:467
  5.1 15.6 %collective-permute-start.1 = (f32[14,24,128]{2,1,0:T(8,128)S(1)}, f32[14,24,128]{2,1,0:T(8,128)S(1)}, u32[]{:S(2)}, u32[]{:S(2)}) collective-permute-start(f32[14,24,128]{2,1,0:T(8,128)S(1)} %get-tuple-element.47), channel_id=1, source_target_pairs={{16,32},{48,64},{80,96},{112,128},{144,160},{176,192},{208,224},{2... | collective-permute-start | bytes 516104 | tf_op jit(solution)/shard_map/ppermute | solution.py:467
  12.4 23.5 %all-to-all-start.1 = ((f32[128,1,384]{2,1,0:T(1,128)}), f32[128,1,384]{2,1,0:T(1,128)S(1)}, u32[]{:S(2)}, u32[]{:S(2)}) async-start(f32[128,1,384]{2,1,0:T(1,128)} %bitcast.18), calls=%async_computation.1 | async-start | bytes 393216 | tf_op jit(solution)/shard_map/all_to_all | solution.py:494
  20.6 3.0 %copy-start.3 = (s32[1,1,4096]{2,1,0:T(1,128)S(1)}, s32[1,1,4096]{2,1,0:T(1,128)}, u32[]{:S(2)}) copy-start(s32[1,1,4096]{2,1,0:T(1,128)} %param.16) | copy-start | bytes 49156
  20.6 3.0 %copy-start.4 = (s32[1,1,4096]{2,1,0:T(1,128)S(1)}, s32[1,1,4096]{2,1,0:T(1,128)}, u32[]{:S(2)}) copy-start(s32[1,1,4096]{2,1,0:T(1,128)} %param.17) | copy-start | bytes 49156
  21.7 3.7 %collective-permute-start.2 = (f32[12,14,128]{2,1,0:T(8,128)S(1)}, f32[12,14,128]{2,1,0:T(8,128)S(1)}, u32[]{:S(2)}, u32[]{:S(2)}) collective-permute-start(f32[12,14,128]{2,1,0:T(8,128)S(1)} %get-tuple-element.49), channel_id=1, source_target_pairs={{0,2},{4,6},{8,10},{12,14},{2,0},{6,4},{10,8},{14,12},{1,3},{5,7},... | collective-permute-start | bytes 258056 | tf_op jit(solution)/shard_map/ppermute | solution.py:467
  22.7 5.1 %collective-permute-start.3 = (f32[12,14,128]{2,1,0:T(8,128)S(1)}, f32[12,14,128]{2,1,0:T(8,128)S(1)}, u32[]{:S(2)}, u32[]{:S(2)}) collective-permute-start(f32[12,14,128]{2,1,0:T(8,128)S(1)} %get-tuple-element.50), channel_id=1, source_target_pairs={{2,4},{6,8},{10,12},{14,0},{4,2},{8,6},{12,10},{0,14},{3,5},{7,9},... | collective-permute-start | bytes 258056 | tf_op jit(solution)/shard_map/ppermute | solution.py:467
  25.4 14.5 %copy-start = (f32[3,8,24,128]{3,2,1,0:T(8,128)S(1)}, f32[3,8,24,128]{3,2,1,0:T(8,128)}, u32[]{:S(2)}) copy-start(f32[3,8,24,128]{3,2,1,0:T(8,128)} %field_ref.1) | copy-start | bytes 884740
  25.4 14.5 %copy-start.1 = (f32[8,24,128]{2,1,0:T(8,128)S(1)}, f32[8,24,128]{2,1,0:T(8,128)}, u32[]{:S(2)}) copy-start(f32[8,24,128]{2,1,0:T(8,128)} %mass_ref.1) | copy-start | bytes 294916
  25.4 14.5 %copy-start.2 = (f32[8,24,128]{2,1,0:T(8,128)S(1)}, f32[8,24,128]{2,1,0:T(8,128)}, u32[]{:S(2)}) copy-start(f32[8,24,128]{2,1,0:T(8,128)} %stiff_ref.3) | copy-start | bytes 294916
  39.1 1.6 %collective-permute-start.5 = (f32[12,6,128]{2,1,0:T(8,128)S(1)}, f32[12,6,128]{2,1,0:T(8,128)S(1)}, u32[]{:S(2)}, u32[]{:S(2)}) collective-permute-start(f32[12,6,128]{2,1,0:T(8,128)S(1)} %get-tuple-element.64), channel_id=1, source_target_pairs={{0,2},{4,6},{8,10},{12,14},{2,0},{6,4},{10,8},{14,12},{1,3},{5,7},... | collective-permute-start | bytes 110600 | tf_op jit(solution)/shard_map/ppermute | solution.py:467
  39.6 3.8 %collective-permute-start.6 = (f32[12,6,128]{2,1,0:T(8,128)S(1)}, f32[12,6,128]{2,1,0:T(8,128)S(1)}, u32[]{:S(2)}, u32[]{:S(2)}) collective-permute-start(f32[12,6,128]{2,1,0:T(8,128)S(1)} %get-tuple-element.65), channel_id=1, source_target_pairs={{2,4},{6,8},{10,12},{14,0},{4,2},{8,6},{12,10},{0,14},{3,5},{7,9},... | collective-permute-start | bytes 110600 | tf_op jit(solution)/shard_map/ppermute | solution.py:467
  40.3 4.1 %collective-permute-start.4 = (f32[16,384]{1,0:T(8,128)S(1)}, f32[16,384]{1,0:T(8,128)S(1)}, u32[]{:S(2)}, u32[]{:S(2)}) collective-permute-start(f32[16,384]{1,0:T(8,128)S(1)} %get-tuple-element.56), channel_id=1, source_target_pairs={{0,1},{1,0},{2,3},{3,2},{4,5},{5,4},{6,7},{7,6},{8,9},{9,8},{10,11... | collective-permute-start | bytes 73736 | tf_op jit(solution)/shard_map/ppermute | solution.py:553
  43.7 2.9 %collective-permute-start.7 = (f32[16,384]{1,0:T(8,128)S(1)}, f32[16,384]{1,0:T(8,128)S(1)}, u32[]{:S(2)}, u32[]{:S(2)}) collective-permute-start(f32[16,384]{1,0:T(8,128)S(1)} %get-tuple-element.67), channel_id=1, source_target_pairs={{0,1},{1,0},{2,3},{3,2},{4,5},{5,4},{6,7},{7,6},{8,9},{9,8},{10,11... | collective-permute-start | bytes 73736 | tf_op jit(solution)/shard_map/ppermute | solution.py:566
  52.6 11.8 %all-to-all-start.2 = ((f32[16,1,1536]{2,1,0:T(1,128)}), f32[16,1,1536]{2,1,0:T(1,128)S(1)}, u32[]{:S(2)}, u32[]{:S(2)}) async-start(f32[16,1,1536]{2,1,0:T(1,128)} %bitcast.22), calls=%async_computation.2 | async-start | bytes 196608 | tf_op jit(solution)/shard_map/all_to_all | solution.py:599
